TPU v7x, 128 devices: a whole 4x4x4 slice. The times are simulated.
128 devices in a mesh: dp: 8 (over z, core), table: 16 (over x, y).
Axes of the slice: x: 4, y: 4, z: 4, core: 2. Of those that a mesh axis runs over, the one named last changes fastest.
Arguments:
- table: bfloat16 [524288, 512], P(('dp', 'table')), may hold values from -10.2 to 10.2
- last_update: int32 [524288], P(('dp', 'table')), may hold values from 0 to 63
- item_owner: int32 [65536, 1], P(('dp', 'table')), may hold values from 0 to 127; in each aligned block of 512 rows (0 to 511, 512 to 1023, ...) at most 8 rows name the same one
- item_slot: int32 [65536], P(('dp', 'table')), may hold values from 0 to 4095
- neg_owner: int32 [16384, 1], P(('dp', 'table')), may hold values from 0 to 127; in each aligned block of 128 rows (0 to 127, 128 to 255, ...) at most 2 rows name the same one
- neg_slot: int32 [16384], P(('dp', 'table')), may hold values from 0 to 4095
- seq_lengths: int32 [128, 4], P(('dp', 'table')), may hold values from 1 to 256, 512 in all within a row
- w_in: bfloat16 [512, 2048], replicated, may hold values from -0.25 to 0.25
- w_out: bfloat16 [512, 512], replicated, may hold values from -0.25 to 0.25
Outputs:
- token_loss: float32 [65536], P(('dp', 'table'))
- table_grad: float32 [524288, 512], P(('dp', 'table'))
- grad_in: float32 [512, 2048], replicated
- grad_out: float32 [512, 512], replicated
Inputs may be any that keep to these rules, and one draw needn't show every extreme that they name: `item_owner`: in each aligned block of 512 rows no owner is named more than 8 times; some owner is named exactly that often. `neg_owner`: in each aligned block of 128 rows no owner is named more than 2 times; some owner is named exactly that often.
All inputs are finite; a program needn't handle non-finite values.
Results may differ from a plain program's by a relative error of at most 0.02.
Values may be sent and summed in bfloat16 or wider, within the bound.
A program may use at most 128 MiB of HBM per device.

v0:
```python
from functools import partial

import jax
import jax.numpy as jnp
from jax import lax
from jax.sharding import PartitionSpec as P

H = 4
DH = 128
TOK_DEV = 512
LMAX = 256
NNEG = 128
NOW = 64


RHO = 0.97
TAU = 0.125
EPS = 1e-05


def normalize(values):
    center = values - jnp.mean(values, -1, keepdims=True)
    return center * lax.rsqrt(jnp.mean(center * center, -1, keepdims=True) + EPS)


def layer_loss(rows32, w_in32, w_out32, lengths):
    width = rows32.shape[1]
    x32 = rows32[:TOK_DEV]
    negatives = rows32[TOK_DEV:].astype(jnp.bfloat16)
    ends = jnp.cumsum(lengths)
    where = jnp.arange(TOK_DEV, dtype=jnp.int32)
    segment = jnp.sum((where[:, None] >= ends[None, :]).astype(jnp.int32), 1)
    normed = normalize(x32).astype(jnp.bfloat16)
    mixed = jax.nn.silu(
        jnp.dot(normed, w_in32.astype(jnp.bfloat16), preferred_element_type=jnp.float32)
    ).astype(jnp.bfloat16)
    gate_part, value, query, key_part = jnp.split(mixed, 4, axis=1)
    query = query.reshape(TOK_DEV, H, DH)
    key_part = key_part.reshape(TOK_DEV, H, DH)
    value = value.reshape(TOK_DEV, H, DH)
    scores = jnp.einsum("qhd,khd->hqk", query, key_part, preferred_element_type=jnp.float32)
    visible = (segment[:, None] == segment[None, :]) & (where[None, :] <= where[:, None])
    weights = (jax.nn.silu(scores) * (1.0 / LMAX) * visible[None].astype(jnp.float32)).astype(
        jnp.bfloat16
    )
    attended = jnp.einsum(
        "hqk,khd->qhd", weights, value, preferred_element_type=jnp.float32
    ).reshape(TOK_DEV, width)
    gated = (normalize(attended) * gate_part.astype(jnp.float32)).astype(jnp.bfloat16)
    out = (
        x32 + jnp.dot(gated, w_out32.astype(jnp.bfloat16), preferred_element_type=jnp.float32)
    ).astype(jnp.bfloat16)
    following = jnp.concatenate([x32[1:], jnp.zeros((1, width), jnp.float32)], 0)
    valid = jnp.concatenate([segment[1:] == segment[:-1], jnp.zeros((1,), bool)]).astype(
        jnp.float32
    )
    positive = jnp.sum(out.astype(jnp.float32) * following, 1) * TAU
    negative = jnp.dot(out, negatives.T, preferred_element_type=jnp.float32) * TAU
    top = lax.stop_gradient(jnp.maximum(positive, jnp.max(negative, 1)))
    total = jnp.exp(positive - top) + jnp.sum(jnp.exp(negative - top[:, None]), 1)
    losses = (jnp.log(total) + top - positive) * valid
    return (jnp.sum(losses), losses)


def send_ids(values):
    return lax.all_to_all(values, ("dp", "table"), split_axis=0, concat_axis=0, tiled=True)


def send_rows(values):
    return lax.all_to_all(values, ("dp", "table"), split_axis=0, concat_axis=0, tiled=True)


def send_grads(values):
    return lax.all_to_all(values, ("dp", "table"), split_axis=0, concat_axis=0, tiled=True)


def on_device(
    table, last_update, item_owner, item_slot, neg_owner, neg_slot, seq_lengths, w_in, w_out
):
    devices = lax.axis_size(("dp", "table"))
    rows_dev = table.shape[0]
    width = table.shape[1]
    capacity = max(2, 2 * TOK_DEV // devices) + max(2, 2 * NNEG // devices)
    owners = jnp.concatenate([item_owner[:, 0], neg_owner[:, 0]])
    slots = jnp.concatenate([item_slot, neg_slot])
    count = owners.shape[0]
    onehot = (owners[:, None] == jnp.arange(devices, dtype=jnp.int32)[None, :]).astype(jnp.int32)
    rank = jnp.sum(jnp.cumsum(onehot, 0) * onehot, 1) - 1
    requests = jnp.full((devices, capacity), -1, jnp.int32).at[owners, rank].set(slots)
    source = (
        jnp.full((devices, capacity), count, jnp.int32)
        .at[owners, rank]
        .set(jnp.arange(count, dtype=jnp.int32))
    )
    incoming = send_ids(requests)
    present = (incoming >= 0).astype(jnp.float32)
    local = jnp.clip(incoming, 0, rows_dev - 1)
    fade = jnp.power(jnp.float32(RHO), (NOW - last_update[local]).astype(jnp.float32)) * present
    served = (table[local].astype(jnp.float32) * fade[..., None]).astype(jnp.bfloat16)
    returned = send_rows(served)
    rows32 = returned[owners, rank].astype(jnp.float32)
    w_in32 = w_in.astype(jnp.float32)
    w_out32 = w_out.astype(jnp.float32)
    fn = partial(lambda r, a, b, s: layer_loss(r, a, b, s), s=seq_lengths[0])
    total, pull, losses = jax.vjp(fn, rows32, w_in32, w_out32, has_aux=True)
    grad_rows, grad_a, grad_b = pull(jnp.float32(1.0))
    grad_in, grad_out = lax.psum((grad_a, grad_b), ("dp", "table"))
    padded = jnp.concatenate([grad_rows, jnp.zeros((1, width), jnp.float32)], 0)
    outgoing = padded[source]
    arrived = send_grads(outgoing)
    contrib = (arrived * fade[..., None]).reshape(-1, width)
    high = contrib.astype(jnp.bfloat16)
    remain = contrib - high.astype(jnp.float32)
    middle = remain.astype(jnp.bfloat16)
    lowest = (remain - middle.astype(jnp.float32)).astype(jnp.bfloat16)
    stacked = jnp.concatenate([high, middle, lowest], 1)
    selector = (jnp.arange(rows_dev, dtype=jnp.int32)[:, None] == local.reshape(1, -1)).astype(
        jnp.bfloat16
    )
    summed = jnp.dot(selector, stacked, preferred_element_type=jnp.float32)
    table_grad = summed[:, :width] + summed[:, width : 2 * width] + summed[:, 2 * width :]
    return (losses, table_grad, grad_in, grad_out)


def solution(mesh):
    placed = (
        P(("dp", "table"), None),
        P(("dp", "table")),
        P(("dp", "table"), None),
        P(("dp", "table")),
        P(("dp", "table"), None),
        P(("dp", "table")),
        P(("dp", "table"), None),
        P(),
        P(),
    )
    return jax.shard_map(
        on_device,
        mesh=mesh,
        in_specs=placed,
        out_specs=(P(("dp", "table")), P(("dp", "table"), None), P(), P()),
        check_vma=False,
    )
```

profile of v0, /device:TPU:1, one launch (start us, length us, event | category | flops | bytes accessed | tf_op | source)
XLA Modules:
  0.0 416.3 jit_solution(11183208753842124814)
XLA Ops:
  7.2 0.8 constant_dynamic-update-slice_fusion.1
  8.0 0.7 constant_dynamic-update-slice_fusion
  8.7 0.7 pad_add_fusion.1
  10.2 0.7 pad_add_fusion.2
  10.9 33.2 %scatter_fusion = s32[128,10]{0,1:T(8,128)S(1)} fusion(s32[128,10]{0,1:T(8,128)S(1)} %broadcast_in_dim.18, s32[640]{0:T(1024)S(1)} %get-tuple-element.5, s32[640]{0:T(1024)S(1)} %pad_add_fusion.2), kind=kCustom, calls=%fused_computation.4 | custom fusion | bytes 12800 | tf_op jit(solution)/shard_map/scatter | solution.py:89
  44.3 20.9 %all_to_all.19 = s32[128,1,10]{2,1,0:T(1,128)S(1)} all-to-all(s32[128,1,10]{2,1,0:T(1,128)S(1)} %copy.71), channel_id=1, replica_groups=mesh['dp'=8,'table'=16] {'dp','table'}, dimensions={0} | all-to-all | bytes 10240 | tf_op jit(solution)/shard_map/all_to_all | solution.py:66
  65.3 6.9 %gather_fusion = bf16[1280,512]{1,0:T(8,128)(2,1)S(1)} fusion(bf16[4096,512]{1,0:T(8,128)(2,1)} %param.9, s32[2048]{0:T(1024)S(1)} %pad_clamp_fusion.1), kind=kCustom, calls=%fused_computation | custom fusion | bytes 2626560 | tf_op jit(solution)/shard_map/gather | solution.py:99
  72.2 2.2 reshape.367
  74.4 7.1 %gather_fusion.1 = s32[1280]{0:T(1024)S(1)} fusion(s32[4096]{0:T(1024)S(1)} %copy-done.2, s32[2048]{0:T(1024)S(1)} %pad_clamp_fusion.1), kind=kCustom, calls=%fused_computation.1 | custom fusion | bytes 15360 | tf_op jit(solution)/shard_map/gather | solution.py:98
  81.7 3.9 multiply_convert_fusion.2
  85.6 5.5 %all-to-all-start.1 = ((bf16[128,10,512]{2,1,0:T(8,128)(2,1)}), bf16[128,10,512]{2,1,0:T(8,128)(2,1)}, u32[]{:S(2)}, u32[]{:S(2)}) async-start(bf16[128,10,512]{2,1,0:T(8,128)(2,1)} %multiply_convert_fusion.2), calls=%async_computation.1 | async-start | bytes 4194304 | tf_op jit(solution)/shard_map/all_to_all | solution.py:70
  91.3 33.2 %scatter_fusion.1 = s32[128,10]{0,1:T(8,128)S(1)} fusion(s32[128,10]{0,1:T(8,128)S(1)} %broadcast_in_dim.25, s32[640]{0:T(1024)S(1)} %get-tuple-element.5, s32[640]{0:T(1024)S(1)} %iota.30), kind=kCustom, calls=%fused_computation.5 | custom fusion | bytes 12800 | tf_op jit(solution)/shard_map/scatter | solution.py:93
  125.0 1.2 fusion.25
  126.1 1.2 fusion.24
  127.3 2.3 copy.74
  129.6 7.3 %gather_fusion.2 = bf16[640,512]{1,0:T(8,128)(2,1)} fusion(bf16[128,10,512]{2,0,1:T(8,128)(2,1)S(1)} %copy.74, s32[640]{0:T(1024)S(1)} %get-tuple-element.4), kind=kCustom, calls=%fused_computation.2 | custom fusion | bytes 1315840 | tf_op jit(solution)/shard_map/gather | solution.py:101
  137.0 2.2 slice.56
  139.1 1.2 convert_element_type.151
  140.8 3.7 multiply_convert_fusion.1
  144.5 1.3 copy-done.11
  145.8 1.2 slice_bitcast_fusion
  147.1 2.1 copy.97
  149.2 2.0 copy.98
  151.2 4.9 %multiply_convert_fusion = (bf16[4,512,512]{2,1,0:T(8,128)(2,1)S(1)}, f32[4,512,512]{2,1,0:T(8,128)}) fusion(f32[512,512]{1,0:T(8,128)} %fusion.25, bf16[512,4,128]{0,2,1:T(8,128)(2,1)} %bitcast.94, bf16[512,4,128]{0,2,1:T(8,128)(2,1)} %bitcast.96), kind=kOutput, calls=%fused_computation.19 | convolution fusion | flops 274726912 | bytes 8388608 | tf_op jit(solution)/shard_map/jvp(qhd,khd->hqk)/dot_general | solution.py:41
  156.1 1.3 copy-done.5
  157.4 1.8 fusion.59
  159.3 2.6 copy.91
  161.9 1.4 fusion.20
  163.2 1.7 fusion.16
  165.0 2.1 multiply_reduce_fusion.1
  167.1 1.2 fusion.60
  168.3 1.1 convert_element_type.158
  169.6 0.7 fusion.47
  170.2 1.4 fusion.15
  171.6 0.8 copy-done.9
  172.4 0.6 multiply_reduce_fusion
  173.1 1.4 fusion.57
  174.5 2.6 fusion.5
  177.1 1.2 fusion.61
  178.4 1.6 fusion.62
  180.0 1.4 convolution_convert_fusion.5
  181.3 0.9 convolution_convert_fusion.8
  182.2 2.1 copy.96
  184.3 2.0 copy.95
  186.3 2.0 copy.94
  188.4 3.6 fusion.2
  192.0 1.5 fusion.18
  194.1 0.5 copy-done.10
  195.3 4.4 %gather_fusion.3 = f32[1280,512]{1,0:T(8,128)} fusion(f32[641,512]{1,0:T(8,128)S(1)} %concatenate.54, s32[2048]{0:T(1024)S(1)} %pad_clamp_fusion), kind=kCustom, calls=%fused_computation.3 | custom fusion | bytes 5248000 | tf_op jit(solution)/shard_map/gather | solution.py:109
  199.7 4.3 %reshape.344 = f32[128,10,512]{2,1,0:T(8,128)} reshape(f32[1280,512]{1,0:T(8,128)} %gather_fusion.3) | data formatting | bytes 5242880 | tf_op jit(solution)/shard_map/gather | solution.py:109
  204.0 10.4 %all-to-all-start.2 = ((f32[128,10,512]{2,1,0:T(8,128)}), f32[128,10,512]{2,1,0:T(8,128)}, u32[]{:S(2)}, u32[]{:S(2)}) async-start(f32[128,10,512]{2,1,0:T(8,128)} %reshape.344), calls=%async_computation.2 | async-start | bytes 8388608 | tf_op jit(solution)/shard_map/all_to_all | solution.py:74
  214.5 0.6 broadcast_clamp_fusion
  215.1 1.0 min.15
  216.1 2.6 fusion.13
  218.7 3.4 fusion.11
  222.1 47.9 %all-to-all-done.2 = f32[128,10,512]{2,1,0:T(8,128)} async-done(((f32[128,10,512]{2,1,0:T(8,128)}), f32[128,10,512]{2,1,0:T(8,128)}, u32[]{:S(2)}, u32[]{:S(2)}) %all-to-all-start.2) | async-done | bytes 2621472 | tf_op jit(solution)/shard_map/all_to_all | solution.py:74
  270.0 4.6 %broadcast_multiply_fusion = f32[128,10,512]{2,1,0:T(8,128)} fusion(f32[128,10,512]{2,1,0:T(8,128)} %all-to-all-done.2, f32[128,10]{1,0:T(8,128)S(1)} %copy-done.23), kind=kLoop, calls=%fused_computation.33 | loop fusion | flops 655360 | bytes 5248000 | tf_op jit(solution)/shard_map/mul | solution.py:111
  274.7 4.6 %reshape.320 = f32[1280,512]{1,0:T(8,128)} reshape(f32[128,10,512]{2,1,0:T(8,128)} %broadcast_multiply_fusion) | data formatting | bytes 5242880 | tf_op jit(solution)/shard_map/reshape | solution.py:111
  279.2 3.3 fusion.58
  282.5 19.5 %fusion = f32[4096,1536]{1,0:T(8,128)} fusion(s32[1280]{0:T(1024)S(1)} %min.15, bf16[1280,512]{1,0:T(8,128)(2,1)S(1)} %get-tuple-element.15, bf16[1280,512]{1,0:T(8,128)(2,1)S(1)} %get-tuple-element.16, bf16[1280,512]{1,0:T(8,128)(2,1)S(1)} %get-tuple-element.14), kind=kOutput, calls=%fused_computation.7 | convolution fusion | flops 16123166720 | bytes 29103104 | tf_op jit(solution)/shard_map/dot_general | solution.py:120
  302.0 13.4 %slice_add_fusion = f32[4096,512]{1,0:T(8,128)} fusion(f32[4096,1536]{1,0:T(8,128)} %fusion), kind=kLoop, calls=%fused_computation.9 | loop fusion | flops 4194304 | bytes 33554432 | tf_op jit(solution)/shard_map/add | solution.py:121
  315.5 88.2 %all-reduce.8.cloned.1.call-done = (f32[512,2048]{1,0:T(8,128)}, f32[512,512]{1,0:T(8,128)}) async-done(((f32[512,2048]{1,0:T(8,128)}, f32[512,512]{1,0:T(8,128)}), (f32[512,2048]{1,0:T(8,128)}, f32[512,512]{1,0:T(8,128)})) %all-reduce.8.cloned.1.call-update) | async-done | bytes 5242896 | tf_op jit(solution)/shard_map/psum | solution.py:107
  403.7 4.9 %copy.124 = f32[512,2048]{1,0:T(8,128)} copy(f32[512,2048]{1,0:T(8,128)} %get-tuple-element.42) | data formatting | bytes 8388608
  408.5 1.0 copy.125
  (97 shorter events, 3.8 us)
Async XLA Ops:
  7.2 133.7 %copy-start = (bf16[512,2048]{1,0:T(8,128)(2,1)S(1)}, bf16[512,2048]{1,0:T(8,128)(2,1)}, u32[]{:S(2)}) copy-start(bf16[512,2048]{1,0:T(8,128)(2,1)} %param.16) | copy-start | bytes 6291460
  72.2 2.2 copy-start.2
  81.6 3.9 copy-start.22
  81.6 9.4 %copy-start.25 = (s32[1,4]{1,0:T(1,128)S(1)}, s32[1,4]{1,0:T(1,128)}, u32[]{:S(2)}) copy-start(s32[1,4]{1,0:T(1,128)} %param.15) | copy-start | bytes 52
  85.6 41.7 %all-to-all-start.1 = ((bf16[128,10,512]{2,1,0:T(8,128)(2,1)}), bf16[128,10,512]{2,1,0:T(8,128)(2,1)}, u32[]{:S(2)}, u32[]{:S(2)}) async-start(bf16[128,10,512]{2,1,0:T(8,128)(2,1)} %multiply_convert_fusion.2), calls=%async_computation.1 | async-start | bytes 4194304 | tf_op jit(solution)/shard_map/all_to_all | solution.py:70
  144.5 1.4 copy-start.11
  151.2 6.2 %copy-start.16 = (bf16[64,4,8,128]{3,2,1,0:T(8,128)(2,1)S(1)}, bf16[64,4,8,128]{3,2,1,0:T(8,128)(2,1)}, u32[]{:S(2)}) copy-start(bf16[64,4,8,128]{3,2,1,0:T(8,128)(2,1)} %get-tuple-element.17) | copy-start | bytes 1572868
  156.1 1.3 copy-start.5
  163.2 7.0 %copy-start.4 = (f32[511,512]{1,0:T(8,128)S(1)}, f32[511,512]{1,0:T(8,128)}, u32[]{:S(2)}) copy-start(f32[511,512]{1,0:T(8,128)} %slice.56) | copy-start | bytes 3139588
  164.9 5.3 %copy-start.13 = (bf16[512,512]{1,0:T(8,128)(2,1)}, bf16[512,512]{1,0:T(8,128)(2,1)S(1)}, u32[]{:S(2)}) copy-start(bf16[512,512]{1,0:T(8,128)(2,1)S(1)} %fusion.16) | copy-start | bytes 1572868
  165.0 7.5 %copy-start.3 = (f32[512,512]{1,0:T(8,128)S(1)}, f32[512,512]{1,0:T(8,128)}, u32[]{:S(2)}) copy-start(f32[512,512]{1,0:T(8,128)} %copy.91) | copy-start | bytes 3145732
  165.0 7.5 %copy-start.12 = (bf16[512,2048]{1,0:T(8,128)(2,1)S(1)}, bf16[512,2048]{1,0:T(8,128)(2,1)}, u32[]{:S(2)}) copy-start(bf16[512,2048]{1,0:T(8,128)(2,1)} %copy-done.11) | copy-start | bytes 6291460
  165.0 7.5 %copy-start.15 = (bf16[512,512]{1,0:T(8,128)(2,1)S(1)}, bf16[512,512]{1,0:T(8,128)(2,1)}, u32[]{:S(2)}) copy-start(bf16[512,512]{1,0:T(8,128)(2,1)} %param.17) | copy-start | bytes 1572868
  170.2 4.2 %copy-start.17 = (bf16[64,4,8,128]{3,2,1,0:T(8,128)(2,1)S(1)}, bf16[64,4,8,128]{3,2,1,0:T(8,128)(2,1)}, u32[]{:S(2)}) copy-start(bf16[64,4,8,128]{3,2,1,0:T(8,128)(2,1)} %get-tuple-element.17) | copy-start | bytes 1572868
  170.2 4.2 %copy-start.20 = (f32[512,512]{1,0:T(8,128)S(1)}, f32[512,512]{1,0:T(8,128)}, u32[]{:S(2)}) copy-start(f32[512,512]{1,0:T(8,128)} %fusion.24) | copy-start | bytes 3145732
  170.2 4.2 %copy-start.26 = (f32[4,512,512]{2,1,0:T(8,128)S(1)}, f32[4,512,512]{2,1,0:T(8,128)}, u32[]{:S(2)}) copy-start(f32[4,512,512]{2,1,0:T(8,128)} %get-tuple-element.29) | copy-start | bytes 12582916
  171.6 0.8 copy-start.9
  174.4 2.6 copy-start.18
  174.4 3.9 copy-start.19
  177.1 2.9 copy-start.6
  192.0 1.5 copy-start.7
  192.0 2.0 copy-start.14
  193.5 1.1 copy-start.10
  193.5 1.6 copy-start.24
  204.0 14.7 %copy-start.8 = (bf16[512,2048]{1,0:T(8,128)(2,1)S(1)}, bf16[512,2048]{1,0:T(8,128)(2,1)}, u32[]{:S(2)}) copy-start(bf16[512,2048]{1,0:T(8,128)(2,1)} %copy-done.7) | copy-start | bytes 6291460
  204.0 66.0 %all-to-all-start.2 = ((f32[128,10,512]{2,1,0:T(8,128)}), f32[128,10,512]{2,1,0:T(8,128)}, u32[]{:S(2)}, u32[]{:S(2)}) async-start(f32[128,10,512]{2,1,0:T(8,128)} %reshape.344), calls=%async_computation.2 | async-start | bytes 8388608 | tf_op jit(solution)/shard_map/all_to_all | solution.py:74
  214.4 189.3 %all-reduce.8.cloned.1.call-start = ((), (), s32[]{:S(2)}) async-start(), calls=%async_computation.3 | async-start | bytes 10485760 | tf_op jit(solution)/shard_map/psum | solution.py:107
  222.1 48.0 %copy-start.23 = (f32[128,10]{1,0:T(8,128)S(1)}, f32[128,10]{1,0:T(8,128)}, u32[]{:S(2)}) copy-start(f32[128,10]{1,0:T(8,128)} %copy-done.22) | copy-start | bytes 15364
  403.7 5.8 %copy-start.1 = (bf16[512,2048]{1,0:T(8,128)(2,1)S(1)}, bf16[512,2048]{1,0:T(8,128)(2,1)}, u32[]{:S(2)}) copy-start(bf16[512,2048]{1,0:T(8,128)(2,1)} %param.16) | copy-start | bytes 6291460
  403.7 4.9 %copy-start.21 = (f32[512,512]{1,0:T(8,128)S(1)}, f32[512,512]{1,0:T(8,128)}, u32[]{:S(2)}) copy-start(f32[512,512]{1,0:T(8,128)} %get-tuple-element.43) | copy-start | bytes 3145732
Sparse Core Ops, SparseCore 0:
  222.2 181.4 all-reduce.7
where the time goes:
time: 418 us; the launch traced here: 416 us
  waiting for transfers between devices  136 us (33%)
  local copies, waits for them, and re-layouts  135 us (32%)
  matrix products  50.5 us (12%)
  other arithmetic  43.4 us (10%)
  blocking collectives  20.9 us (5%)
  starting transfers between devices  15.9 us (4%)
  between operations  14.5 us (3%)
    psum x1, waiting for transfers between devices, on_device(): grad_in, grad_out = lax.psum((grad_a, grad_b), ('dp', 'table'))  88.2 us
    all_to_all x1, waiting for transfers between devices, send_grads(): lax.all_to_all(values, ('dp', 'table'), split_axis=0, concat_axis=0, tile...  47.9 us
    scatter x1, local copies, waits for them, and re-layouts, on_device(): source = jnp.full((devices, capacity), count, jnp.int32).at[owners, rank]...  33.2 us
    scatter x1, local copies, waits for them, and re-layouts, on_device(): jnp.full((devices, capacity), -1, jnp.int32).at[owners, rank].set(slots)  33.2 us
    all_to_all x1, blocking collectives, send_ids(): lax.all_to_all(values, ('dp', 'table'), split_axis=0, concat_axis=0, tile...  20.9 us
    dot_general x1, matrix products, on_device(): summed = jnp.dot(selector, stacked, preferred_element_type=jnp.float32)  19.5 us
    add x1, other arithmetic, on_device(): summed[:, :width] + summed[:, width:2 * width] + summed[:, 2 * width:]  13.4 us
    unnamed x58, local copies, waits for them, and re-layouts  11.9 us
  transfers between devices with their start and end apart: 3, of which 2 were waited for; matrix products, arithmetic and copies ran while one was open for 21% of the time, Pallas kernels for 0%

commit v1 on v0

v1 whole, which is shorter than its diff:
```python
import functools

import jax
import jax.numpy as jnp
from jax import lax
from jax.experimental import pallas as pl
from jax.experimental.pallas import tpu as pltpu
from jax.sharding import PartitionSpec as P

D = 512
H = 4
DH = 128
TOK = 512
NEG = 128
ALL = TOK + NEG
DEV = 128
CAP = 10
MSG = 48
LMAX = 256
NOW = 64
ROWS = 4096
WIDE = 5 * D
LOG_RHO = -0.030459207484708574
TAU = 0.125
EPS = 1e-05
MESH = pl.DeviceIdType.MESH
VMEM = pl.BlockSpec(memory_space=pltpu.VMEM)
ANY = pl.BlockSpec(memory_space=pl.ANY)
F32 = jnp.float32
BF16 = jnp.bfloat16
PARTS = ((0, 896), (896, 896), (1792, 768))


def nt(a, b):
    return lax.dot_general(a, b, (((1,), (1,)), ((), ())), preferred_element_type=F32)


def nn(a, b):
    return jnp.dot(a, b, preferred_element_type=F32)


def tn(a, b):
    return lax.dot_general(a, b, (((0,), (0,)), ((), ())), preferred_element_type=F32)


def iota(shape, dim):
    return lax.broadcasted_iota(jnp.int32, shape, dim)


class Place:
    def __init__(self):
        self.dp = lax.axis_index("dp")
        self.tb = lax.axis_index("table")
        self.me = self.dp * 16 + self.tb
        self.z = self.dp // 2
        self.core = lax.rem(self.dp, 2)
        self.x = self.tb // 4
        self.y = lax.rem(self.tb, 4)

    def along(self, axis, shift):
        z, x, y = self.z, self.x, self.y
        if axis == "z":
            z = lax.rem(z + shift, 4)
        if axis == "x":
            x = lax.rem(x + shift, 4)
        if axis == "y":
            y = lax.rem(y + shift, 4)
        return (z * 2 + self.core, x * 4 + y)

    def sibling(self):
        return (self.z * 2 + 1 - self.core, self.tb)


def announce(place):
    barrier = pltpu.get_barrier_semaphore()

    def greet(k, carry):
        other = lax.rem(place.me + k, DEV)
        pl.semaphore_signal(
            barrier, inc=1, device_id=(other // 16, lax.rem(other, 16)), device_id_type=MESH
        )
        return carry

    lax.fori_loop(1, DEV, greet, 0)
    return barrier


def peers(place, c):
    zs = [lax.rem(place.z + j, 4) * 2 for j in range(4)]
    xs = [lax.rem(place.x + j, 4) * 4 for j in range(4)]
    ys = [lax.rem(place.y + c + j, 4) for j in range(4)]
    cores = [place.core, 1 - place.core]
    return [
        (zs[a] + cores[k], xs[(a + b) % 4] + ys[a])
        for b in range(4)
        for a in range(4)
        for k in range(2)
    ]


def fetch_kernel(
    item_owner,
    neg_owner,
    item_slot,
    neg_slot,
    table_ref,
    update_ref,
    rows_ref,
    ids_ref,
    pos_ref,
    table_vmem,
    faded,
    asked,
    stage,
    outbox,
    local_sem,
    id_send,
    id_recv,
    row_send,
    row_recv,
):
    place = Place()
    load = pltpu.make_async_copy(table_ref, table_vmem, local_sem)
    load.start()
    barrier = announce(place)
    owner = jnp.concatenate([item_owner[...], neg_owner[...]], 1)
    slot = jnp.concatenate([item_slot[...], neg_slot[...]], 1)
    onehot = (iota((DEV, ALL), 0) == owner).astype(F32)
    upto = (iota((ALL, ALL), 0) <= iota((ALL, ALL), 1)).astype(F32).astype(BF16)
    count = nn(onehot.astype(BF16), upto)
    rank = jnp.sum(onehot * count, 0, keepdims=True).astype(jnp.int32) - 1
    ranked = (iota((DEV, ALL), 0) == rank).astype(F32).astype(BF16)
    high = (onehot * (slot // 64).astype(F32)).astype(BF16)
    low = (onehot * (slot % 64).astype(F32)).astype(BF16)
    asked[...] = (64.0 * nt(high, ranked) + nt(low, ranked)).astype(jnp.int32)
    pos_ref[...] = rank * DEV + owner
    pl.semaphore_wait(barrier, DEV - 1)

    def ask(c, carry):
        for k, (d, t) in enumerate(peers(place, c)):

            def send(d=d, t=t):
                pltpu.make_async_remote_copy(
                    src_ref=asked.at[pl.ds(d * 16 + t, 1)],
                    dst_ref=ids_ref.at[pl.ds(place.me, 1)],
                    send_sem=id_send,
                    recv_sem=id_recv,
                    device_id=(d, t),
                    device_id_type=MESH,
                ).start()

            if k == 0:
                pl.when(c > 0)(send)
            else:
                send()
        return carry

    lax.fori_loop(0, 4, ask, 0)
    ids_ref[pl.ds(place.me, 1), :] = asked[pl.ds(place.me, 1), :]
    fade = jnp.exp((NOW - update_ref[...]).astype(F32) * LOG_RHO)
    fade = jnp.transpose(jnp.concatenate([fade, jnp.zeros((96, 128), F32)], 0))
    load.wait()
    for c in range(32):
        block = table_vmem[c * 128 : (c + 1) * 128, :].astype(F32) * fade[:, c : c + 1]
        faded[c * 128 : (c + 1) * 128, :] = block.astype(BF16)
    most = asked.at[pl.ds(0, DEV - 1)]
    pltpu.make_async_copy(most, most, id_send).wait()
    pltpu.make_async_copy(most, most, id_recv).wait()

    def serve(c, carry):
        group = peers(place, c)
        wanted = jnp.concatenate([ids_ref[pl.ds(d * 16 + t, 1), :] for d, t in group], 0)
        chosen = [
            (iota((32, ROWS), 1) == wanted[:, r : r + 1]).astype(F32).astype(BF16)
            for r in range(CAP)
        ]
        found = nn(jnp.concatenate(chosen, 0), faded[...])
        for r in range(CAP):
            for b in range(4):
                stage[pl.ds(4 * r + b, 32, stride=MSG), :] = found[
                    r * 32 : (r + 1) * 32, b * 128 : (b + 1) * 128
                ]
        base = c * 32
        outbox[pl.ds(base, 32)] = stage[...].astype(BF16).reshape(32, MSG, 128)
        for k, (d, t) in enumerate(group):

            def send(k=k, d=d, t=t):
                pltpu.make_async_remote_copy(
                    src_ref=outbox.at[base + k],
                    dst_ref=rows_ref.at[place.me],
                    send_sem=row_send,
                    recv_sem=row_recv,
                    device_id=(d, t),
                    device_id_type=MESH,
                ).start()

            if k == 0:
                pl.when(c > 0)(send)
            else:
                send()
        return carry

    for r in range(CAP * 4, MSG):
        stage[pl.ds(r, 32, stride=MSG), :] = jnp.zeros((32, 128), F32)
    lax.fori_loop(0, 4, serve, 0)
    rows_ref[place.me] = outbox[0]
    most = outbox.at[pl.ds(0, DEV - 1)]
    pltpu.make_async_copy(most, most, row_send).wait()
    pltpu.make_async_copy(most, most, row_recv).wait()


def fetch(item_owner, neg_owner, item_slot, neg_slot, table, update):
    return pl.pallas_call(
        fetch_kernel,
        out_shape=(
            jax.ShapeDtypeStruct((DEV, MSG, 128), BF16),
            jax.ShapeDtypeStruct((DEV, 128), jnp.int32),
            jax.ShapeDtypeStruct((1, ALL), jnp.int32),
        ),
        in_specs=[VMEM, VMEM, VMEM, VMEM, ANY, VMEM],
        out_specs=(VMEM, VMEM, VMEM),
        scratch_shapes=[
            pltpu.VMEM((ROWS, D), BF16),
            pltpu.VMEM((ROWS, D), BF16),
            pltpu.VMEM((DEV, 128), jnp.int32),
            pltpu.VMEM((32 * MSG, 128), F32),
            pltpu.VMEM((DEV, MSG, 128), BF16),
            pltpu.SemaphoreType.DMA,
            pltpu.SemaphoreType.DMA,
            pltpu.SemaphoreType.DMA,
            pltpu.SemaphoreType.DMA,
            pltpu.SemaphoreType.DMA,
        ],
        compiler_params=pltpu.CompilerParams(
            collective_id=0, has_side_effects=True, vmem_limit_bytes=50 << 20
        ),
        name="fetch",
    )(
        item_owner.reshape(1, TOK),
        neg_owner.reshape(1, NEG),
        item_slot.reshape(1, TOK),
        neg_slot.reshape(1, NEG),
        table,
        update,
    )


def reduce_kernel(
    box_ref,
    grad_ref,
    arrived_ref,
    total_ref,
    half,
    acc0,
    acc1,
    acc2,
    in1,
    in2,
    in3,
    row_send,
    row_recv,
    core_send,
    core_recv,
    step_send,
    step_recv,
):
    place = Place()
    barrier = announce(place)
    arrived_ref[place.me] = box_ref[place.me]
    pl.semaphore_wait(barrier, DEV - 1)
    mine = pl.multiple_of(place.core * 256, 256)
    other = pl.multiple_of((1 - place.core) * 256, 256)
    swap = pltpu.make_async_remote_copy(
        src_ref=grad_ref.at[pl.ds(other, 256)],
        dst_ref=half,
        send_sem=core_send.at[0],
        recv_sem=core_recv.at[0],
        device_id=place.sibling(),
        device_id_type=MESH,
    )
    swap.start()

    def post(c):
        for k, (d, t) in enumerate(peers(place, c)):
            if c == 0 and k == 0:
                continue
            pltpu.make_async_remote_copy(
                src_ref=box_ref.at[d * 16 + t],
                dst_ref=arrived_ref.at[place.me],
                send_sem=row_send,
                recv_sem=row_recv,
                device_id=(d, t),
                device_id_type=MESH,
            ).start()

    coordinate = {"x": place.x, "y": place.y, "z": place.z}
    axes = (("x", "y", "z"), ("y", "z", "x"), ("z", "x", "y"))

    def send(p, step, shift, src, dst):
        copy = pltpu.make_async_remote_copy(
            src_ref=src,
            dst_ref=dst,
            send_sem=step_send.at[p, step, shift - 1],
            recv_sem=step_recv.at[p, step, shift - 1],
            device_id=place.along(axes[p][(0, 1, 2, 1, 0)[step]], shift),
            device_id_type=MESH,
        )
        copy.start()
        return copy

    post(0)
    swap.wait()
    acc0[...] = (grad_ref[pl.ds(mine, 256), :].astype(F32) + half[...].astype(F32)).astype(BF16)
    first = []
    for p, (start, width) in enumerate(PARTS):
        at = coordinate[axes[p][0]]
        cols = pl.ds(start, width)
        for shift in (1, 2, 3):
            to = pl.multiple_of(lax.rem(at + shift, 4) * 64, 64)
            first.append(
                send(p, 0, shift, acc0.at[pl.ds(to, 64), cols], in1.at[shift - 1, :, cols])
            )
    post(1)
    second = []
    for p, (start, width) in enumerate(PARTS):
        at = coordinate[axes[p][0]]
        cols = pl.ds(start, width)
        for copy in first[3 * p : 3 * p + 3]:
            copy.wait()
        total = acc0[pl.ds(pl.multiple_of(at * 64, 64), 64), cols].astype(F32)
        for k in range(3):
            total += in1[k, :, cols].astype(F32)
        acc1[:, cols] = total.astype(BF16)
        at = coordinate[axes[p][1]]
        for shift in (1, 2, 3):
            to = pl.multiple_of(lax.rem(at + shift, 4) * 16, 16)
            second.append(
                send(p, 1, shift, acc1.at[pl.ds(to, 16), cols], in2.at[shift - 1, :, cols])
            )
    post(2)
    third = []
    for p, (start, width) in enumerate(PARTS):
        at = coordinate[axes[p][1]]
        cols = pl.ds(start, width)
        for copy in second[3 * p : 3 * p + 3]:
            copy.wait()
        total = acc1[pl.ds(pl.multiple_of(at * 16, 16), 16), cols].astype(F32)
        for k in range(3):
            total += in2[k, :, cols].astype(F32)
        acc2[:, cols] = total.astype(BF16)
        at = coordinate[axes[p][2]]
        in3[at, :, cols] = acc2[:, cols]
        for shift in (1, 2, 3):
            third.append(send(p, 2, shift, acc2.at[:, cols], in3.at[at, :, cols]))
    post(3)
    fourth = []
    places = []
    for p, (start, width) in enumerate(PARTS):
        cols = pl.ds(start, width)
        for copy in third[3 * p : 3 * p + 3]:
            copy.wait()
        total = in3[0, :, cols].astype(F32)
        for k in range(1, 4):
            total += in3[k, :, cols].astype(F32)
        wide = pl.multiple_of(mine + coordinate[axes[p][0]] * 64, 64)
        narrow = pl.multiple_of(wide + coordinate[axes[p][1]] * 16, 16)
        places.append(wide)
        total_ref[pl.ds(narrow, 16), cols] = total.astype(BF16)
        piece = total_ref.at[pl.ds(narrow, 16), cols]
        for shift in (1, 2, 3):
            fourth.append(send(p, 3, shift, piece, piece))
    fifth = []
    for p, (start, width) in enumerate(PARTS):
        for copy in fourth[3 * p : 3 * p + 3]:
            copy.wait()
        piece = total_ref.at[pl.ds(places[p], 64), pl.ds(start, width)]
        for shift in (1, 2, 3):
            fifth.append(send(p, 4, shift, piece, piece))
    last = []
    for p, (start, width) in enumerate(PARTS):
        for copy in fifth[3 * p : 3 * p + 3]:
            copy.wait()
        piece = total_ref.at[pl.ds(mine, 256), pl.ds(start, width)]
        copy = pltpu.make_async_remote_copy(
            src_ref=piece,
            dst_ref=piece,
            send_sem=core_send.at[p + 1],
            recv_sem=core_recv.at[p + 1],
            device_id=place.sibling(),
            device_id_type=MESH,
        )
        copy.start()
        last.append(copy)
    for copy in last:
        copy.wait()
    most = box_ref.at[pl.ds(0, DEV - 1)]
    pltpu.make_async_copy(most, most, row_send).wait()
    pltpu.make_async_copy(most, most, row_recv).wait()


def reduce(box, grad):
    return pl.pallas_call(
        reduce_kernel,
        out_shape=(
            jax.ShapeDtypeStruct((DEV, MSG, 128), BF16),
            jax.ShapeDtypeStruct((D, WIDE), BF16),
        ),
        in_specs=[VMEM, VMEM],
        out_specs=(VMEM, VMEM),
        scratch_shapes=[
            pltpu.VMEM((256, WIDE), BF16),
            pltpu.VMEM((256, WIDE), BF16),
            pltpu.VMEM((64, WIDE), BF16),
            pltpu.VMEM((16, WIDE), BF16),
            pltpu.VMEM((3, 64, WIDE), BF16),
            pltpu.VMEM((3, 16, WIDE), BF16),
            pltpu.VMEM((4, 16, WIDE), BF16),
            pltpu.SemaphoreType.DMA,
            pltpu.SemaphoreType.DMA,
            pltpu.SemaphoreType.DMA((4,)),
            pltpu.SemaphoreType.DMA((4,)),
            pltpu.SemaphoreType.DMA((3, 5, 3)),
            pltpu.SemaphoreType.DMA((3, 5, 3)),
        ],
        compiler_params=pltpu.CompilerParams(
            collective_id=1, has_side_effects=True, vmem_limit_bytes=48 << 20
        ),
        name="reduce",
    )(box, grad)


def scatter_kernel(arrived_ref, ids_ref, update_ref, out_ref, wide, rows, slots):
    step = pl.program_id(0)

    @pl.when(step == 0)
    def _():
        for s in range(8):
            block = arrived_ref[s * 16 : (s + 1) * 16].astype(F32)
            wide[s * 16 * MSG : (s + 1) * 16 * MSG, :] = block.reshape(16 * MSG, 128)
        for c in range(CAP):
            for b in range(4):
                piece = wide[pl.ds(4 * c + b, DEV, stride=MSG), :]
                rows[c * 128 : (c + 1) * 128, b * 128 : (b + 1) * 128] = piece.astype(BF16)
        slots[...] = jnp.transpose(ids_ref[...])[:16, :]

    fade = jnp.exp((NOW - update_ref[...]).astype(F32) * LOG_RHO)
    fade = jnp.transpose(jnp.concatenate([fade, jnp.zeros((120, 128), F32)], 0))
    for s in range(8):
        first = step * 1024 + s * 128
        chosen = [
            (iota((128, 128), 0) + first == slots[c : c + 1, :]).astype(F32).astype(BF16)
            for c in range(CAP)
        ]
        summed = nn(jnp.concatenate(chosen, 1), rows[...])
        out_ref[s * 128 : (s + 1) * 128, :] = summed * fade[:, s : s + 1]


def scatter(arrived, ids, update):
    return pl.pallas_call(
        scatter_kernel,
        grid=(4,),
        out_shape=jax.ShapeDtypeStruct((ROWS, D), F32),
        in_specs=[
            pl.BlockSpec((DEV, MSG, 128), lambda i: (0, 0, 0)),
            pl.BlockSpec((DEV, 128), lambda i: (0, 0)),
            pl.BlockSpec((8, 128), lambda i: (i, 0)),
        ],
        out_specs=pl.BlockSpec((1024, D), lambda i: (i, 0)),
        scratch_shapes=[
            pltpu.VMEM((DEV * MSG, 128), F32),
            pltpu.VMEM((CAP * 128, D), BF16),
            pltpu.VMEM((16, 128), jnp.int32),
        ],
        compiler_params=pltpu.CompilerParams(vmem_limit_bytes=48 << 20),
        name="scatter",
    )(arrived, ids, update)


def normalize(values):
    center = values - jnp.mean(values, -1, keepdims=True)
    return center * lax.rsqrt(jnp.mean(center * center, -1, keepdims=True) + EPS)


def layer_loss(rows32, w_in32, w_out32, lengths):
    width = rows32.shape[1]
    x32 = rows32[:TOK]
    negatives = rows32[TOK:].astype(jnp.bfloat16)
    ends = jnp.cumsum(lengths)
    where = jnp.arange(TOK, dtype=jnp.int32)
    segment = jnp.sum((where[:, None] >= ends[None, :]).astype(jnp.int32), 1)
    normed = normalize(x32).astype(jnp.bfloat16)
    mixed = jax.nn.silu(
        jnp.dot(normed, w_in32.astype(jnp.bfloat16), preferred_element_type=jnp.float32)
    ).astype(jnp.bfloat16)
    gate_part, value, query, key_part = jnp.split(mixed, 4, axis=1)
    query = query.reshape(TOK, H, DH)
    key_part = key_part.reshape(TOK, H, DH)
    value = value.reshape(TOK, H, DH)
    scores = jnp.einsum("qhd,khd->hqk", query, key_part, preferred_element_type=jnp.float32)
    visible = (segment[:, None] == segment[None, :]) & (where[None, :] <= where[:, None])
    weights = (jax.nn.silu(scores) * (1.0 / LMAX) * visible[None].astype(jnp.float32)).astype(
        jnp.bfloat16
    )
    attended = jnp.einsum(
        "hqk,khd->qhd", weights, value, preferred_element_type=jnp.float32
    ).reshape(TOK, width)
    gated = (normalize(attended) * gate_part.astype(jnp.float32)).astype(jnp.bfloat16)
    out = (
        x32 + jnp.dot(gated, w_out32.astype(jnp.bfloat16), preferred_element_type=jnp.float32)
    ).astype(jnp.bfloat16)
    following = jnp.concatenate([x32[1:], jnp.zeros((1, width), jnp.float32)], 0)
    valid = jnp.concatenate([segment[1:] == segment[:-1], jnp.zeros((1,), bool)]).astype(
        jnp.float32
    )
    positive = jnp.sum(out.astype(jnp.float32) * following, 1) * TAU
    negative = jnp.dot(out, negatives.T, preferred_element_type=jnp.float32) * TAU
    top = lax.stop_gradient(jnp.maximum(positive, jnp.max(negative, 1)))
    total = jnp.exp(positive - top) + jnp.sum(jnp.exp(negative - top[:, None]), 1)
    losses = (jnp.log(total) + top - positive) * valid
    return (jnp.sum(losses), losses)


def layer(rows, pos, w_in, w_out, lengths):
    flat = rows[:, : 4 * CAP].reshape(DEV, CAP, D)
    owner, rank = pos[0] % DEV, pos[0] // DEV
    rows32 = flat[owner, rank].astype(F32)
    fn = lambda r, a, b: layer_loss(r, a, b, lengths)
    total, pull, losses = jax.vjp(fn, rows32, w_in.astype(F32), w_out.astype(F32), has_aux=True)
    grad_rows, grad_a, grad_b = pull(jnp.float32(1.0))
    chosen = (jnp.arange(CAP * DEV)[:, None] == pos).astype(BF16)
    sent = jnp.dot(chosen, grad_rows.astype(BF16), preferred_element_type=F32).astype(BF16)
    sent = sent.reshape(CAP, DEV, 4, 128).transpose(1, 0, 2, 3).reshape(DEV, 4 * CAP, 128)
    box = jnp.pad(sent, ((0, 0), (0, MSG - 4 * CAP), (0, 0)))
    grad = jnp.concatenate([grad_a, grad_b], 1).astype(BF16)
    return losses, box, grad


def on_device(
    table, last_update, item_owner, item_slot, neg_owner, neg_slot, seq_lengths, w_in, w_out
):
    update = last_update.reshape(ROWS // 128, 128)
    rows, ids, pos = fetch(item_owner, neg_owner, item_slot, neg_slot, table, update)
    losses, box, grad = layer(rows, pos, w_in, w_out, seq_lengths[0])
    arrived, total = reduce(box, grad)
    table_grad = scatter(arrived, ids, update)
    grad_in = total[:, : 4 * D].astype(F32)
    grad_out = total[:, 4 * D :].astype(F32)
    return (losses, table_grad, grad_in, grad_out)


def solution(mesh):
    placed = (
        P(("dp", "table"), None),
        P(("dp", "table")),
        P(("dp", "table"), None),
        P(("dp", "table")),
        P(("dp", "table"), None),
        P(("dp", "table")),
        P(("dp", "table"), None),
        P(),
        P(),
    )
    return jax.shard_map(
        on_device,
        mesh=mesh,
        in_specs=placed,
        out_specs=(P(("dp", "table")), P(("dp", "table"), None), P(), P()),
        check_vma=False,
    )
```

time: 418 us -> 189 us (0.45)
  waiting for transfers between devices: 136 us -> 0 us
  Pallas kernels: 0 us -> 100 us
  local copies, waits for them, and re-layouts: 135 us -> 38.2 us
  other arithmetic: 43.4 us -> 17.2 us
  blocking collectives: 20.9 us -> 0 us
  matrix products: 50.5 us -> 31.9 us
  starting transfers between devices: 15.9 us -> 0 us
  between operations: 14.5 us -> 1.07 us
    pallas_call x0 -> x3, Pallas kernels: none -> 100 us  [the longest x1 51 us: reduce(): pl.pallas_call(reduce_kernel, out_shape=(jax.ShapeDtypeStruct((DEV, MSG,...]
    psum x1 -> x0, waiting for transfers between devices: 88.2 us -> none  [on_device(): grad_in, grad_out = lax.psum((grad_a, grad_b), ('dp', 'table'))]
    scatter x2 -> x0, local copies, waits for them, and re-layouts: 66.5 us -> none  [the longest x1 33.2 us: on_device(): source = jnp.full((devices, capacity), count, jnp.int32).at[owners, rank]...]
    all_to_all x2 -> x0, waiting for transfers between devices: 47.9 us -> none  [the longest x1 47.9 us: send_grads(): lax.all_to_all(values, ('dp', 'table'), split_axis=0, concat_axis=0, tile...]
    all_to_all x1 -> x0, blocking collectives: 20.9 us -> none  [send_ids(): lax.all_to_all(values, ('dp', 'table'), split_axis=0, concat_axis=0, tile...]
    gather x5 -> x2, local copies, waits for them, and re-layouts: 30 us -> 9.55 us  [layer(): rows32 = flat[owner, rank].astype(F32)]
    dot_general x1, matrix products: 19.5 us -> 3.51 us  [layer(): jnp.dot(chosen, grad_rows.astype(BF16), preferred_element_type=F32)]
    all_to_all x2 -> x0, starting transfers between devices: 15.9 us -> none  [the longest x1 10.4 us: send_grads(): lax.all_to_all(values, ('dp', 'table'), split_axis=0, concat_axis=0, tile...]
  transfers between devices with their start and end apart: 3 -> 0, of which waited for: 2 -> 0; matrix products, arithmetic and copies ran while one was open for 21% -> 0% of each run, Pallas kernels for 0% -> 0%
where the time goes in v1:
time: 189 us
  Pallas kernels  100 us (53%)
  local copies, waits for them, and re-layouts  38.2 us (20%)
  matrix products  31.9 us (17%)
  other arithmetic  17.2 us (9%)
    pallas_call x1, Pallas kernels, reduce(): pl.pallas_call(reduce_kernel, out_shape=(jax.ShapeDtypeStruct((DEV, MSG,...  51 us
    pallas_call x1, Pallas kernels, fetch(): pl.pallas_call(fetch_kernel, out_shape=(jax.ShapeDtypeStruct((DEV, MSG, 1...  40.2 us
    gather x2, local copies, waits for them, and re-layouts, layer(): rows32 = flat[owner, rank].astype(F32)  9.55 us
    dot_general x3, matrix products, layer_loss(): jnp.einsum('qhd,khd->hqk', query, key_part, preferred_element_type=jnp.fl...  9.48 us
    pallas_call x1, Pallas kernels, scatter(): pl.pallas_call(scatter_kernel, grid=(4,), out_shape=jax.ShapeDtypeStruct(...  9.09 us
    unnamed x57, local copies, waits for them, and re-layouts  8.63 us
    dot_general x3, matrix products, layer_loss(): jnp.einsum('hqk,khd->qhd', weights, value, preferred_element_type=jnp.flo...  7.01 us
    dot_general x3, matrix products, layer_loss(): jnp.dot(normed, w_in32.astype(jnp.bfloat16), preferred_element_type=jnp.f...  6.42 us

profile of v1, /device:TPU:1, one launch (start us, length us, event | category | flops | bytes accessed | tf_op | source)
XLA Modules:
  0.0 188.6 jit_solution(16948820413289127788)
XLA Ops:
  0.7 0.9 copy-done.1
  1.5 0.7 copy-done.3
  2.2 0.7 copy-done.4
  2.9 0.7 copy-done.5
  3.5 0.7 copy-done.6
  4.2 40.2 %fetch.1 = (bf16[128,48,128]{2,1,0:T(8,128)(2,1)S(1)}, s32[128,128]{1,0:T(8,128)S(1)}, s32[1,640]{1,0:T(1,128)S(1)}) custom-call(s32[1,512]{1,0:T(1,128)S(1)} %bitcast.93, s32[1,128]{1,0:T(1,128)S(1)} %bitcast.95, s32[1,512]{1,0:T(1,128)S(1)} %bitcast.94, s32[1,128]{1,0:T(1,128)S(1)} %bitcast.96, bf16[4096,512]{1,0:T(8,128)(2,1)} %table_ref.1, ...), custom_call_target="tpu_custom_call" | custom-call | tf_op jit(solution)/shard_map/fetch/pallas_call | solution.py:213
  44.4 0.1 slice.28
  44.6 1.9 %copy.50 = bf16[128,40,128]{0,2,1:T(8,128)(2,1)} copy(bf16[128,40,128]{2,1,0:T(8,128)(2,1)S(1)} %slice.28) | data formatting | bytes 2621440 | tf_op jit(solution)/shard_map/slice | solution.py:524
  46.5 1.6 copy.51
  48.1 7.4 %gather_fusion = bf16[640,512]{1,0:T(8,128)(2,1)} fusion(bf16[128,10,512]{2,0,1:T(8,128)(2,1)S(1)} %copy.51, s32[640]{0:T(1024)S(1)} %fusion.41), kind=kCustom, calls=%fused_computation | custom fusion | bytes 1315840 | tf_op jit(solution)/shard_map/gather | solution.py:526
  55.5 2.2 %copy.52 = bf16[640,512]{0,1:T(8,128)(2,1)} copy(bf16[640,512]{1,0:T(8,128)(2,1)} %gather_fusion) | data formatting | bytes 1310720 | tf_op jit(solution)/shard_map/gather | solution.py:526
  57.6 1.2 convert_element_type.124
  58.8 0.1 slice_reduce_fusion
  58.9 0.2 multiply_reduce_fusion.2
  59.1 3.9 %multiply_convert_fusion.1 = (bf16[512,2048]{1,0:T(8,128)(2,1)S(1)}, f32[512,2048]{1,0:T(8,128)}) fusion(bf16[512,2048]{1,0:T(8,128)(2,1)S(1)} %copy-done, f32[640,512]{0,1:T(8,128)S(1)} %convert_element_type.124, f32[512]{0:T(512)S(1)} %fusion.44, f32[512]{0:T(512)S(1)} %broadcast_multiply_fusion.1), kind=kOutput, calls=%fused_computation.11 | convolution fusion | flops 1079771136 | bytes 9441280 | tf_op jit(solution)/shard_map/jvp()/dot_general | solution.py:493
  62.9 1.3 copy-done.19
  64.3 1.2 slice_bitcast_fusion
  65.5 2.0 %copy.81 = bf16[512,512]{0,1:T(8,128)(2,1)} copy(bf16[512,512]{1,0:T(8,128)(2,1)} %get-tuple-element.20) | data formatting | bytes 1048576 | tf_op jit(solution)/shard_map/jvp()/reshape | solution.py:496
  67.5 2.1 %copy.82 = bf16[512,512]{0,1:T(8,128)(2,1)} copy(bf16[512,512]{1,0:T(8,128)(2,1)} %get-tuple-element.19) | data formatting | bytes 1048576 | tf_op jit(solution)/shard_map/jvp()/reshape | solution.py:497
  69.6 0.2 reduce-window.8
  69.7 0.1 convert_reduce_fusion
  69.8 0.2 fusion.18
  70.0 4.7 %multiply_convert_fusion = (bf16[4,512,512]{2,1,0:T(8,128)(2,1)S(1)}, f32[4,512,512]{2,1,0:T(8,128)}) fusion(f32[512,512]{1,0:T(8,128)S(1)} %fusion.18, bf16[512,4,128]{0,2,1:T(8,128)(2,1)} %bitcast.101, bf16[512,4,128]{0,2,1:T(8,128)(2,1)} %bitcast.103), kind=kOutput, calls=%fused_computation.9 | convolution fusion | flops 274726912 | bytes 8388608 | tf_op jit(solution)/shard_map/jvp(qhd,khd->hqk)/dot_general | solution.py:499
  74.7 0.8 fusion.51
  75.6 0.9 copy-done.8
  76.5 0.2 fusion.13
  76.7 2.6 %copy.75 = f32[512,512]{1,0:T(8,128)} copy(f32[512,512]{0,1:T(8,128)} %bitcast.97) | data formatting | bytes 2097152 | tf_op jit(solution)/shard_map/jvp()/reshape | solution.py:506
  79.4 1.7 fusion.9
  81.1 0.3 slice.37
  81.4 0.5 multiply_reduce_fusion.1
  82.0 1.6 fusion.52
  83.7 0.1 slice_compare_fusion
  83.7 0.7 fusion.43
  84.4 1.2 fusion.8
  85.7 0.6 multiply_reduce_fusion
  86.3 0.2 copy-done.15
  86.5 1.3 fusion.50
  87.9 1.4 convolution_convert_fusion.5
  89.3 2.0 %copy.78 = bf16[512,512]{1,0:T(8,128)(2,1)} copy(bf16[512,512]{0,1:T(8,128)(2,1)} %bitcast.100) | data formatting | bytes 1048576 | tf_op jit(solution)/shard_map/transpose(jvp())/reshape | solution.py:498
  91.3 0.2 fusion.17
  91.5 4.8 %fusion.3 = bf16[4,512,512]{2,1,0:T(8,128)(2,1)S(1)} fusion(f32[4,512,512]{2,1,0:T(8,128)} %get-tuple-element.26, f32[512,512]{1,0:T(8,128)S(1)} %fusion.17, bf16[64,4,8,128]{3,2,1,0:T(8,128)(2,1)} %get-tuple-element.18, f32[512,512]{1,0:T(8,128)} %copy-done.21, f32[512]{0:T(512)S(1)} %negate_multiply_fusion.1), kind=kOutput, calls=%fused_computation.8 | convolution fusion | flops 282591232 | bytes 8914944 | tf_op jit(solution)/shard_map/transpose(jvp(hqk,khd->qhd))/dot_general | solution.py:504
  96.4 1.3 copy-done.12
  97.7 1.6 fusion.54
  99.3 2.1 %copy.79 = bf16[512,512]{1,0:T(8,128)(2,1)} copy(bf16[512,512]{0,1:T(8,128)(2,1)} %bitcast.106) | data formatting | bytes 1048576 | tf_op jit(solution)/shard_map/transpose(jvp())/reshape | solution.py:496
  101.3 3.2 %fusion.53 = bf16[4,512,128]{1,2,0:T(8,128)(2,1)} fusion(bf16[4,512,512]{2,1,0:T(8,128)(2,1)} %copy-done.12, bf16[512,4,128]{0,2,1:T(8,128)(2,1)} %bitcast.102), kind=kOutput, calls=%fused_computation.126 | convolution fusion | flops 268435456 | bytes 3145728 | tf_op jit(solution)/shard_map/transpose(jvp(qhd,khd->hqk))/dot_general | solution.py:499
  104.5 2.0 %copy.80 = bf16[512,512]{1,0:T(8,128)(2,1)} copy(bf16[512,512]{0,1:T(8,128)(2,1)} %bitcast.105) | data formatting | bytes 1048576 | tf_op jit(solution)/shard_map/transpose(jvp())/reshape | solution.py:497
  106.6 3.6 %fusion = bf16[512,2048]{1,0:T(8,128)(2,1)S(1)} fusion(f32[512,2048]{1,0:T(8,128)} %get-tuple-element.24, bf16[512,512]{1,0:T(8,128)(2,1)} %copy.80, bf16[512,512]{1,0:T(8,128)(2,1)} %copy.79, bf16[512,512]{1,0:T(8,128)(2,1)} %copy.78, bf16[512,512]{1,0:T(8,128)(2,1)} %get-tuple-element.21), kind=kLoop, calls=%fused_computation.5 | loop fusion | flops 18874368 | bytes 8388608 | tf_op jit(solution)/shard_map/transpose(jvp(jit(silu)))/add_any | solution.py:492
  110.2 1.3 convolution_convert_fusion
  111.5 0.5 convolution_convert_fusion.1
  112.0 1.7 pad_maximum_fusion.grad_ref
  113.7 1.0 convolution_convert_fusion.8
  114.7 1.3 fusion.11
  116.0 0.3 fusion.25
  116.3 0.1 convert_element_type.131
  116.4 0.1 slice_multiply_fusion
  116.5 1.5 add_add_fusion.2
  118.0 3.5 %fusion.5 = bf16[1280,512]{1,0:T(8,128)(2,1)} fusion(s32[640]{0:T(1024)S(1)} %reduce.5, f32[512,512]{0,1:T(8,128)} %add_add_fusion.2, bf16[128,512]{0,1:T(8,128)(2,1)} %convolution_convert_fusion.8), kind=kOutput, calls=%fused_computation.16 | convolution fusion | flops 841318400 | bytes 2492928 | tf_op jit(solution)/shard_map/dot_general | solution.py:531
  121.5 2.7 %reshape.317 = bf16[10,128,4,128]{3,2,1,0:T(4,128)(2,1)S(1)} reshape(bf16[1280,512]{1,0:T(8,128)(2,1)} %fusion.5) | data formatting | bytes 2621440 | tf_op jit(solution)/shard_map/reshape | solution.py:532
  124.2 0.5 copy.68
  124.7 0.1 pad.21.box_ref
  124.8 51.0 %reduce.7 = (bf16[128,48,128]{2,1,0:T(8,128)(2,1)S(1)}, bf16[512,2560]{1,0:T(8,128)(2,1)S(1)}) custom-call(bf16[128,48,128]{2,1,0:T(8,128)(2,1)S(1)} %pad.21.box_ref, bf16[512,2560]{1,0:T(8,128)(2,1)} %pad_maximum_fusion.grad_ref), custom_call_target="tpu_custom_call" | custom-call | tf_op jit(solution)/shard_map/reduce/pallas_call | solution.py:402
  175.9 9.1 %scatter.1 = f32[4096,512]{1,0:T(8,128)} custom-call(bf16[128,48,128]{2,1,0:T(8,128)(2,1)S(1)} %get-tuple-element.11.arrived_ref, s32[128,128]{1,0:T(8,128)S(1)} %get-tuple-element.12.ids_ref, s32[32,128]{1,0:T(8,128)S(1)} %bitcast.92), custom_call_target="tpu_custom_call" | custom-call | tf_op jit(solution)/shard_map/scatter/pallas_call | solution.py:459
  185.0 2.6 %slice_convert_fusion = f32[512,2048]{1,0:T(8,128)} fusion(bf16[512,2560]{1,0:T(8,128)(2,1)S(1)} %get-tuple-element.13), kind=kLoop, calls=%fused_computation.18 | loop fusion | flops 1048576 | bytes 6291456 | tf_op jit(solution)/shard_map/convert_element_type | solution.py:546
  187.5 1.1 slice_convert_fusion.1
  (59 shorter events, 0.4 us)
Async XLA Ops:
  0.6 58.4 %copy-start = (bf16[512,2048]{1,0:T(8,128)(2,1)S(1)}, bf16[512,2048]{1,0:T(8,128)(2,1)}, u32[]{:S(2)}) copy-start(bf16[512,2048]{1,0:T(8,128)(2,1)} %param.16) | copy-start | bytes 6291460
  0.6 0.9 copy-start.1
  1.5 0.7 copy-start.3
  2.2 0.7 copy-start.4
  2.9 0.7 copy-start.5
  3.5 0.7 copy-start.6
  62.9 1.3 copy-start.19
  64.3 5.3 %copy-start.27 = (s32[1,4]{1,0:T(1,128)S(1)}, s32[1,4]{1,0:T(1,128)}, u32[]{:S(2)}) copy-start(s32[1,4]{1,0:T(1,128)} %param.15) | copy-start | bytes 52
  70.0 4.7 %copy-start.25 = (bf16[64,4,8,128]{3,2,1,0:T(8,128)(2,1)S(1)}, bf16[64,4,8,128]{3,2,1,0:T(8,128)(2,1)}, u32[]{:S(2)}) copy-start(bf16[64,4,8,128]{3,2,1,0:T(8,128)(2,1)} %get-tuple-element.18) | copy-start | bytes 1572868
  74.7 2.0 %copy-start.13 = (bf16[4,512,512]{2,1,0:T(8,128)(2,1)}, bf16[4,512,512]{2,1,0:T(8,128)(2,1)S(1)}, u32[]{:S(2)}) copy-start(bf16[4,512,512]{2,1,0:T(8,128)(2,1)S(1)} %get-tuple-element.25) | copy-start | bytes 6291460
  75.6 1.0 copy-start.8
  79.4 1.7 copy-start.9
  79.4 2.0 %copy-start.24 = (bf16[512,512]{1,0:T(8,128)(2,1)S(1)}, bf16[512,512]{1,0:T(8,128)(2,1)}, u32[]{:S(2)}) copy-start(bf16[512,512]{1,0:T(8,128)(2,1)} %param.17) | copy-start | bytes 1572868
  81.1 0.9 copy-start.17
  81.4 4.3 %copy-start.7 = (f32[512,512]{1,0:T(8,128)S(1)}, f32[512,512]{1,0:T(8,128)}, u32[]{:S(2)}) copy-start(f32[512,512]{1,0:T(8,128)} %copy.75) | copy-start | bytes 3145732
  81.4 4.3 %copy-start.20 = (bf16[512,2048]{1,0:T(8,128)(2,1)S(1)}, bf16[512,2048]{1,0:T(8,128)(2,1)}, u32[]{:S(2)}) copy-start(bf16[512,2048]{1,0:T(8,128)(2,1)} %copy-done.19) | copy-start | bytes 6291460
  81.9 4.4 %copy-start.10 = (bf16[512,512]{0,1:T(8,128)(2,1)}, bf16[512,512]{0,1:T(8,128)(2,1)S(1)}, u32[]{:S(2)}) copy-start(bf16[512,512]{0,1:T(8,128)(2,1)S(1)} %get-tuple-element.30) | copy-start | bytes 1572868
  83.6 2.7 %copy-start.22 = (f32[512,128]{0,1:T(8,128)}, f32[512,128]{0,1:T(8,128)S(1)}, u32[]{:S(2)}) copy-start(f32[512,128]{0,1:T(8,128)S(1)} %get-tuple-element.32) | copy-start | bytes 786436
  85.7 0.8 copy-start.15
  86.3 1.6 copy-start.14
  87.8 1.4 copy-start.21
  91.5 6.2 %copy-start.26 = (bf16[512,512]{0,1:T(8,128)(2,1)S(1)}, bf16[512,512]{0,1:T(8,128)(2,1)}, u32[]{:S(2)}) copy-start(bf16[512,512]{0,1:T(8,128)(2,1)} %copy.82) | copy-start | bytes 1572868
  96.3 1.3 copy-start.12
  110.2 1.3 copy-start.16
  110.2 1.3 copy-start.18
  112.0 1.7 copy-start.11
  112.0 1.7 copy-start.23
  124.8 51.0 %copy-start.2 = (s32[4096]{0:T(1024)S(1)}, s32[4096]{0:T(1024)}, u32[]{:S(2)}) copy-start(s32[4096]{0:T(1024)} %param.10) | copy-start | bytes 49156

commit v2 on v1

--- a/solution.py
+++ b/solution.py
@@ -476,63 +476,237 @@
     )(arrived, ids, update)
 
 
-def normalize(values):
-    center = values - jnp.mean(values, -1, keepdims=True)
-    return center * lax.rsqrt(jnp.mean(center * center, -1, keepdims=True) + EPS)
-
-
-def layer_loss(rows32, w_in32, w_out32, lengths):
-    width = rows32.shape[1]
-    x32 = rows32[:TOK]
-    negatives = rows32[TOK:].astype(jnp.bfloat16)
-    ends = jnp.cumsum(lengths)
-    where = jnp.arange(TOK, dtype=jnp.int32)
-    segment = jnp.sum((where[:, None] >= ends[None, :]).astype(jnp.int32), 1)
-    normed = normalize(x32).astype(jnp.bfloat16)
-    mixed = jax.nn.silu(
-        jnp.dot(normed, w_in32.astype(jnp.bfloat16), preferred_element_type=jnp.float32)
-    ).astype(jnp.bfloat16)
-    gate_part, value, query, key_part = jnp.split(mixed, 4, axis=1)
-    query = query.reshape(TOK, H, DH)
-    key_part = key_part.reshape(TOK, H, DH)
-    value = value.reshape(TOK, H, DH)
-    scores = jnp.einsum("qhd,khd->hqk", query, key_part, preferred_element_type=jnp.float32)
-    visible = (segment[:, None] == segment[None, :]) & (where[None, :] <= where[:, None])
-    weights = (jax.nn.silu(scores) * (1.0 / LMAX) * visible[None].astype(jnp.float32)).astype(
-        jnp.bfloat16
-    )
-    attended = jnp.einsum(
-        "hqk,khd->qhd", weights, value, preferred_element_type=jnp.float32
-    ).reshape(TOK, width)
-    gated = (normalize(attended) * gate_part.astype(jnp.float32)).astype(jnp.bfloat16)
-    out = (
-        x32 + jnp.dot(gated, w_out32.astype(jnp.bfloat16), preferred_element_type=jnp.float32)
-    ).astype(jnp.bfloat16)
-    following = jnp.concatenate([x32[1:], jnp.zeros((1, width), jnp.float32)], 0)
-    valid = jnp.concatenate([segment[1:] == segment[:-1], jnp.zeros((1,), bool)]).astype(
-        jnp.float32
-    )
-    positive = jnp.sum(out.astype(jnp.float32) * following, 1) * TAU
-    negative = jnp.dot(out, negatives.T, preferred_element_type=jnp.float32) * TAU
-    top = lax.stop_gradient(jnp.maximum(positive, jnp.max(negative, 1)))
-    total = jnp.exp(positive - top) + jnp.sum(jnp.exp(negative - top[:, None]), 1)
-    losses = (jnp.log(total) + top - positive) * valid
-    return (jnp.sum(losses), losses)
+def layer_kernel(
+    lengths,
+    rows_ref,
+    pos_ref,
+    w_in,
+    w_out,
+    loss_ref,
+    box_ref,
+    grad_ref,
+    flat,
+    held,
+    where,
+    x32,
+    n32,
+    nb,
+    scale1,
+    negatives,
+    mixed,
+    slope,
+    weights,
+    bend,
+    attended,
+    gated,
+    d_out,
+    d_next,
+    d_att,
+    d_score,
+    d_pre,
+    grads,
+):
+    for s in range(8):
+        block = rows_ref[s * 16 : (s + 1) * 16].astype(F32)
+        flat[s * 16 * MSG : (s + 1) * 16 * MSG, :] = block.reshape(16 * MSG, 128)
+    for c in range(CAP):
+        for b in range(4):
+            piece = flat[pl.ds(4 * c + b, DEV, stride=MSG), :]
+            held[c * 128 : (c + 1) * 128, b * 128 : (b + 1) * 128] = piece.astype(BF16)
+    where[...] = jnp.transpose(jnp.broadcast_to(pos_ref[...], (128, ALL)))
+
+    def take(i):
+        at = where[i * 128 : (i + 1) * 128, :]
+        chosen = [
+            (iota((128, 128), 1) + c * 128 == at).astype(F32).astype(BF16) for c in range(CAP)
+        ]
+        return nn(jnp.concatenate(chosen, 1), held[...])
+
+    for i in range(4):
+        x = take(i)
+        span = pl.ds(i * 128, 128)
+        x32[span, :] = x
+        center = x - jnp.mean(x, -1, keepdims=True)
+        scale = lax.rsqrt(jnp.mean(center * center, -1, keepdims=True) + EPS)
+        normed = center * scale
+        n32[span, :] = normed
+        nb[span, :] = normed.astype(BF16)
+        scale1[span, :] = scale
+    x = take(4)
+    x32[pl.ds(512, 128), :] = x
+    negatives[...] = x.astype(BF16)
+
+    def project(cb, carry):
+        cols = pl.ds(pl.multiple_of(cb * 256, 256), 256)
+        pre = nn(nb[...], w_in[:, cols])
+        sig = jax.nn.sigmoid(pre)
+        mixed[:, cols] = (pre * sig).astype(BF16)
+        slope[:, cols] = (sig * (1.0 + pre * (1.0 - sig))).astype(BF16)
+        return carry
+
+    lax.fori_loop(0, 8, project, 0)
+
+    end1 = lengths[0, 0]
+    end2 = end1 + lengths[0, 1]
+    end3 = end2 + lengths[0, 2]
+
+    def lanes(part, h):
+        return pl.ds(pl.multiple_of(part * 512 + h * 128, 128), 128)
+
+    def visible(i):
+        row = iota((256, 256 * (i + 1)), 0) + 256 * i
+        col = iota((256, 256 * (i + 1)), 1)
+        start = jnp.where(
+            row >= end3, end3, jnp.where(row >= end2, end2, jnp.where(row >= end1, end1, 0))
+        )
+        return jnp.where((col <= row) & (col >= start), 1.0 / LMAX, 0.0).astype(F32)
+
+    def attend(h, carry):
+        for i in range(2):
+            span, past = pl.ds(256 * i, 256), pl.ds(0, 256 * (i + 1))
+            score = nt(mixed[span, lanes(2, h)], mixed[past, lanes(3, h)])
+            sig = jax.nn.sigmoid(score)
+            seen = visible(i)
+            weight = (score * sig * seen).astype(BF16)
+            weights[h, span, past] = weight
+            bend[h, span, past] = (sig * (1.0 + score * (1.0 - sig)) * seen).astype(BF16)
+            attended[span, lanes(0, h)] = nn(weight, mixed[past, lanes(1, h)])
+        return carry
+
+    lax.fori_loop(0, H, attend, 0)
+
+    d_next[pl.ds(0, 8), :] = jnp.zeros((8, D), F32)
+    d_negatives = jnp.zeros((NEG, D), F32)
+    for i in range(2):
+        span = pl.ds(256 * i, 256)
+        values = attended[span, :]
+        center = values - jnp.mean(values, -1, keepdims=True)
+        scale = lax.rsqrt(jnp.mean(center * center, -1, keepdims=True) + EPS)
+        normed = center * scale
+        gate = mixed[span, 0:512].astype(F32)
+        gated_b = (normed * gate).astype(BF16)
+        gated[span, :] = gated_b
+        out_b = (x32[span, :] + nn(gated_b, w_out[...])).astype(BF16)
+        out = out_b.astype(F32)
+        following = x32[pl.ds(256 * i + 1, 256), :]
+        positive = jnp.sum(out * following, -1, keepdims=True) * TAU
+        negative = nt(out_b, negatives[...]) * TAU
+        top = jnp.maximum(positive, jnp.max(negative, -1, keepdims=True))
+        exp_p = jnp.exp(positive - top)
+        exp_n = jnp.exp(negative - top)
+        total = exp_p + jnp.sum(exp_n, -1, keepdims=True)
+        row = iota((256, 1), 0) + (256 * i + 1)
+        valid = (row != end1) & (row != end2) & (row != end3) & (row != TOK)
+        valid = jnp.where(valid, 1.0, 0.0).astype(F32)
+        loss = (jnp.log(total) + top - positive) * valid
+        loss_ref[:, span] = jnp.transpose(jnp.broadcast_to(loss, (256, 128)))[:1, :]
+        share = valid / total
+        d_pos = (exp_p * share - valid) * TAU
+        d_neg = (exp_n * (share * TAU)).astype(BF16)
+        d_out_b = (d_pos * following + nn(d_neg, negatives[...])).astype(BF16)
+        d_out[span, :] = d_out_b
+        d_next[pl.ds(256 * i + 8, 256), :] = d_pos * out
+        d_negatives += tn(d_neg, out_b)
+        d_gated = nt(d_out_b, w_out[...])
+        d_pre[span, 0:512] = (d_gated * normed * slope[span, 0:512].astype(F32)).astype(BF16)
+        d_normed = d_gated * gate
+        d_values = scale * (
+            d_normed
+            - jnp.mean(d_normed, -1, keepdims=True)
+            - normed * jnp.mean(d_normed * normed, -1, keepdims=True)
+        )
+        d_att[span, :] = d_values.astype(BF16)
+    grads[pl.ds(TOK, NEG), :] = d_negatives.astype(BF16)
+
+    def back(h, carry):
+        for i in range(2):
+            span, past = pl.ds(256 * i, 256), pl.ds(0, 256 * (i + 1))
+            d_weight = nt(d_att[span, lanes(0, h)], mixed[past, lanes(1, h)])
+            d_s = (d_weight * bend[h, span, past].astype(F32)).astype(BF16)
+            d_score[span, past] = d_s
+            d_q = nn(d_s, mixed[past, lanes(3, h)])
+            d_pre[span, lanes(2, h)] = (d_q * slope[span, lanes(2, h)].astype(F32)).astype(BF16)
+        for i in range(2):
+            span, future = pl.ds(256 * i, 256), pl.ds(256 * i, 512 - 256 * i)
+            d_v = tn(weights[h, future, span], d_att[future, lanes(0, h)])
+            d_pre[span, lanes(1, h)] = (d_v * slope[span, lanes(1, h)].astype(F32)).astype(BF16)
+            d_k = tn(d_score[future, span], mixed[future, lanes(2, h)])
+            d_pre[span, lanes(3, h)] = (d_k * slope[span, lanes(3, h)].astype(F32)).astype(BF16)
+        return carry
+
+    lax.fori_loop(0, H, back, 0)
+
+    for i in range(2):
+        span = pl.ds(256 * i, 256)
+        d_normed = nt(d_pre[span, :], w_in[...])
+        normed = n32[span, :]
+        d_x = scale1[span, :] * (
+            d_normed
+            - jnp.mean(d_normed, -1, keepdims=True)
+            - normed * jnp.mean(d_normed * normed, -1, keepdims=True)
+        )
+        d_x += d_out[span, :].astype(F32) + d_next[pl.ds(256 * i + 7, 256), :]
+        grads[span, :] = d_x.astype(BF16)
+
+    for j in range(CAP // 2):
+        at = iota((256, ALL), 0) + j * 256
+        sent = nn((at == pos_ref[...]).astype(F32).astype(BF16), grads[...])
+        for c in range(2):
+            for b in range(4):
+                flat[pl.ds(4 * (2 * j + c) + b, DEV, stride=MSG), :] = sent[
+                    c * 128 : (c + 1) * 128, b * 128 : (b + 1) * 128
+                ]
+    for s in range(8):
+        block = flat[s * 16 * MSG : (s + 1) * 16 * MSG, :].astype(BF16)
+        box_ref[s * 16 : (s + 1) * 16] = block.reshape(16, MSG, 128)
+
+    def weigh(cb, carry):
+        cols = pl.ds(pl.multiple_of(cb * 256, 256), 256)
+        grad_ref[:, cols] = tn(nb[...], d_pre[:, cols]).astype(BF16)
+        return carry
+
+    lax.fori_loop(0, 8, weigh, 0)
+    for cb in range(2):
+        cols = pl.ds(cb * 256, 256)
+        grad_ref[:, pl.ds(2048 + cb * 256, 256)] = tn(gated[...], d_out[:, cols]).astype(BF16)
 
 
 def layer(rows, pos, w_in, w_out, lengths):
-    flat = rows[:, : 4 * CAP].reshape(DEV, CAP, D)
-    owner, rank = pos[0] % DEV, pos[0] // DEV
-    rows32 = flat[owner, rank].astype(F32)
-    fn = lambda r, a, b: layer_loss(r, a, b, lengths)
-    total, pull, losses = jax.vjp(fn, rows32, w_in.astype(F32), w_out.astype(F32), has_aux=True)
-    grad_rows, grad_a, grad_b = pull(jnp.float32(1.0))
-    chosen = (jnp.arange(CAP * DEV)[:, None] == pos).astype(BF16)
-    sent = jnp.dot(chosen, grad_rows.astype(BF16), preferred_element_type=F32).astype(BF16)
-    sent = sent.reshape(CAP, DEV, 4, 128).transpose(1, 0, 2, 3).reshape(DEV, 4 * CAP, 128)
-    box = jnp.pad(sent, ((0, 0), (0, MSG - 4 * CAP), (0, 0)))
-    grad = jnp.concatenate([grad_a, grad_b], 1).astype(BF16)
-    return losses, box, grad
+    losses, box, grad = pl.pallas_call(
+        layer_kernel,
+        out_shape=(
+            jax.ShapeDtypeStruct((1, TOK), F32),
+            jax.ShapeDtypeStruct((DEV, MSG, 128), BF16),
+            jax.ShapeDtypeStruct((D, WIDE), BF16),
+        ),
+        in_specs=[pl.BlockSpec(memory_space=pltpu.SMEM), VMEM, VMEM, VMEM, VMEM],
+        out_specs=(VMEM, VMEM, VMEM),
+        scratch_shapes=[
+            pltpu.VMEM((DEV * MSG, 128), F32),
+            pltpu.VMEM((CAP * DEV, D), BF16),
+            pltpu.VMEM((ALL, 128), jnp.int32),
+            pltpu.VMEM((ALL, D), F32),
+            pltpu.VMEM((TOK, D), F32),
+            pltpu.VMEM((TOK, D), BF16),
+            pltpu.VMEM((TOK, 1), F32),
+            pltpu.VMEM((NEG, D), BF16),
+            pltpu.VMEM((TOK, 4 * D), BF16),
+            pltpu.VMEM((TOK, 4 * D), BF16),
+            pltpu.VMEM((H, TOK, TOK), BF16),
+            pltpu.VMEM((H, TOK, TOK), BF16),
+            pltpu.VMEM((TOK, D), F32),
+            pltpu.VMEM((TOK, D), BF16),
+            pltpu.VMEM((TOK, D), BF16),
+            pltpu.VMEM((TOK + 8, D), F32),
+            pltpu.VMEM((TOK, D), BF16),
+            pltpu.VMEM((TOK, TOK), BF16),
+            pltpu.VMEM((TOK, 4 * D), BF16),
+            pltpu.VMEM((ALL, D), BF16),
+        ],
+        compiler_params=pltpu.CompilerParams(vmem_limit_bytes=56 << 20),
+        name="layer",
+    )(lengths, rows, pos, w_in, w_out)
+    return losses.reshape(TOK), box, grad
 
 
 def on_device(
@@ -540,7 +714,7 @@
 ):
     update = last_update.reshape(ROWS // 128, 128)
     rows, ids, pos = fetch(item_owner, neg_owner, item_slot, neg_slot, table, update)
-    losses, box, grad = layer(rows, pos, w_in, w_out, seq_lengths[0])
+    losses, box, grad = layer(rows, pos, w_in, w_out, seq_lengths)
     arrived, total = reduce(box, grad)
     table_grad = scatter(arrived, ids, update)
     grad_in = total[:, : 4 * D].astype(F32)

time: 189 us -> 135 us (0.71)
  matrix products: 31.9 us -> 0 us
  local copies, waits for them, and re-layouts: 38.2 us -> 6.51 us
  Pallas kernels: 100 us -> 124 us
  other arithmetic: 17.2 us -> 3.66 us
    dot_general x16 -> x0, matrix products: 31.9 us -> none  [the longest x3 9.48 us: layer_loss(): jnp.einsum('qhd,khd->hqk', query, key_part, preferred_element_type=jnp.fl...]
    pallas_call x0 -> x1, Pallas kernels: none -> 24.1 us  [layer(): pl.pallas_call(layer_kernel, out_shape=(jax.ShapeDtypeStruct((1, TOK), F3...]
    reshape x9 -> x0, local copies, waits for them, and re-layouts: 17.6 us -> none  [the longest x2 4.11 us: layer_loss(): query = query.reshape(TOK, H, DH)]
    gather x2 -> x0, local copies, waits for them, and re-layouts: 9.55 us -> none  [layer(): rows32 = flat[owner, rank].astype(F32)]
    add_any x2 -> x0, other arithmetic: 5.1 us -> none  [the longest x1 3.61 us: layer_loss(): jax.nn.silu(jnp.dot(normed, w_in32.astype(jnp.bfloat16), preferred_elemen...]
    convert_element_type x4 -> x0, other arithmetic: 3.16 us -> none  [the longest x1 1.7 us: layer_loss(): (normalize(attended) * gate_part.astype(jnp.float32)).astype(jnp.bfloat16)]
    slice x3 -> x0, local copies, waits for them, and re-layouts: 2.28 us -> none  [the longest x2 2 us: layer(): flat = rows[:, :4 * CAP].reshape(DEV, CAP, D)]
    reduce_sum x7 -> x0, other arithmetic: 2.22 us -> none  [the longest x3 1.73 us: normalize(): center = values - jnp.mean(values, -1, keepdims=True)]
where the time goes in v2:
time: 135 us
  Pallas kernels  124 us (92%)
  local copies, waits for them, and re-layouts  6.51 us (5%)
  other arithmetic  3.66 us (3%)
    pallas_call x1, Pallas kernels, reduce(): pl.pallas_call(reduce_kernel, out_shape=(jax.ShapeDtypeStruct((DEV, MSG,...  50.8 us
    pallas_call x1, Pallas kernels, fetch(): pl.pallas_call(fetch_kernel, out_shape=(jax.ShapeDtypeStruct((DEV, MSG, 1...  40.2 us
    pallas_call x1, Pallas kernels, layer(): pl.pallas_call(layer_kernel, out_shape=(jax.ShapeDtypeStruct((1, TOK), F3...  24.1 us
    pallas_call x1, Pallas kernels, scatter(): pl.pallas_call(scatter_kernel, grid=(4,), out_shape=jax.ShapeDtypeStruct(...  8.81 us
    unnamed x18, local copies, waits for them, and re-layouts  6.51 us

profile of v2, /device:TPU:1, one launch (start us, length us, event | category | flops | bytes accessed | tf_op | source)
XLA Modules:
  0.0 134.7 jit_solution(17652760286442415768)
XLA Ops:
  0.6 0.0 copy-start.2
  0.6 0.7 copy-done.2
  1.4 0.0 copy-start.5
  1.4 0.7 copy-done.5
  2.0 0.0 copy-start.6
  2.0 0.7 copy-done.6
  2.7 0.0 copy-start.7
  2.7 0.7 copy-done.7
  3.4 0.0 copy-start.8
  3.4 0.7 copy-done.8
  4.0 40.2 %fetch.1 = (bf16[128,48,128]{2,1,0:T(8,128)(2,1)S(1)}, s32[128,128]{1,0:T(8,128)S(1)}, s32[1,640]{1,0:T(1,128)S(1)}) custom-call(s32[1,512]{1,0:T(1,128)S(1)} %bitcast.8, s32[1,128]{1,0:T(1,128)S(1)} %bitcast.10, s32[1,512]{1,0:T(1,128)S(1)} %bitcast.9, s32[1,128]{1,0:T(1,128)S(1)} %bitcast.11, bf16[4096,512]{1,0:T(8,128)(2,1)} %table_ref.1, ...), custom_call_target="tpu_custom_call" | custom-call | tf_op jit(solution)/shard_map/fetch/pallas_call | solution.py:213
  44.2 0.0 copy-start
  44.2 1.1 copy-done
  45.4 0.0 copy-start.4
  45.4 0.6 copy-done.4
  46.0 24.1 %layer.1 = (f32[1,512]{1,0:T(1,128)}, bf16[128,48,128]{2,1,0:T(8,128)(2,1)}, bf16[512,2560]{1,0:T(8,128)(2,1)}) custom-call(s32[1,4]{1,0:T(1,128)} %lengths.1, bf16[128,48,128]{2,1,0:T(8,128)(2,1)} %copy-done, s32[1,640]{1,0:T(1,128)} %copy-done.4, bf16[512,2048]{1,0:T(8,128)(2,1)} %w_in.1, bf16[512,512]{1,0:T(8,128)(2,1)} %w_out.1), custom_call_target="tpu_custom_call" | custom-call | tf_op jit(solution)/shard_map/layer/pallas_call | solution.py:675
  70.0 0.0 copy-start.1
  70.0 1.4 %copy-done.1 = bf16[128,48,128]{2,1,0:T(8,128)(2,1)S(1)} copy-done((bf16[128,48,128]{2,1,0:T(8,128)(2,1)S(1)}, bf16[128,48,128]{2,1,0:T(8,128)(2,1)}, u32[]{:S(2)}) %copy-start.1) | copy-done | bytes 1572888
  71.4 50.8 %reduce.1 = (bf16[128,48,128]{2,1,0:T(8,128)(2,1)S(1)}, bf16[512,2560]{1,0:T(8,128)(2,1)S(1)}) custom-call(bf16[128,48,128]{2,1,0:T(8,128)(2,1)S(1)} %copy-done.1, bf16[512,2560]{1,0:T(8,128)(2,1)} %get-tuple-element.16.grad_ref), custom_call_target="tpu_custom_call" | custom-call | tf_op jit(solution)/shard_map/reduce/pallas_call | solution.py:402
  122.2 1.1 slice_convert_fusion.1
  123.3 0.0 copy-start.3
  123.3 2.6 %slice_convert_fusion = f32[512,2048]{1,0:T(8,128)} fusion(bf16[512,2560]{1,0:T(8,128)(2,1)S(1)} %get-tuple-element.19), kind=kLoop, calls=%fused_computation | loop fusion | flops 1048576 | bytes 6291456 | tf_op jit(solution)/shard_map/convert_element_type | solution.py:720
  125.9 0.0 copy-done.3
  125.9 8.8 %scatter.1 = f32[4096,512]{1,0:T(8,128)} custom-call(bf16[128,48,128]{2,1,0:T(8,128)(2,1)S(1)} %get-tuple-element.17.arrived_ref, s32[128,128]{1,0:T(8,128)S(1)} %get-tuple-element.18.ids_ref, s32[32,128]{1,0:T(8,128)S(1)} %bitcast.7), custom_call_target="tpu_custom_call" | custom-call | tf_op jit(solution)/shard_map/scatter/pallas_call | solution.py:459
Async XLA Ops:
  0.6 0.7 copy-start.2
  1.4 0.7 copy-start.5
  2.0 0.7 copy-start.6
  2.7 0.7 copy-start.7
  3.4 0.7 copy-start.8
  44.2 1.1 copy-start
  45.4 0.6 copy-start.4
  70.0 1.4 %copy-start.1 = (bf16[128,48,128]{2,1,0:T(8,128)(2,1)S(1)}, bf16[128,48,128]{2,1,0:T(8,128)(2,1)}, u32[]{:S(2)}) copy-start(bf16[128,48,128]{2,1,0:T(8,128)(2,1)} %get-tuple-element.15.box_ref) | copy-start | bytes 4718596
  123.3 2.6 %copy-start.3 = (s32[4096]{0:T(1024)S(1)}, s32[4096]{0:T(1024)}, u32[]{:S(2)}) copy-start(s32[4096]{0:T(1024)} %param.10) | copy-start | bytes 49156

commit v3 on v2

--- a/solution.py
+++ b/solution.py
@@ -28,7 +28,6 @@
 ANY = pl.BlockSpec(memory_space=pl.ANY)
 F32 = jnp.float32
 BF16 = jnp.bfloat16
-PARTS = ((0, 896), (896, 896), (1792, 768))
 
 
 def nt(a, b):
@@ -99,15 +98,21 @@
 
 
 def fetch_kernel(
-    item_owner,
-    neg_owner,
-    item_slot,
-    neg_slot,
+    item_owner_ref,
+    neg_owner_ref,
+    item_slot_ref,
+    neg_slot_ref,
     table_ref,
     update_ref,
     rows_ref,
     ids_ref,
     pos_ref,
+    item_owner,
+    neg_owner,
+    item_slot,
+    neg_slot,
+    update,
+    small_sem,
     table_vmem,
     faded,
     asked,
@@ -120,9 +125,23 @@
     row_recv,
 ):
     place = Place()
+    pairs = (
+        (item_owner_ref, item_owner),
+        (neg_owner_ref, neg_owner),
+        (item_slot_ref, item_slot),
+        (neg_slot_ref, neg_slot),
+        (update_ref, update),
+    )
+    loads = [
+        pltpu.make_async_copy(src, dst, small_sem.at[n]) for n, (src, dst) in enumerate(pairs)
+    ]
+    for copy in loads:
+        copy.start()
     load = pltpu.make_async_copy(table_ref, table_vmem, local_sem)
     load.start()
     barrier = announce(place)
+    for copy in loads:
+        copy.wait()
     owner = jnp.concatenate([item_owner[...], neg_owner[...]], 1)
     slot = jnp.concatenate([item_slot[...], neg_slot[...]], 1)
     onehot = (iota((DEV, ALL), 0) == owner).astype(F32)
@@ -157,7 +176,7 @@
 
     lax.fori_loop(0, 4, ask, 0)
     ids_ref[pl.ds(place.me, 1), :] = asked[pl.ds(place.me, 1), :]
-    fade = jnp.exp((NOW - update_ref[...]).astype(F32) * LOG_RHO)
+    fade = jnp.exp((NOW - update[...]).astype(F32) * LOG_RHO)
     fade = jnp.transpose(jnp.concatenate([fade, jnp.zeros((96, 128), F32)], 0))
     load.wait()
     for c in range(32):
@@ -217,9 +236,15 @@
             jax.ShapeDtypeStruct((DEV, 128), jnp.int32),
             jax.ShapeDtypeStruct((1, ALL), jnp.int32),
         ),
-        in_specs=[VMEM, VMEM, VMEM, VMEM, ANY, VMEM],
+        in_specs=[ANY] * 6,
         out_specs=(VMEM, VMEM, VMEM),
         scratch_shapes=[
+            pltpu.VMEM((1, TOK), jnp.int32),
+            pltpu.VMEM((1, NEG), jnp.int32),
+            pltpu.VMEM((1, TOK), jnp.int32),
+            pltpu.VMEM((1, NEG), jnp.int32),
+            pltpu.VMEM((ROWS // 128, 128), jnp.int32),
+            pltpu.SemaphoreType.DMA((5,)),
             pltpu.VMEM((ROWS, D), BF16),
             pltpu.VMEM((ROWS, D), BF16),
             pltpu.VMEM((DEV, 128), jnp.int32),
@@ -245,192 +270,21 @@
     )
 
 
-def reduce_kernel(
-    box_ref,
-    grad_ref,
+def scatter_kernel(
     arrived_ref,
+    ids_ref,
+    update_ref,
     total_ref,
-    half,
-    acc0,
-    acc1,
-    acc2,
-    in1,
-    in2,
-    in3,
-    row_send,
-    row_recv,
-    core_send,
-    core_recv,
-    step_send,
-    step_recv,
+    out_ref,
+    grad_in_ref,
+    grad_out_ref,
+    wide,
+    rows,
+    slots,
 ):
-    place = Place()
-    barrier = announce(place)
-    arrived_ref[place.me] = box_ref[place.me]
-    pl.semaphore_wait(barrier, DEV - 1)
-    mine = pl.multiple_of(place.core * 256, 256)
-    other = pl.multiple_of((1 - place.core) * 256, 256)
-    swap = pltpu.make_async_remote_copy(
-        src_ref=grad_ref.at[pl.ds(other, 256)],
-        dst_ref=half,
-        send_sem=core_send.at[0],
-        recv_sem=core_recv.at[0],
-        device_id=place.sibling(),
-        device_id_type=MESH,
-    )
-    swap.start()
-
-    def post(c):
-        for k, (d, t) in enumerate(peers(place, c)):
-            if c == 0 and k == 0:
-                continue
-            pltpu.make_async_remote_copy(
-                src_ref=box_ref.at[d * 16 + t],
-                dst_ref=arrived_ref.at[place.me],
-                send_sem=row_send,
-                recv_sem=row_recv,
-                device_id=(d, t),
-                device_id_type=MESH,
-            ).start()
-
-    coordinate = {"x": place.x, "y": place.y, "z": place.z}
-    axes = (("x", "y", "z"), ("y", "z", "x"), ("z", "x", "y"))
-
-    def send(p, step, shift, src, dst):
-        copy = pltpu.make_async_remote_copy(
-            src_ref=src,
-            dst_ref=dst,
-            send_sem=step_send.at[p, step, shift - 1],
-            recv_sem=step_recv.at[p, step, shift - 1],
-            device_id=place.along(axes[p][(0, 1, 2, 1, 0)[step]], shift),
-            device_id_type=MESH,
-        )
-        copy.start()
-        return copy
-
-    post(0)
-    swap.wait()
-    acc0[...] = (grad_ref[pl.ds(mine, 256), :].astype(F32) + half[...].astype(F32)).astype(BF16)
-    first = []
-    for p, (start, width) in enumerate(PARTS):
-        at = coordinate[axes[p][0]]
-        cols = pl.ds(start, width)
-        for shift in (1, 2, 3):
-            to = pl.multiple_of(lax.rem(at + shift, 4) * 64, 64)
-            first.append(
-                send(p, 0, shift, acc0.at[pl.ds(to, 64), cols], in1.at[shift - 1, :, cols])
-            )
-    post(1)
-    second = []
-    for p, (start, width) in enumerate(PARTS):
-        at = coordinate[axes[p][0]]
-        cols = pl.ds(start, width)
-        for copy in first[3 * p : 3 * p + 3]:
-            copy.wait()
-        total = acc0[pl.ds(pl.multiple_of(at * 64, 64), 64), cols].astype(F32)
-        for k in range(3):
-            total += in1[k, :, cols].astype(F32)
-        acc1[:, cols] = total.astype(BF16)
-        at = coordinate[axes[p][1]]
-        for shift in (1, 2, 3):
-            to = pl.multiple_of(lax.rem(at + shift, 4) * 16, 16)
-            second.append(
-                send(p, 1, shift, acc1.at[pl.ds(to, 16), cols], in2.at[shift - 1, :, cols])
-            )
-    post(2)
-    third = []
-    for p, (start, width) in enumerate(PARTS):
-        at = coordinate[axes[p][1]]
-        cols = pl.ds(start, width)
-        for copy in second[3 * p : 3 * p + 3]:
-            copy.wait()
-        total = acc1[pl.ds(pl.multiple_of(at * 16, 16), 16), cols].astype(F32)
-        for k in range(3):
-            total += in2[k, :, cols].astype(F32)
-        acc2[:, cols] = total.astype(BF16)
-        at = coordinate[axes[p][2]]
-        in3[at, :, cols] = acc2[:, cols]
-        for shift in (1, 2, 3):
-            third.append(send(p, 2, shift, acc2.at[:, cols], in3.at[at, :, cols]))
-    post(3)
-    fourth = []
-    places = []
-    for p, (start, width) in enumerate(PARTS):
-        cols = pl.ds(start, width)
-        for copy in third[3 * p : 3 * p + 3]:
-            copy.wait()
-        total = in3[0, :, cols].astype(F32)
-        for k in range(1, 4):
-            total += in3[k, :, cols].astype(F32)
-        wide = pl.multiple_of(mine + coordinate[axes[p][0]] * 64, 64)
-        narrow = pl.multiple_of(wide + coordinate[axes[p][1]] * 16, 16)
-        places.append(wide)
-        total_ref[pl.ds(narrow, 16), cols] = total.astype(BF16)
-        piece = total_ref.at[pl.ds(narrow, 16), cols]
-        for shift in (1, 2, 3):
-            fourth.append(send(p, 3, shift, piece, piece))
-    fifth = []
-    for p, (start, width) in enumerate(PARTS):
-        for copy in fourth[3 * p : 3 * p + 3]:
-            copy.wait()
-        piece = total_ref.at[pl.ds(places[p], 64), pl.ds(start, width)]
-        for shift in (1, 2, 3):
-            fifth.append(send(p, 4, shift, piece, piece))
-    last = []
-    for p, (start, width) in enumerate(PARTS):
-        for copy in fifth[3 * p : 3 * p + 3]:
-            copy.wait()
-        piece = total_ref.at[pl.ds(mine, 256), pl.ds(start, width)]
-        copy = pltpu.make_async_remote_copy(
-            src_ref=piece,
-            dst_ref=piece,
-            send_sem=core_send.at[p + 1],
-            recv_sem=core_recv.at[p + 1],
-            device_id=place.sibling(),
-            device_id_type=MESH,
-        )
-        copy.start()
-        last.append(copy)
-    for copy in last:
-        copy.wait()
-    most = box_ref.at[pl.ds(0, DEV - 1)]
-    pltpu.make_async_copy(most, most, row_send).wait()
-    pltpu.make_async_copy(most, most, row_recv).wait()
-
-
-def reduce(box, grad):
-    return pl.pallas_call(
-        reduce_kernel,
-        out_shape=(
-            jax.ShapeDtypeStruct((DEV, MSG, 128), BF16),
-            jax.ShapeDtypeStruct((D, WIDE), BF16),
-        ),
-        in_specs=[VMEM, VMEM],
-        out_specs=(VMEM, VMEM),
-        scratch_shapes=[
-            pltpu.VMEM((256, WIDE), BF16),
-            pltpu.VMEM((256, WIDE), BF16),
-            pltpu.VMEM((64, WIDE), BF16),
-            pltpu.VMEM((16, WIDE), BF16),
-            pltpu.VMEM((3, 64, WIDE), BF16),
-            pltpu.VMEM((3, 16, WIDE), BF16),
-            pltpu.VMEM((4, 16, WIDE), BF16),
-            pltpu.SemaphoreType.DMA,
-            pltpu.SemaphoreType.DMA,
-            pltpu.SemaphoreType.DMA((4,)),
-            pltpu.SemaphoreType.DMA((4,)),
-            pltpu.SemaphoreType.DMA((3, 5, 3)),
-            pltpu.SemaphoreType.DMA((3, 5, 3)),
-        ],
-        compiler_params=pltpu.CompilerParams(
-            collective_id=1, has_side_effects=True, vmem_limit_bytes=48 << 20
-        ),
-        name="reduce",
-    )(box, grad)
-
-
-def scatter_kernel(arrived_ref, ids_ref, update_ref, out_ref, wide, rows, slots):
     step = pl.program_id(0)
+    grad_out_ref[...] = total_ref[:, :D].astype(F32)
+    grad_in_ref[...] = total_ref[:, D:].astype(F32)
 
     @pl.when(step == 0)
     def _():
@@ -455,17 +309,26 @@
         out_ref[s * 128 : (s + 1) * 128, :] = summed * fade[:, s : s + 1]
 
 
-def scatter(arrived, ids, update):
+def scatter(arrived, ids, update, total):
     return pl.pallas_call(
         scatter_kernel,
         grid=(4,),
-        out_shape=jax.ShapeDtypeStruct((ROWS, D), F32),
+        out_shape=(
+            jax.ShapeDtypeStruct((ROWS, D), F32),
+            jax.ShapeDtypeStruct((D, 4 * D), F32),
+            jax.ShapeDtypeStruct((D, D), F32),
+        ),
         in_specs=[
             pl.BlockSpec((DEV, MSG, 128), lambda i: (0, 0, 0)),
             pl.BlockSpec((DEV, 128), lambda i: (0, 0)),
             pl.BlockSpec((8, 128), lambda i: (i, 0)),
+            pl.BlockSpec((128, WIDE), lambda i: (i, 0)),
         ],
-        out_specs=pl.BlockSpec((1024, D), lambda i: (i, 0)),
+        out_specs=(
+            pl.BlockSpec((1024, D), lambda i: (i, 0)),
+            pl.BlockSpec((128, 4 * D), lambda i: (i, 0)),
+            pl.BlockSpec((128, D), lambda i: (i, 0)),
+        ),
         scratch_shapes=[
             pltpu.VMEM((DEV * MSG, 128), F32),
             pltpu.VMEM((CAP * 128, D), BF16),
@@ -473,18 +336,150 @@
         ],
         compiler_params=pltpu.CompilerParams(vmem_limit_bytes=48 << 20),
         name="scatter",
-    )(arrived, ids, update)
+    )(arrived, ids, update, total)
+
+
+class Wave:
+    AXES = (("x", "y", "z"), ("y", "z", "x"), ("z", "x", "y"))
+
+    def __init__(self, place, number, parts, refs):
+        self.place, self.number, self.parts = place, number, parts
+        (self.grad, self.total, self.half, self.acc0, self.acc1, self.acc2) = refs[:6]
+        (self.in1, self.in2, self.in3) = refs[6:9]
+        (self.core_send, self.core_recv, self.step_send, self.step_recv) = refs[9:]
+        self.mine = pl.multiple_of(place.core * 256, 256)
+        self.other = pl.multiple_of((1 - place.core) * 256, 256)
+        self.at = {"x": place.x, "y": place.y, "z": place.z}
+        self.first, self.second, self.third, self.fourth, self.fifth = [], [], [], [], []
+
+    def across(self, slot, src, dst):
+        copy = pltpu.make_async_remote_copy(
+            src_ref=src,
+            dst_ref=dst,
+            send_sem=self.core_send.at[self.number, slot],
+            recv_sem=self.core_recv.at[self.number, slot],
+            device_id=self.place.sibling(),
+            device_id_type=MESH,
+        )
+        copy.start()
+        return copy
+
+    def send(self, p, step, shift, src, dst):
+        copy = pltpu.make_async_remote_copy(
+            src_ref=src,
+            dst_ref=dst,
+            send_sem=self.step_send.at[self.number, p, step, shift - 1],
+            recv_sem=self.step_recv.at[self.number, p, step, shift - 1],
+            device_id=self.place.along(self.AXES[p][(0, 1, 2, 1, 0)[step]], shift),
+            device_id_type=MESH,
+        )
+        copy.start()
+        return copy
+
+    def coordinate(self, p, level):
+        return self.at[self.AXES[p][level]]
+
+    def swap(self):
+        self.swaps = []
+        for p, (start, width) in enumerate(self.parts):
+            cols = pl.ds(start, width)
+            self.swaps.append(
+                self.across(p, self.grad.at[pl.ds(self.other, 256), cols], self.half.at[:, cols])
+            )
+
+    def scatter1(self):
+        for p, (start, width) in enumerate(self.parts):
+            cols = pl.ds(start, width)
+            self.swaps[p].wait()
+            self.acc0[:, cols] = (
+                self.grad[pl.ds(self.mine, 256), cols].astype(F32)
+                + self.half[:, cols].astype(F32)
+            ).astype(BF16)
+            for shift in (1, 2, 3):
+                to = pl.multiple_of(lax.rem(self.coordinate(p, 0) + shift, 4) * 64, 64)
+                src = self.acc0.at[pl.ds(to, 64), cols]
+                self.first.append(self.send(p, 0, shift, src, self.in1.at[shift - 1, :, cols]))
+
+    def scatter2(self):
+        for p, (start, width) in enumerate(self.parts):
+            cols = pl.ds(start, width)
+            for copy in self.first[3 * p : 3 * p + 3]:
+                copy.wait()
+            own = pl.multiple_of(self.coordinate(p, 0) * 64, 64)
+            total = self.acc0[pl.ds(own, 64), cols].astype(F32)
+            for k in range(3):
+                total += self.in1[k, :, cols].astype(F32)
+            self.acc1[:, cols] = total.astype(BF16)
+            for shift in (1, 2, 3):
+                to = pl.multiple_of(lax.rem(self.coordinate(p, 1) + shift, 4) * 16, 16)
+                src = self.acc1.at[pl.ds(to, 16), cols]
+                self.second.append(self.send(p, 1, shift, src, self.in2.at[shift - 1, :, cols]))
+
+    def exchange(self):
+        for p, (start, width) in enumerate(self.parts):
+            cols = pl.ds(start, width)
+            for copy in self.second[3 * p : 3 * p + 3]:
+                copy.wait()
+            own = pl.multiple_of(self.coordinate(p, 1) * 16, 16)
+            total = self.acc1[pl.ds(own, 16), cols].astype(F32)
+            for k in range(3):
+                total += self.in2[k, :, cols].astype(F32)
+            self.acc2[:, cols] = total.astype(BF16)
+            at = self.coordinate(p, 2)
+            self.in3[at, :, cols] = self.acc2[:, cols]
+            for shift in (1, 2, 3):
+                self.third.append(
+                    self.send(p, 2, shift, self.acc2.at[:, cols], self.in3.at[at, :, cols])
+                )
+
+    def gather4(self):
+        for p, (start, width) in enumerate(self.parts):
+            cols = pl.ds(start, width)
+            for copy in self.third[3 * p : 3 * p + 3]:
+                copy.wait()
+            total = self.in3[0, :, cols].astype(F32)
+            for k in range(1, 4):
+                total += self.in3[k, :, cols].astype(F32)
+            wide = pl.multiple_of(self.mine + self.coordinate(p, 0) * 64, 64)
+            narrow = pl.multiple_of(wide + self.coordinate(p, 1) * 16, 16)
+            self.total[pl.ds(narrow, 16), cols] = total.astype(BF16)
+            piece = self.total.at[pl.ds(narrow, 16), cols]
+            for shift in (1, 2, 3):
+                self.fourth.append(self.send(p, 3, shift, piece, piece))
+
+    def gather5(self):
+        for p, (start, width) in enumerate(self.parts):
+            for copy in self.fourth[3 * p : 3 * p + 3]:
+                copy.wait()
+            wide = pl.multiple_of(self.mine + self.coordinate(p, 0) * 64, 64)
+            piece = self.total.at[pl.ds(wide, 64), pl.ds(start, width)]
+            for shift in (1, 2, 3):
+                self.fifth.append(self.send(p, 4, shift, piece, piece))
+
+    def restore(self):
+        self.last = []
+        for p, (start, width) in enumerate(self.parts):
+            for copy in self.fifth[3 * p : 3 * p + 3]:
+                copy.wait()
+            piece = self.total.at[pl.ds(self.mine, 256), pl.ds(start, width)]
+            self.last.append(self.across(3 + p, piece, piece))
+
+    def finish(self):
+        for copy in self.last:
+            copy.wait()
 
 
 def layer_kernel(
     lengths,
     rows_ref,
     pos_ref,
+    w_in_ref,
+    w_out_ref,
+    loss_ref,
+    arrived_ref,
+    total_ref,
     w_in,
     w_out,
-    loss_ref,
-    box_ref,
-    grad_ref,
     flat,
     held,
     where,
@@ -505,7 +500,47 @@
     d_score,
     d_pre,
     grads,
+    box,
+    grad,
+    half,
+    acc0,
+    acc1,
+    acc2,
+    in1,
+    in2,
+    in3,
+    load_sem,
+    row_send,
+    row_recv,
+    core_send,
+    core_recv,
+    step_send,
+    step_recv,
 ):
+    place = Place()
+    load_in = pltpu.make_async_copy(w_in_ref, w_in, load_sem.at[0])
+    load_out = pltpu.make_async_copy(w_out_ref, w_out, load_sem.at[1])
+    load_in.start()
+    load_out.start()
+    barrier = announce(place)
+    refs = (grad, total_ref, half, acc0, acc1, acc2, in1, in2, in3)
+    refs += (core_send, core_recv, step_send, step_recv)
+    wave_a = Wave(place, 0, ((0, 384), (384, 384), (768, 256)), refs)
+    wave_b = Wave(place, 1, ((1024, 512), (1536, 512), (2048, 512)), refs)
+    groups = [peers(place, c) for c in range(4)]
+
+    def post(first, last):
+        for n in range(first, last):
+            d, t = groups[n // 32][n % 32]
+            pltpu.make_async_remote_copy(
+                src_ref=box.at[d * 16 + t],
+                dst_ref=arrived_ref.at[place.me],
+                send_sem=row_send,
+                recv_sem=row_recv,
+                device_id=(d, t),
+                device_id_type=MESH,
+            ).start()
+
     for s in range(8):
         block = rows_ref[s * 16 : (s + 1) * 16].astype(F32)
         flat[s * 16 * MSG : (s + 1) * 16 * MSG, :] = block.reshape(16 * MSG, 128)
@@ -536,6 +571,8 @@
     x32[pl.ds(512, 128), :] = x
     negatives[...] = x.astype(BF16)
 
+    load_in.wait()
+
     def project(cb, carry):
         cols = pl.ds(pl.multiple_of(cb * 256, 256), 256)
         pre = nn(nb[...], w_in[:, cols])
@@ -575,6 +612,7 @@
 
     lax.fori_loop(0, H, attend, 0)
 
+    load_out.wait()
     d_next[pl.ds(0, 8), :] = jnp.zeros((8, D), F32)
     d_negatives = jnp.zeros((NEG, D), F32)
     for i in range(2):
@@ -634,7 +672,24 @@
             d_pre[span, lanes(3, h)] = (d_k * slope[span, lanes(3, h)].astype(F32)).astype(BF16)
         return carry
 
-    lax.fori_loop(0, H, back, 0)
+    for cb in range(2):
+        cols = pl.ds(cb * 256, 256)
+        grad[:, cols] = tn(gated[...], d_out[:, cols]).astype(BF16)
+    for cb in range(2):
+        grad[:, pl.ds(512 + cb * 256, 256)] = tn(nb[...], d_pre[:, pl.ds(cb * 256, 256)]).astype(
+            BF16
+        )
+    pl.semaphore_wait(barrier, DEV - 1)
+    wave_a.swap()
+    lax.fori_loop(0, 2, back, 0)
+    wave_a.scatter1()
+    lax.fori_loop(2, 4, back, 0)
+    for cb in range(2, 8):
+        grad[:, pl.ds(512 + cb * 256, 256)] = tn(nb[...], d_pre[:, pl.ds(cb * 256, 256)]).astype(
+            BF16
+        )
+    wave_b.swap()
+    wave_a.scatter2()
 
     for i in range(2):
         span = pl.ds(256 * i, 256)
@@ -648,6 +703,8 @@
         d_x += d_out[span, :].astype(F32) + d_next[pl.ds(256 * i + 7, 256), :]
         grads[span, :] = d_x.astype(BF16)
 
+    wave_a.exchange()
+
     for j in range(CAP // 2):
         at = iota((256, ALL), 0) + j * 256
         sent = nn((at == pos_ref[...]).astype(F32).astype(BF16), grads[...])
@@ -658,30 +715,43 @@
                 ]
     for s in range(8):
         block = flat[s * 16 * MSG : (s + 1) * 16 * MSG, :].astype(BF16)
-        box_ref[s * 16 : (s + 1) * 16] = block.reshape(16, MSG, 128)
-
-    def weigh(cb, carry):
-        cols = pl.ds(pl.multiple_of(cb * 256, 256), 256)
-        grad_ref[:, cols] = tn(nb[...], d_pre[:, cols]).astype(BF16)
-        return carry
-
-    lax.fori_loop(0, 8, weigh, 0)
-    for cb in range(2):
-        cols = pl.ds(cb * 256, 256)
-        grad_ref[:, pl.ds(2048 + cb * 256, 256)] = tn(gated[...], d_out[:, cols]).astype(BF16)
+        box[s * 16 : (s + 1) * 16] = block.reshape(16, MSG, 128)
+
+    wave_b.scatter1()
+    arrived_ref[place.me] = box[place.me]
+    post(1, 32)
+    wave_a.gather4()
+    post(32, 48)
+    wave_b.scatter2()
+    post(48, 64)
+    wave_a.gather5()
+    post(64, 96)
+    wave_b.exchange()
+    post(96, 128)
+    wave_b.gather4()
+    wave_a.restore()
+    wave_b.gather5()
+    wave_b.restore()
+    wave_a.finish()
+    wave_b.finish()
+    most = box.at[pl.ds(0, DEV - 1)]
+    pltpu.make_async_copy(most, most, row_send).wait()
+    pltpu.make_async_copy(most, most, row_recv).wait()
 
 
 def layer(rows, pos, w_in, w_out, lengths):
-    losses, box, grad = pl.pallas_call(
+    return pl.pallas_call(
         layer_kernel,
         out_shape=(
             jax.ShapeDtypeStruct((1, TOK), F32),
             jax.ShapeDtypeStruct((DEV, MSG, 128), BF16),
             jax.ShapeDtypeStruct((D, WIDE), BF16),
         ),
-        in_specs=[pl.BlockSpec(memory_space=pltpu.SMEM), VMEM, VMEM, VMEM, VMEM],
+        in_specs=[pl.BlockSpec(memory_space=pltpu.SMEM), VMEM, VMEM, ANY, ANY],
         out_specs=(VMEM, VMEM, VMEM),
         scratch_shapes=[
+            pltpu.VMEM((D, 4 * D), BF16),
+            pltpu.VMEM((D, D), BF16),
             pltpu.VMEM((DEV * MSG, 128), F32),
             pltpu.VMEM((CAP * DEV, D), BF16),
             pltpu.VMEM((ALL, 128), jnp.int32),
@@ -702,11 +772,28 @@
             pltpu.VMEM((TOK, TOK), BF16),
             pltpu.VMEM((TOK, 4 * D), BF16),
             pltpu.VMEM((ALL, D), BF16),
+            pltpu.VMEM((DEV, MSG, 128), BF16),
+            pltpu.VMEM((D, WIDE), BF16),
+            pltpu.VMEM((256, WIDE), BF16),
+            pltpu.VMEM((256, WIDE), BF16),
+            pltpu.VMEM((64, WIDE), BF16),
+            pltpu.VMEM((16, WIDE), BF16),
+            pltpu.VMEM((3, 64, WIDE), BF16),
+            pltpu.VMEM((3, 16, WIDE), BF16),
+            pltpu.VMEM((4, 16, WIDE), BF16),
+            pltpu.SemaphoreType.DMA((2,)),
+            pltpu.SemaphoreType.DMA,
+            pltpu.SemaphoreType.DMA,
+            pltpu.SemaphoreType.DMA((2, 6)),
+            pltpu.SemaphoreType.DMA((2, 6)),
+            pltpu.SemaphoreType.DMA((2, 3, 5, 3)),
+            pltpu.SemaphoreType.DMA((2, 3, 5, 3)),
         ],
-        compiler_params=pltpu.CompilerParams(vmem_limit_bytes=56 << 20),
+        compiler_params=pltpu.CompilerParams(
+            collective_id=1, has_side_effects=True, vmem_limit_bytes=58 << 20
+        ),
         name="layer",
     )(lengths, rows, pos, w_in, w_out)
-    return losses.reshape(TOK), box, grad
 
 
 def on_device(
@@ -714,12 +801,9 @@
 ):
     update = last_update.reshape(ROWS // 128, 128)
     rows, ids, pos = fetch(item_owner, neg_owner, item_slot, neg_slot, table, update)
-    losses, box, grad = layer(rows, pos, w_in, w_out, seq_lengths)
-    arrived, total = reduce(box, grad)
-    table_grad = scatter(arrived, ids, update)
-    grad_in = total[:, : 4 * D].astype(F32)
-    grad_out = total[:, 4 * D :].astype(F32)
-    return (losses, table_grad, grad_in, grad_out)
+    losses, arrived, total = layer(rows, pos, w_in, w_out, seq_lengths)
+    table_grad, grad_in, grad_out = scatter(arrived, ids, update, total)
+    return (losses.reshape(TOK), table_grad, grad_in, grad_out)
 
 
 def solution(mesh):

time: 135 us -> 125 us (0.926)
  Pallas kernels: 124 us -> 116 us
  other arithmetic: 3.66 us -> 0 us
  local copies, waits for them, and re-layouts: 6.51 us -> 8.83 us
    pallas_call x2 -> x1, Pallas kernels: 59.6 us -> 9.18 us  [scatter(): pl.pallas_call(scatter_kernel, grid=(4,), out_shape=(jax.ShapeDtypeStruct...]
    pallas_call x1, Pallas kernels: 24.1 us -> 65.8 us  [layer(): pl.pallas_call(layer_kernel, out_shape=(jax.ShapeDtypeStruct((1, TOK), F3...]
    convert_element_type x2 -> x0, other arithmetic: 3.66 us -> none  [the longest x1 2.56 us: on_device(): grad_in = total[:, :4 * D].astype(F32)]
    unnamed x18 -> x23, local copies, waits for them, and re-layouts: 6.51 us -> 8.83 us
where the time goes in v3:
time: 125 us
  Pallas kernels  116 us (93%)
  local copies, waits for them, and re-layouts  8.83 us (7%)
    pallas_call x1, Pallas kernels, layer(): pl.pallas_call(layer_kernel, out_shape=(jax.ShapeDtypeStruct((1, TOK), F3...  65.8 us
    pallas_call x1, Pallas kernels, fetch(): pl.pallas_call(fetch_kernel, out_shape=(jax.ShapeDtypeStruct((DEV, MSG, 1...  40.5 us
    pallas_call x1, Pallas kernels, scatter(): pl.pallas_call(scatter_kernel, grid=(4,), out_shape=(jax.ShapeDtypeStruct...  9.18 us
    unnamed x23, local copies, waits for them, and re-layouts  8.83 us

profile of v3, /device:TPU:1, one launch (start us, length us, event | category | flops | bytes accessed | tf_op | source)
XLA Modules:
  0.0 125.1 jit_solution(3374822016885753109)
XLA Ops:
  0.6 0.0 copy-start.3
  0.6 0.7 copy-done.3
  1.4 0.0 copy-start.6
  1.4 0.7 copy-done.6
  2.0 0.0 copy-start.7
  2.0 0.7 copy-done.7
  2.7 0.0 copy-start.8
  2.7 0.7 copy-done.8
  3.4 0.0 copy-start.9
  3.4 0.7 copy-done.9
  4.0 40.5 %fetch.1 = (bf16[128,48,128]{2,1,0:T(8,128)(2,1)S(1)}, s32[128,128]{1,0:T(8,128)S(1)}, s32[1,640]{1,0:T(1,128)S(1)}) custom-call(s32[1,512]{1,0:T(1,128)S(1)} %bitcast.8, s32[1,128]{1,0:T(1,128)S(1)} %bitcast.10, s32[1,512]{1,0:T(1,128)S(1)} %bitcast.9, s32[1,128]{1,0:T(1,128)S(1)} %bitcast.11, bf16[4096,512]{1,0:T(8,128)(2,1)} %table_ref.1, ...), custom_call_target="tpu_custom_call" | custom-call | tf_op jit(solution)/shard_map/fetch/pallas_call | solution.py:232
  44.6 0.0 copy-start.2
  44.6 1.1 copy-done.2
  45.7 0.0 copy-start.5
  45.7 0.6 copy-done.5
  46.3 0.0 copy-start.4
  46.3 65.8 %layer.1 = (f32[1,512]{1,0:T(1,128)}, bf16[128,48,128]{2,1,0:T(8,128)(2,1)}, bf16[512,2560]{1,0:T(8,128)(2,1)}) custom-call(s32[1,4]{1,0:T(1,128)} %lengths.1, bf16[128,48,128]{2,1,0:T(8,128)(2,1)} %copy-done.2, s32[1,640]{1,0:T(1,128)} %copy-done.5, bf16[512,2048]{1,0:T(8,128)(2,1)} %w_in_ref.1, bf16[512,512]{1,0:T(8,128)(2,1)} %w_out_ref.1), custom_call_target="tpu_custom_call" | custom-call | tf_op jit(solution)/shard_map/layer/pallas_call | solution.py:743
  112.1 0.0 copy-start.10
  112.1 0.0 copy-done.4
  112.1 0.0 copy-start
  112.2 1.7 %copy-done = bf16[512,2560]{1,0:T(8,128)(2,1)S(1)} copy-done((bf16[512,2560]{1,0:T(8,128)(2,1)S(1)}, bf16[512,2560]{1,0:T(8,128)(2,1)}, u32[]{:S(2)}) %copy-start) | copy-done | bytes 2621464
  113.9 0.0 copy-start.1
  113.9 1.4 %copy-done.1 = bf16[128,48,128]{2,1,0:T(8,128)(2,1)S(1)} copy-done((bf16[128,48,128]{2,1,0:T(8,128)(2,1)S(1)}, bf16[128,48,128]{2,1,0:T(8,128)(2,1)}, u32[]{:S(2)}) %copy-start.1) | copy-done | bytes 1572888
  115.3 9.2 %scatter.1 = (f32[4096,512]{1,0:T(8,128)}, f32[512,2048]{1,0:T(8,128)}, f32[512,512]{1,0:T(8,128)}) custom-call(bf16[128,48,128]{2,1,0:T(8,128)(2,1)S(1)} %copy-done.1, s32[128,128]{1,0:T(8,128)S(1)} %get-tuple-element.17.ids_ref, s32[32,128]{1,0:T(8,128)S(1)} %bitcast.7, bf16[512,2560]{1,0:T(8,128)(2,1)S(1)} %copy-done), custom_call_target="tpu_custom_call" | custom-call | tf_op jit(solution)/shard_map/scatter/pallas_call | solution.py:313
  124.5 0.0 copy-done.10
  124.5 0.6 copy.14
Async XLA Ops:
  0.6 0.7 copy-start.3
  1.4 0.7 copy-start.6
  2.0 0.7 copy-start.7
  2.7 0.7 copy-start.8
  3.4 0.7 copy-start.9
  44.6 1.1 copy-start.2
  45.7 0.6 copy-start.5
  46.3 65.8 %copy-start.4 = (s32[4096]{0:T(1024)S(1)}, s32[4096]{0:T(1024)}, u32[]{:S(2)}) copy-start(s32[4096]{0:T(1024)} %param.10) | copy-start | bytes 49156
  112.1 12.3 %copy-start.10 = (f32[1,512]{1,0:T(1,128)S(1)}, f32[1,512]{1,0:T(1,128)}, u32[]{:S(2)}) copy-start(f32[1,512]{1,0:T(1,128)} %get-tuple-element.15) | copy-start | bytes 6148
  112.1 1.7 %copy-start = (bf16[512,2560]{1,0:T(8,128)(2,1)S(1)}, bf16[512,2560]{1,0:T(8,128)(2,1)}, u32[]{:S(2)}) copy-start(bf16[512,2560]{1,0:T(8,128)(2,1)} %get-tuple-element.18.total_ref) | copy-start | bytes 7864324
  113.9 1.4 %copy-start.1 = (bf16[128,48,128]{2,1,0:T(8,128)(2,1)S(1)}, bf16[128,48,128]{2,1,0:T(8,128)(2,1)}, u32[]{:S(2)}) copy-start(bf16[128,48,128]{2,1,0:T(8,128)(2,1)} %get-tuple-element.16.arrived_ref) | copy-start | bytes 4718596

commit v4 on v3

--- a/solution.py
+++ b/solution.py
@@ -14,8 +14,11 @@
 NEG = 128
 ALL = TOK + NEG
 DEV = 128
-CAP = 10
-MSG = 48
+CAP_T = 8
+CAP_N = 2
+CAP = CAP_T + CAP_N
+MSG_T = 32
+MSG_N = 16
 LMAX = 256
 NOW = 64
 ROWS = 4096
@@ -25,7 +28,7 @@
 EPS = 1e-05
 MESH = pl.DeviceIdType.MESH
 VMEM = pl.BlockSpec(memory_space=pltpu.VMEM)
-ANY = pl.BlockSpec(memory_space=pl.ANY)
+HBM = pl.BlockSpec(memory_space=pltpu.HBM)
 F32 = jnp.float32
 BF16 = jnp.bfloat16
 
@@ -95,248 +98,6 @@
         for a in range(4)
         for k in range(2)
     ]
-
-
-def fetch_kernel(
-    item_owner_ref,
-    neg_owner_ref,
-    item_slot_ref,
-    neg_slot_ref,
-    table_ref,
-    update_ref,
-    rows_ref,
-    ids_ref,
-    pos_ref,
-    item_owner,
-    neg_owner,
-    item_slot,
-    neg_slot,
-    update,
-    small_sem,
-    table_vmem,
-    faded,
-    asked,
-    stage,
-    outbox,
-    local_sem,
-    id_send,
-    id_recv,
-    row_send,
-    row_recv,
-):
-    place = Place()
-    pairs = (
-        (item_owner_ref, item_owner),
-        (neg_owner_ref, neg_owner),
-        (item_slot_ref, item_slot),
-        (neg_slot_ref, neg_slot),
-        (update_ref, update),
-    )
-    loads = [
-        pltpu.make_async_copy(src, dst, small_sem.at[n]) for n, (src, dst) in enumerate(pairs)
-    ]
-    for copy in loads:
-        copy.start()
-    load = pltpu.make_async_copy(table_ref, table_vmem, local_sem)
-    load.start()
-    barrier = announce(place)
-    for copy in loads:
-        copy.wait()
-    owner = jnp.concatenate([item_owner[...], neg_owner[...]], 1)
-    slot = jnp.concatenate([item_slot[...], neg_slot[...]], 1)
-    onehot = (iota((DEV, ALL), 0) == owner).astype(F32)
-    upto = (iota((ALL, ALL), 0) <= iota((ALL, ALL), 1)).astype(F32).astype(BF16)
-    count = nn(onehot.astype(BF16), upto)
-    rank = jnp.sum(onehot * count, 0, keepdims=True).astype(jnp.int32) - 1
-    ranked = (iota((DEV, ALL), 0) == rank).astype(F32).astype(BF16)
-    high = (onehot * (slot // 64).astype(F32)).astype(BF16)
-    low = (onehot * (slot % 64).astype(F32)).astype(BF16)
-    asked[...] = (64.0 * nt(high, ranked) + nt(low, ranked)).astype(jnp.int32)
-    pos_ref[...] = rank * DEV + owner
-    pl.semaphore_wait(barrier, DEV - 1)
-
-    def ask(c, carry):
-        for k, (d, t) in enumerate(peers(place, c)):
-
-            def send(d=d, t=t):
-                pltpu.make_async_remote_copy(
-                    src_ref=asked.at[pl.ds(d * 16 + t, 1)],
-                    dst_ref=ids_ref.at[pl.ds(place.me, 1)],
-                    send_sem=id_send,
-                    recv_sem=id_recv,
-                    device_id=(d, t),
-                    device_id_type=MESH,
-                ).start()
-
-            if k == 0:
-                pl.when(c > 0)(send)
-            else:
-                send()
-        return carry
-
-    lax.fori_loop(0, 4, ask, 0)
-    ids_ref[pl.ds(place.me, 1), :] = asked[pl.ds(place.me, 1), :]
-    fade = jnp.exp((NOW - update[...]).astype(F32) * LOG_RHO)
-    fade = jnp.transpose(jnp.concatenate([fade, jnp.zeros((96, 128), F32)], 0))
-    load.wait()
-    for c in range(32):
-        block = table_vmem[c * 128 : (c + 1) * 128, :].astype(F32) * fade[:, c : c + 1]
-        faded[c * 128 : (c + 1) * 128, :] = block.astype(BF16)
-    most = asked.at[pl.ds(0, DEV - 1)]
-    pltpu.make_async_copy(most, most, id_send).wait()
-    pltpu.make_async_copy(most, most, id_recv).wait()
-
-    def serve(c, carry):
-        group = peers(place, c)
-        wanted = jnp.concatenate([ids_ref[pl.ds(d * 16 + t, 1), :] for d, t in group], 0)
-        chosen = [
-            (iota((32, ROWS), 1) == wanted[:, r : r + 1]).astype(F32).astype(BF16)
-            for r in range(CAP)
-        ]
-        found = nn(jnp.concatenate(chosen, 0), faded[...])
-        for r in range(CAP):
-            for b in range(4):
-                stage[pl.ds(4 * r + b, 32, stride=MSG), :] = found[
-                    r * 32 : (r + 1) * 32, b * 128 : (b + 1) * 128
-                ]
-        base = c * 32
-        outbox[pl.ds(base, 32)] = stage[...].astype(BF16).reshape(32, MSG, 128)
-        for k, (d, t) in enumerate(group):
-
-            def send(k=k, d=d, t=t):
-                pltpu.make_async_remote_copy(
-                    src_ref=outbox.at[base + k],
-                    dst_ref=rows_ref.at[place.me],
-                    send_sem=row_send,
-                    recv_sem=row_recv,
-                    device_id=(d, t),
-                    device_id_type=MESH,
-                ).start()
-
-            if k == 0:
-                pl.when(c > 0)(send)
-            else:
-                send()
-        return carry
-
-    for r in range(CAP * 4, MSG):
-        stage[pl.ds(r, 32, stride=MSG), :] = jnp.zeros((32, 128), F32)
-    lax.fori_loop(0, 4, serve, 0)
-    rows_ref[place.me] = outbox[0]
-    most = outbox.at[pl.ds(0, DEV - 1)]
-    pltpu.make_async_copy(most, most, row_send).wait()
-    pltpu.make_async_copy(most, most, row_recv).wait()
-
-
-def fetch(item_owner, neg_owner, item_slot, neg_slot, table, update):
-    return pl.pallas_call(
-        fetch_kernel,
-        out_shape=(
-            jax.ShapeDtypeStruct((DEV, MSG, 128), BF16),
-            jax.ShapeDtypeStruct((DEV, 128), jnp.int32),
-            jax.ShapeDtypeStruct((1, ALL), jnp.int32),
-        ),
-        in_specs=[ANY] * 6,
-        out_specs=(VMEM, VMEM, VMEM),
-        scratch_shapes=[
-            pltpu.VMEM((1, TOK), jnp.int32),
-            pltpu.VMEM((1, NEG), jnp.int32),
-            pltpu.VMEM((1, TOK), jnp.int32),
-            pltpu.VMEM((1, NEG), jnp.int32),
-            pltpu.VMEM((ROWS // 128, 128), jnp.int32),
-            pltpu.SemaphoreType.DMA((5,)),
-            pltpu.VMEM((ROWS, D), BF16),
-            pltpu.VMEM((ROWS, D), BF16),
-            pltpu.VMEM((DEV, 128), jnp.int32),
-            pltpu.VMEM((32 * MSG, 128), F32),
-            pltpu.VMEM((DEV, MSG, 128), BF16),
-            pltpu.SemaphoreType.DMA,
-            pltpu.SemaphoreType.DMA,
-            pltpu.SemaphoreType.DMA,
-            pltpu.SemaphoreType.DMA,
-            pltpu.SemaphoreType.DMA,
-        ],
-        compiler_params=pltpu.CompilerParams(
-            collective_id=0, has_side_effects=True, vmem_limit_bytes=50 << 20
-        ),
-        name="fetch",
-    )(
-        item_owner.reshape(1, TOK),
-        neg_owner.reshape(1, NEG),
-        item_slot.reshape(1, TOK),
-        neg_slot.reshape(1, NEG),
-        table,
-        update,
-    )
-
-
-def scatter_kernel(
-    arrived_ref,
-    ids_ref,
-    update_ref,
-    total_ref,
-    out_ref,
-    grad_in_ref,
-    grad_out_ref,
-    wide,
-    rows,
-    slots,
-):
-    step = pl.program_id(0)
-    grad_out_ref[...] = total_ref[:, :D].astype(F32)
-    grad_in_ref[...] = total_ref[:, D:].astype(F32)
-
-    @pl.when(step == 0)
-    def _():
-        for s in range(8):
-            block = arrived_ref[s * 16 : (s + 1) * 16].astype(F32)
-            wide[s * 16 * MSG : (s + 1) * 16 * MSG, :] = block.reshape(16 * MSG, 128)
-        for c in range(CAP):
-            for b in range(4):
-                piece = wide[pl.ds(4 * c + b, DEV, stride=MSG), :]
-                rows[c * 128 : (c + 1) * 128, b * 128 : (b + 1) * 128] = piece.astype(BF16)
-        slots[...] = jnp.transpose(ids_ref[...])[:16, :]
-
-    fade = jnp.exp((NOW - update_ref[...]).astype(F32) * LOG_RHO)
-    fade = jnp.transpose(jnp.concatenate([fade, jnp.zeros((120, 128), F32)], 0))
-    for s in range(8):
-        first = step * 1024 + s * 128
-        chosen = [
-            (iota((128, 128), 0) + first == slots[c : c + 1, :]).astype(F32).astype(BF16)
-            for c in range(CAP)
-        ]
-        summed = nn(jnp.concatenate(chosen, 1), rows[...])
-        out_ref[s * 128 : (s + 1) * 128, :] = summed * fade[:, s : s + 1]
-
-
-def scatter(arrived, ids, update, total):
-    return pl.pallas_call(
-        scatter_kernel,
-        grid=(4,),
-        out_shape=(
-            jax.ShapeDtypeStruct((ROWS, D), F32),
-            jax.ShapeDtypeStruct((D, 4 * D), F32),
-            jax.ShapeDtypeStruct((D, D), F32),
-        ),
-        in_specs=[
-            pl.BlockSpec((DEV, MSG, 128), lambda i: (0, 0, 0)),
-            pl.BlockSpec((DEV, 128), lambda i: (0, 0)),
-            pl.BlockSpec((8, 128), lambda i: (i, 0)),
-            pl.BlockSpec((128, WIDE), lambda i: (i, 0)),
-        ],
-        out_specs=(
-            pl.BlockSpec((1024, D), lambda i: (i, 0)),
-            pl.BlockSpec((128, 4 * D), lambda i: (i, 0)),
-            pl.BlockSpec((128, D), lambda i: (i, 0)),
-        ),
-        scratch_shapes=[
-            pltpu.VMEM((DEV * MSG, 128), F32),
-            pltpu.VMEM((CAP * 128, D), BF16),
-            pltpu.VMEM((16, 128), jnp.int32),
-        ],
-        compiler_params=pltpu.CompilerParams(vmem_limit_bytes=48 << 20),
-        name="scatter",
-    )(arrived, ids, update, total)
 
 
 class Wave:
@@ -469,20 +230,37 @@
             copy.wait()
 
 
-def layer_kernel(
+def step_kernel(
     lengths,
-    rows_ref,
-    pos_ref,
+    item_owner_ref,
+    neg_owner_ref,
+    item_slot_ref,
+    neg_slot_ref,
+    table_ref,
+    update_ref,
     w_in_ref,
     w_out_ref,
     loss_ref,
-    arrived_ref,
+    arrived_t,
+    arrived_n,
+    ids_ref,
     total_ref,
+    item_owner,
+    neg_owner,
+    item_slot,
+    neg_slot,
+    update,
+    table,
     w_in,
     w_out,
-    flat,
+    asked,
+    outbox_t,
+    outbox_n,
+    rows_t,
+    rows_n,
+    flat_t,
+    flat_n,
     held,
-    where,
     x32,
     n32,
     nb,
@@ -500,7 +278,8 @@
     d_score,
     d_pre,
     grads,
-    box,
+    box_t,
+    box_n,
     grad,
     half,
     acc0,
@@ -510,55 +289,176 @@
     in2,
     in3,
     load_sem,
-    row_send,
-    row_recv,
+    id_sem,
+    out_sem_t,
+    out_sem_n,
+    back_sem_t,
+    back_sem_n,
     core_send,
     core_recv,
     step_send,
     step_recv,
 ):
     place = Place()
-    load_in = pltpu.make_async_copy(w_in_ref, w_in, load_sem.at[0])
-    load_out = pltpu.make_async_copy(w_out_ref, w_out, load_sem.at[1])
-    load_in.start()
-    load_out.start()
+    pairs = (
+        (item_owner_ref, item_owner),
+        (neg_owner_ref, neg_owner),
+        (item_slot_ref, item_slot),
+        (neg_slot_ref, neg_slot),
+        (update_ref, update),
+        (table_ref, table),
+        (w_in_ref, w_in),
+        (w_out_ref, w_out),
+    )
+    loads = [pltpu.make_async_copy(src, dst, load_sem.at[n]) for n, (src, dst) in enumerate(pairs)]
+    for copy in loads:
+        copy.start()
     barrier = announce(place)
-    refs = (grad, total_ref, half, acc0, acc1, acc2, in1, in2, in3)
-    refs += (core_send, core_recv, step_send, step_recv)
-    wave_a = Wave(place, 0, ((0, 384), (384, 384), (768, 256)), refs)
-    wave_b = Wave(place, 1, ((1024, 512), (1536, 512), (2048, 512)), refs)
-    groups = [peers(place, c) for c in range(4)]
-
-    def post(first, last):
-        for n in range(first, last):
-            d, t = groups[n // 32][n % 32]
+    for copy in loads[:5]:
+        copy.wait()
+
+    owner = jnp.concatenate([item_owner[...], neg_owner[...]], 1)
+    slot = jnp.concatenate([item_slot[...], neg_slot[...]], 1)
+    onehot = (iota((DEV, ALL), 0) == owner).astype(F32)
+    before, after = iota((ALL, ALL), 0), iota((ALL, ALL), 1)
+    upto = (before <= after) & ((before >= TOK) | (after < TOK))
+    count = nn(onehot.astype(BF16), upto.astype(F32).astype(BF16))
+    rank = jnp.sum(onehot * count, 0, keepdims=True).astype(jnp.int32) - 1
+    rank = rank + jnp.where(iota((1, ALL), 1) >= TOK, CAP_T, 0)
+    ranked = (iota((DEV, ALL), 0) == rank).astype(F32).astype(BF16)
+    high = (onehot * (slot // 64).astype(F32)).astype(BF16)
+    low = (onehot * (slot % 64).astype(F32)).astype(BF16)
+    asked[...] = (64.0 * nt(high, ranked) + nt(low, ranked)).astype(jnp.int32)
+    pos = rank * DEV + owner
+    pl.semaphore_wait(barrier, DEV - 1)
+
+    def each(c, send):
+        for k, (d, t) in enumerate(peers(place, c)):
+            if k == 0:
+                pl.when(c > 0)(functools.partial(send, k, d, t))
+            else:
+                send(k, d, t)
+
+    def drain(like, sems):
+        most = like.at[pl.ds(0, DEV - 1)]
+        pltpu.make_async_copy(most, most, sems.at[0]).wait()
+        pltpu.make_async_copy(most, most, sems.at[1]).wait()
+
+    def ask(c, carry):
+        def send(k, d, t):
             pltpu.make_async_remote_copy(
-                src_ref=box.at[d * 16 + t],
-                dst_ref=arrived_ref.at[place.me],
-                send_sem=row_send,
-                recv_sem=row_recv,
+                src_ref=asked.at[pl.ds(d * 16 + t, 1)],
+                dst_ref=ids_ref.at[pl.ds(place.me, 1)],
+                send_sem=id_sem.at[0],
+                recv_sem=id_sem.at[1],
                 device_id=(d, t),
                 device_id_type=MESH,
             ).start()
 
-    for s in range(8):
-        block = rows_ref[s * 16 : (s + 1) * 16].astype(F32)
-        flat[s * 16 * MSG : (s + 1) * 16 * MSG, :] = block.reshape(16 * MSG, 128)
-    for c in range(CAP):
+        each(c, send)
+        return carry
+
+    lax.fori_loop(0, 4, ask, 0)
+    ids_ref[pl.ds(place.me, 1), :] = asked[pl.ds(place.me, 1), :]
+    fade = jnp.exp((NOW - update[...]).astype(F32) * LOG_RHO)
+    fade = jnp.transpose(jnp.concatenate([fade, jnp.zeros((96, 128), F32)], 0))
+    loads[5].wait()
+    for c in range(32):
+        block = table[c * 128 : (c + 1) * 128, :].astype(F32) * fade[:, c : c + 1]
+        table[c * 128 : (c + 1) * 128, :] = block.astype(BF16)
+    drain(asked, id_sem)
+
+    def find(wanted, ranks):
+        count = wanted.shape[0]
+        chosen = [
+            (iota((count, ROWS), 1) == wanted[:, r : r + 1]).astype(F32).astype(BF16)
+            for r in ranks
+        ]
+        return nn(jnp.concatenate(chosen, 0), table[...])
+
+    def asked_by(c):
+        return [ids_ref[pl.ds(d * 16 + t, 1), :] for d, t in peers(place, c)]
+
+    def serve(c, carry):
+        found = find(jnp.concatenate(asked_by(c), 0), range(CAP_T))
+        for r in range(CAP_T):
+            for b in range(4):
+                flat_t[pl.ds(4 * r + b, 32, stride=MSG_T), :] = found[
+                    r * 32 : (r + 1) * 32, b * 128 : (b + 1) * 128
+                ]
+        base = c * 32
+        packed = flat_t[pl.ds(0, 32 * MSG_T), :].astype(BF16)
+        outbox_t[pl.ds(base, 32)] = packed.reshape(32, MSG_T, 128)
+
+        def send(k, d, t):
+            pltpu.make_async_remote_copy(
+                src_ref=outbox_t.at[base + k],
+                dst_ref=rows_t.at[place.me],
+                send_sem=out_sem_t.at[0],
+                recv_sem=out_sem_t.at[1],
+                device_id=(d, t),
+                device_id_type=MESH,
+            ).start()
+
+        each(c, send)
+        return carry
+
+    lax.fori_loop(0, 4, serve, 0)
+    rows_t[place.me] = outbox_t[0]
+    wanted = jnp.concatenate([row for c in range(4) for row in asked_by(c)], 0)
+    flat_n[...] = jnp.zeros((DEV * MSG_N, 128), F32)
+    for r in range(CAP_N):
+        found = find(wanted, (CAP_T + r,))
         for b in range(4):
-            piece = flat[pl.ds(4 * c + b, DEV, stride=MSG), :]
-            held[c * 128 : (c + 1) * 128, b * 128 : (b + 1) * 128] = piece.astype(BF16)
-    where[...] = jnp.transpose(jnp.broadcast_to(pos_ref[...], (128, ALL)))
-
-    def take(i):
+            flat_n[pl.ds(4 * r + b, DEV, stride=MSG_N), :] = found[:, b * 128 : (b + 1) * 128]
+    outbox_n[...] = flat_n[...].astype(BF16).reshape(DEV, MSG_N, 128)
+
+    def serve_n(c, carry):
+        base = c * 32
+
+        def send(k, d, t):
+            pltpu.make_async_remote_copy(
+                src_ref=outbox_n.at[base + k],
+                dst_ref=rows_n.at[place.me],
+                send_sem=out_sem_n.at[0],
+                recv_sem=out_sem_n.at[1],
+                device_id=(d, t),
+                device_id_type=MESH,
+            ).start()
+
+        each(c, send)
+        return carry
+
+    lax.fori_loop(0, 4, serve_n, 0)
+    rows_n[place.me] = outbox_n[0]
+
+    where = jnp.transpose(jnp.broadcast_to(pos, (128, ALL)))
+    drain(outbox_t, out_sem_t)
+
+    def unpack(rows, flat, msg):
+        for s in range(8):
+            block = rows[s * 16 : (s + 1) * 16].astype(F32)
+            flat[s * 16 * msg : (s + 1) * 16 * msg, :] = block.reshape(16 * msg, 128)
+
+    def hold(flat, first, count, msg):
+        for c in range(count):
+            for b in range(4):
+                piece = flat[pl.ds(4 * c + b, DEV, stride=msg), :]
+                at = (first + c) * 128
+                held[at : at + 128, b * 128 : (b + 1) * 128] = piece.astype(BF16)
+
+    def take(i, first, count):
         at = where[i * 128 : (i + 1) * 128, :]
         chosen = [
-            (iota((128, 128), 1) + c * 128 == at).astype(F32).astype(BF16) for c in range(CAP)
+            (iota((128, 128), 1) + c * 128 == at).astype(F32).astype(BF16)
+            for c in range(first, first + count)
         ]
-        return nn(jnp.concatenate(chosen, 1), held[...])
-
+        return nn(jnp.concatenate(chosen, 1), held[first * 128 : (first + count) * 128, :])
+
+    unpack(rows_t, flat_t, MSG_T)
+    hold(flat_t, 0, CAP_T, MSG_T)
     for i in range(4):
-        x = take(i)
+        x = take(i, 0, CAP_T)
         span = pl.ds(i * 128, 128)
         x32[span, :] = x
         center = x - jnp.mean(x, -1, keepdims=True)
@@ -567,11 +467,8 @@
         n32[span, :] = normed
         nb[span, :] = normed.astype(BF16)
         scale1[span, :] = scale
-    x = take(4)
-    x32[pl.ds(512, 128), :] = x
-    negatives[...] = x.astype(BF16)
-
-    load_in.wait()
+
+    loads[6].wait()
 
     def project(cb, carry):
         cols = pl.ds(pl.multiple_of(cb * 256, 256), 256)
@@ -612,7 +509,13 @@
 
     lax.fori_loop(0, H, attend, 0)
 
-    load_out.wait()
+    loads[7].wait()
+    drain(outbox_n, out_sem_n)
+    unpack(rows_n, flat_n, MSG_N)
+    hold(flat_n, CAP_T, CAP_N, MSG_N)
+    x = take(4, CAP_T, CAP_N)
+    x32[pl.ds(512, 128), :] = x
+    negatives[...] = x.astype(BF16)
     d_next[pl.ds(0, 8), :] = jnp.zeros((8, D), F32)
     d_negatives = jnp.zeros((NEG, D), F32)
     for i in range(2):
@@ -654,7 +557,31 @@
             - normed * jnp.mean(d_normed * normed, -1, keepdims=True)
         )
         d_att[span, :] = d_values.astype(BF16)
-    grads[pl.ds(TOK, NEG), :] = d_negatives.astype(BF16)
+    mine = pos[:, TOK:]
+    d_negatives = d_negatives.astype(BF16)
+    for c in range(CAP_N):
+        at = iota((DEV, NEG), 0) + (CAP_T + c) * DEV
+        sent = nn((at == mine).astype(F32).astype(BF16), d_negatives)
+        for b in range(4):
+            flat_n[pl.ds(4 * c + b, DEV, stride=MSG_N), :] = sent[:, b * 128 : (b + 1) * 128]
+    box_n[...] = flat_n[...].astype(BF16).reshape(DEV, MSG_N, 128)
+    arrived_n[place.me] = box_n[place.me]
+
+    def post_n(c, carry):
+        def send(k, d, t):
+            pltpu.make_async_remote_copy(
+                src_ref=box_n.at[d * 16 + t],
+                dst_ref=arrived_n.at[place.me],
+                send_sem=back_sem_n.at[0],
+                recv_sem=back_sem_n.at[1],
+                device_id=(d, t),
+                device_id_type=MESH,
+            ).start()
+
+        each(c, send)
+        return carry
+
+    lax.fori_loop(0, 4, post_n, 0)
 
     def back(h, carry):
         for i in range(2):
@@ -672,6 +599,24 @@
             d_pre[span, lanes(3, h)] = (d_k * slope[span, lanes(3, h)].astype(F32)).astype(BF16)
         return carry
 
+    refs = (grad, total_ref, half, acc0, acc1, acc2, in1, in2, in3)
+    refs += (core_send, core_recv, step_send, step_recv)
+    wave_a = Wave(place, 0, ((0, 384), (384, 384), (768, 256)), refs)
+    wave_b = Wave(place, 1, ((1024, 512), (1536, 512), (2048, 512)), refs)
+    groups = [peers(place, c) for c in range(4)]
+
+    def post(first, last):
+        for n in range(first, last):
+            d, t = groups[n // 32][n % 32]
+            pltpu.make_async_remote_copy(
+                src_ref=box_t.at[d * 16 + t],
+                dst_ref=arrived_t.at[place.me],
+                send_sem=back_sem_t.at[0],
+                recv_sem=back_sem_t.at[1],
+                device_id=(d, t),
+                device_id_type=MESH,
+            ).start()
+
     for cb in range(2):
         cols = pl.ds(cb * 256, 256)
         grad[:, cols] = tn(gated[...], d_out[:, cols]).astype(BF16)
@@ -679,7 +624,6 @@
         grad[:, pl.ds(512 + cb * 256, 256)] = tn(nb[...], d_pre[:, pl.ds(cb * 256, 256)]).astype(
             BF16
         )
-    pl.semaphore_wait(barrier, DEV - 1)
     wave_a.swap()
     lax.fori_loop(0, 2, back, 0)
     wave_a.scatter1()
@@ -705,20 +649,20 @@
 
     wave_a.exchange()
 
-    for j in range(CAP // 2):
-        at = iota((256, ALL), 0) + j * 256
-        sent = nn((at == pos_ref[...]).astype(F32).astype(BF16), grads[...])
+    for j in range(CAP_T // 2):
+        at = iota((256, TOK), 0) + j * 256
+        sent = nn((at == pos[:, :TOK]).astype(F32).astype(BF16), grads[...])
         for c in range(2):
             for b in range(4):
-                flat[pl.ds(4 * (2 * j + c) + b, DEV, stride=MSG), :] = sent[
+                flat_t[pl.ds(4 * (2 * j + c) + b, DEV, stride=MSG_T), :] = sent[
                     c * 128 : (c + 1) * 128, b * 128 : (b + 1) * 128
                 ]
     for s in range(8):
-        block = flat[s * 16 * MSG : (s + 1) * 16 * MSG, :].astype(BF16)
-        box[s * 16 : (s + 1) * 16] = block.reshape(16, MSG, 128)
+        block = flat_t[s * 16 * MSG_T : (s + 1) * 16 * MSG_T, :].astype(BF16)
+        box_t[s * 16 : (s + 1) * 16] = block.reshape(16, MSG_T, 128)
 
     wave_b.scatter1()
-    arrived_ref[place.me] = box[place.me]
+    arrived_t[place.me] = box_t[place.me]
     post(1, 32)
     wave_a.gather4()
     post(32, 48)
@@ -734,27 +678,39 @@
     wave_b.restore()
     wave_a.finish()
     wave_b.finish()
-    most = box.at[pl.ds(0, DEV - 1)]
-    pltpu.make_async_copy(most, most, row_send).wait()
-    pltpu.make_async_copy(most, most, row_recv).wait()
-
-
-def layer(rows, pos, w_in, w_out, lengths):
+    drain(box_n, back_sem_n)
+    drain(box_t, back_sem_t)
+
+
+def step(lengths, item_owner, neg_owner, item_slot, neg_slot, table, update, w_in, w_out):
     return pl.pallas_call(
-        layer_kernel,
+        step_kernel,
         out_shape=(
             jax.ShapeDtypeStruct((1, TOK), F32),
-            jax.ShapeDtypeStruct((DEV, MSG, 128), BF16),
+            jax.ShapeDtypeStruct((DEV, MSG_T, 128), BF16),
+            jax.ShapeDtypeStruct((DEV, MSG_N, 128), BF16),
+            jax.ShapeDtypeStruct((DEV, 128), jnp.int32),
             jax.ShapeDtypeStruct((D, WIDE), BF16),
         ),
-        in_specs=[pl.BlockSpec(memory_space=pltpu.SMEM), VMEM, VMEM, ANY, ANY],
-        out_specs=(VMEM, VMEM, VMEM),
+        in_specs=[pl.BlockSpec(memory_space=pltpu.SMEM)] + [HBM] * 8,
+        out_specs=(VMEM,) * 5,
         scratch_shapes=[
+            pltpu.VMEM((1, TOK), jnp.int32),
+            pltpu.VMEM((1, NEG), jnp.int32),
+            pltpu.VMEM((1, TOK), jnp.int32),
+            pltpu.VMEM((1, NEG), jnp.int32),
+            pltpu.VMEM((ROWS // 128, 128), jnp.int32),
+            pltpu.VMEM((ROWS, D), BF16),
             pltpu.VMEM((D, 4 * D), BF16),
             pltpu.VMEM((D, D), BF16),
-            pltpu.VMEM((DEV * MSG, 128), F32),
+            pltpu.VMEM((DEV, 128), jnp.int32),
+            pltpu.VMEM((DEV, MSG_T, 128), BF16),
+            pltpu.VMEM((DEV, MSG_N, 128), BF16),
+            pltpu.VMEM((DEV, MSG_T, 128), BF16),
+            pltpu.VMEM((DEV, MSG_N, 128), BF16),
+            pltpu.VMEM((DEV * MSG_T, 128), F32),
+            pltpu.VMEM((DEV * MSG_N, 128), F32),
             pltpu.VMEM((CAP * DEV, D), BF16),
-            pltpu.VMEM((ALL, 128), jnp.int32),
             pltpu.VMEM((ALL, D), F32),
             pltpu.VMEM((TOK, D), F32),
             pltpu.VMEM((TOK, D), BF16),
@@ -771,8 +727,9 @@
             pltpu.VMEM((TOK, D), BF16),
             pltpu.VMEM((TOK, TOK), BF16),
             pltpu.VMEM((TOK, 4 * D), BF16),
-            pltpu.VMEM((ALL, D), BF16),
-            pltpu.VMEM((DEV, MSG, 128), BF16),
+            pltpu.VMEM((TOK, D), BF16),
+            pltpu.VMEM((DEV, MSG_T, 128), BF16),
+            pltpu.VMEM((DEV, MSG_N, 128), BF16),
             pltpu.VMEM((D, WIDE), BF16),
             pltpu.VMEM((256, WIDE), BF16),
             pltpu.VMEM((256, WIDE), BF16),
@@ -781,28 +738,118 @@
             pltpu.VMEM((3, 64, WIDE), BF16),
             pltpu.VMEM((3, 16, WIDE), BF16),
             pltpu.VMEM((4, 16, WIDE), BF16),
+            pltpu.SemaphoreType.DMA((8,)),
             pltpu.SemaphoreType.DMA((2,)),
-            pltpu.SemaphoreType.DMA,
-            pltpu.SemaphoreType.DMA,
+            pltpu.SemaphoreType.DMA((2,)),
+            pltpu.SemaphoreType.DMA((2,)),
+            pltpu.SemaphoreType.DMA((2,)),
+            pltpu.SemaphoreType.DMA((2,)),
             pltpu.SemaphoreType.DMA((2, 6)),
             pltpu.SemaphoreType.DMA((2, 6)),
             pltpu.SemaphoreType.DMA((2, 3, 5, 3)),
             pltpu.SemaphoreType.DMA((2, 3, 5, 3)),
         ],
         compiler_params=pltpu.CompilerParams(
-            collective_id=1, has_side_effects=True, vmem_limit_bytes=58 << 20
+            collective_id=0, has_side_effects=True, vmem_limit_bytes=60 << 20
         ),
-        name="layer",
-    )(lengths, rows, pos, w_in, w_out)
+        name="step",
+    )(lengths, item_owner, neg_owner, item_slot, neg_slot, table, update, w_in, w_out)
+
+
+def scatter_kernel(
+    arrived_t,
+    arrived_n,
+    ids_ref,
+    update_ref,
+    total_ref,
+    out_ref,
+    grad_in_ref,
+    grad_out_ref,
+    wide_t,
+    wide_n,
+    rows,
+    slots,
+):
+    step = pl.program_id(0)
+    grad_out_ref[...] = total_ref[:, :D].astype(F32)
+    grad_in_ref[...] = total_ref[:, D:].astype(F32)
+
+    @pl.when(step == 0)
+    def _():
+        for arrived, wide, first, count, msg in (
+            (arrived_t, wide_t, 0, CAP_T, MSG_T),
+            (arrived_n, wide_n, CAP_T, CAP_N, MSG_N),
+        ):
+            for s in range(8):
+                block = arrived[s * 16 : (s + 1) * 16].astype(F32)
+                wide[s * 16 * msg : (s + 1) * 16 * msg, :] = block.reshape(16 * msg, 128)
+            for c in range(count):
+                for b in range(4):
+                    piece = wide[pl.ds(4 * c + b, DEV, stride=msg), :]
+                    at = (first + c) * 128
+                    rows[at : at + 128, b * 128 : (b + 1) * 128] = piece.astype(BF16)
+        slots[...] = jnp.transpose(ids_ref[...])[:16, :]
+
+    fade = jnp.exp((NOW - update_ref[...]).astype(F32) * LOG_RHO)
+    fade = jnp.transpose(jnp.concatenate([fade, jnp.zeros((120, 128), F32)], 0))
+    for s in range(8):
+        first = step * 1024 + s * 128
+        chosen = [
+            (iota((128, 128), 0) + first == slots[c : c + 1, :]).astype(F32).astype(BF16)
+            for c in range(CAP)
+        ]
+        summed = nn(jnp.concatenate(chosen, 1), rows[...])
+        out_ref[s * 128 : (s + 1) * 128, :] = summed * fade[:, s : s + 1]
+
+
+def scatter(arrived_t, arrived_n, ids, update, total):
+    return pl.pallas_call(
+        scatter_kernel,
+        grid=(4,),
+        out_shape=(
+            jax.ShapeDtypeStruct((ROWS, D), F32),
+            jax.ShapeDtypeStruct((D, 4 * D), F32),
+            jax.ShapeDtypeStruct((D, D), F32),
+        ),
+        in_specs=[
+            pl.BlockSpec((DEV, MSG_T, 128), lambda i: (0, 0, 0)),
+            pl.BlockSpec((DEV, MSG_N, 128), lambda i: (0, 0, 0)),
+            pl.BlockSpec((DEV, 128), lambda i: (0, 0)),
+            pl.BlockSpec((8, 128), lambda i: (i, 0)),
+            pl.BlockSpec((128, WIDE), lambda i: (i, 0)),
+        ],
+        out_specs=(
+            pl.BlockSpec((1024, D), lambda i: (i, 0)),
+            pl.BlockSpec((128, 4 * D), lambda i: (i, 0)),
+            pl.BlockSpec((128, D), lambda i: (i, 0)),
+        ),
+        scratch_shapes=[
+            pltpu.VMEM((DEV * MSG_T, 128), F32),
+            pltpu.VMEM((DEV * MSG_N, 128), F32),
+            pltpu.VMEM((CAP * 128, D), BF16),
+            pltpu.VMEM((16, 128), jnp.int32),
+        ],
+        compiler_params=pltpu.CompilerParams(vmem_limit_bytes=48 << 20),
+        name="scatter",
+    )(arrived_t, arrived_n, ids, update, total)
 
 
 def on_device(
     table, last_update, item_owner, item_slot, neg_owner, neg_slot, seq_lengths, w_in, w_out
 ):
     update = last_update.reshape(ROWS // 128, 128)
-    rows, ids, pos = fetch(item_owner, neg_owner, item_slot, neg_slot, table, update)
-    losses, arrived, total = layer(rows, pos, w_in, w_out, seq_lengths)
-    table_grad, grad_in, grad_out = scatter(arrived, ids, update, total)
+    losses, arrived_t, arrived_n, ids, total = step(
+        seq_lengths,
+        item_owner.reshape(1, TOK),
+        neg_owner.reshape(1, NEG),
+        item_slot.reshape(1, TOK),
+        neg_slot.reshape(1, NEG),
+        table,
+        update,
+        w_in,
+        w_out,
+    )
+    table_grad, grad_in, grad_out = scatter(arrived_t, arrived_n, ids, update, total)
     return (losses.reshape(TOK), table_grad, grad_in, grad_out)
 
 

time: 125 us -> 117 us (0.936)
  Pallas kernels: 116 us -> 111 us
  local copies, waits for them, and re-layouts: 8.83 us -> 5.43 us
    pallas_call x2 -> x1, Pallas kernels: 106 us -> 101 us  [step(): pl.pallas_call(step_kernel, out_shape=(jax.ShapeDtypeStruct((1, TOK), F32...]
    unnamed x23 -> x13, local copies, waits for them, and re-layouts: 8.83 us -> 5.43 us
where the time goes in v4:
time: 117 us
  Pallas kernels  111 us (95%)
  local copies, waits for them, and re-layouts  5.43 us (5%)
    pallas_call x1, Pallas kernels, step(): pl.pallas_call(step_kernel, out_shape=(jax.ShapeDtypeStruct((1, TOK), F32...  101 us
    pallas_call x1, Pallas kernels, scatter(): pl.pallas_call(scatter_kernel, grid=(4,), out_shape=(jax.ShapeDtypeStruct...  10.1 us
    unnamed x13, local copies, waits for them, and re-layouts  5.43 us

profile of v4, /device:TPU:1, one launch (start us, length us, event | category | flops | bytes accessed | tf_op | source)
XLA Modules:
  0.0 116.8 jit_solution(6327005239880550873)
XLA Ops:
  0.6 0.0 copy-start.4
  0.6 100.5 %step.1 = (f32[1,512]{1,0:T(1,128)}, bf16[128,32,128]{2,1,0:T(8,128)(2,1)}, bf16[128,16,128]{2,1,0:T(8,128)(2,1)}, s32[128,128]{1,0:T(8,128)}, bf16[512,2560]{1,0:T(8,128)(2,1)}) custom-call(s32[1,4]{1,0:T(1,128)} %lengths.1, s32[1,512]{1,0:T(1,128)} %bitcast.8, s32[1,128]{1,0:T(1,128)} %bitcast.11, s32[1,512]{1,0:T(1,128)} %bitcast.9, s32[1,128]{1,0:T(1,128)} %bitcast.12, ...), custom_call_target="tpu_custom_call" | custom-call | tf_op jit(solution)/shard_map/step/pallas_call | solution.py:686
  101.2 0.0 copy-start.5
  101.2 0.0 copy-done.4
  101.2 0.0 copy-start
  101.2 1.7 %copy-done = bf16[512,2560]{1,0:T(8,128)(2,1)S(1)} copy-done((bf16[512,2560]{1,0:T(8,128)(2,1)S(1)}, bf16[512,2560]{1,0:T(8,128)(2,1)}, u32[]{:S(2)}) %copy-start) | copy-done | bytes 2621464
  102.9 0.0 copy-start.1
  102.9 1.2 %copy-done.1 = bf16[128,32,128]{2,1,0:T(8,128)(2,1)S(1)} copy-done((bf16[128,32,128]{2,1,0:T(8,128)(2,1)S(1)}, bf16[128,32,128]{2,1,0:T(8,128)(2,1)}, u32[]{:S(2)}) %copy-start.1) | copy-done | bytes 1048600
  104.2 0.0 copy-start.2
  104.2 1.0 copy-done.2
  105.2 0.0 copy-start.3
  105.2 0.8 copy-done.3
  106.1 10.1 %scatter.1 = (f32[4096,512]{1,0:T(8,128)}, f32[512,2048]{1,0:T(8,128)}, f32[512,512]{1,0:T(8,128)}) custom-call(bf16[128,32,128]{2,1,0:T(8,128)(2,1)S(1)} %copy-done.1, bf16[128,16,128]{2,1,0:T(8,128)(2,1)S(1)} %copy-done.2, s32[128,128]{1,0:T(8,128)S(1)} %copy-done.3, s32[32,128]{1,0:T(8,128)S(1)} %bitcast.7, bf16[512,2560]{1,0:T(8,128)(2,1)S(1)} %copy-done), custom_call_target="tpu_custom_call" | custom-call | tf_op jit(solution)/shard_map/scatter/pallas_call | solution.py:806
  116.2 0.0 copy-done.5
  116.2 0.6 copy.14
Async XLA Ops:
  0.6 100.6 %copy-start.4 = (s32[4096]{0:T(1024)S(1)}, s32[4096]{0:T(1024)}, u32[]{:S(2)}) copy-start(s32[4096]{0:T(1024)} %param.10) | copy-start | bytes 49156
  101.2 15.0 %copy-start.5 = (f32[1,512]{1,0:T(1,128)S(1)}, f32[1,512]{1,0:T(1,128)}, u32[]{:S(2)}) copy-start(f32[1,512]{1,0:T(1,128)} %get-tuple-element.12) | copy-start | bytes 6148
  101.2 1.7 %copy-start = (bf16[512,2560]{1,0:T(8,128)(2,1)S(1)}, bf16[512,2560]{1,0:T(8,128)(2,1)}, u32[]{:S(2)}) copy-start(bf16[512,2560]{1,0:T(8,128)(2,1)} %get-tuple-element.16.total_ref) | copy-start | bytes 7864324
  102.9 1.2 %copy-start.1 = (bf16[128,32,128]{2,1,0:T(8,128)(2,1)S(1)}, bf16[128,32,128]{2,1,0:T(8,128)(2,1)}, u32[]{:S(2)}) copy-start(bf16[128,32,128]{2,1,0:T(8,128)(2,1)} %get-tuple-element.13.arrived_t) | copy-start | bytes 3145732
  104.2 1.0 copy-start.2
  105.2 0.8 copy-start.3

commit v5 on v4

--- a/solution.py
+++ b/solution.py
@@ -45,6 +45,10 @@
     return lax.dot_general(a, b, (((0,), (0,)), ((), ())), preferred_element_type=F32)
 
 
+def sigmoid(values):
+    return 0.5 + 0.5 * jnp.tanh(0.5 * values)
+
+
 def iota(shape, dim):
     return lax.broadcasted_iota(jnp.int32, shape, dim)
 
@@ -59,15 +63,11 @@
         self.x = self.tb // 4
         self.y = lax.rem(self.tb, 4)
 
-    def along(self, axis, shift):
-        z, x, y = self.z, self.x, self.y
-        if axis == "z":
-            z = lax.rem(z + shift, 4)
-        if axis == "x":
-            x = lax.rem(x + shift, 4)
-        if axis == "y":
-            y = lax.rem(y + shift, 4)
-        return (z * 2 + self.core, x * 4 + y)
+    def along(self, *shifts):
+        at = {"z": self.z, "x": self.x, "y": self.y}
+        for axis, shift in shifts:
+            at[axis] = lax.rem(at[axis] + shift, 4)
+        return (at["z"] * 2 + self.core, at["x"] * 4 + at["y"])
 
     def sibling(self):
         return (self.z * 2 + 1 - self.core, self.tb)
@@ -102,16 +102,16 @@
 
 class Wave:
     AXES = (("x", "y", "z"), ("y", "z", "x"), ("z", "x", "y"))
+    PLANE = tuple((j, k) for j in range(4) for k in range(4))[1:]
 
     def __init__(self, place, number, parts, refs):
         self.place, self.number, self.parts = place, number, parts
-        (self.grad, self.total, self.half, self.acc0, self.acc1, self.acc2) = refs[:6]
-        (self.in1, self.in2, self.in3) = refs[6:9]
-        (self.core_send, self.core_recv, self.step_send, self.step_recv) = refs[9:]
+        (self.grad, self.total, self.half, self.acc0, self.acc1, self.in1, self.in2) = refs[:7]
+        (self.core_send, self.core_recv, self.line_send, self.line_recv, self.plane_sem) = refs[7:]
         self.mine = pl.multiple_of(place.core * 256, 256)
         self.other = pl.multiple_of((1 - place.core) * 256, 256)
         self.at = {"x": place.x, "y": place.y, "z": place.z}
-        self.first, self.second, self.third, self.fourth, self.fifth = [], [], [], [], []
+        self.first, self.fifth = [], []
 
     def across(self, slot, src, dst):
         copy = pltpu.make_async_remote_copy(
@@ -129,13 +129,28 @@
         copy = pltpu.make_async_remote_copy(
             src_ref=src,
             dst_ref=dst,
-            send_sem=self.step_send.at[self.number, p, step, shift - 1],
-            recv_sem=self.step_recv.at[self.number, p, step, shift - 1],
-            device_id=self.place.along(self.AXES[p][(0, 1, 2, 1, 0)[step]], shift),
+            send_sem=self.line_send.at[self.number, p, step, shift - 1],
+            recv_sem=self.line_recv.at[self.number, p, step, shift - 1],
+            device_id=self.place.along((self.AXES[p][0], shift)),
             device_id_type=MESH,
         )
         copy.start()
         return copy
+
+    def spread(self, p, step, j, k, src, dst):
+        pltpu.make_async_remote_copy(
+            src_ref=src,
+            dst_ref=dst,
+            send_sem=self.plane_sem.at[self.number, p, step, 0],
+            recv_sem=self.plane_sem.at[self.number, p, step, 1],
+            device_id=self.place.along((self.AXES[p][1], j), (self.AXES[p][2], k)),
+            device_id_type=MESH,
+        ).start()
+
+    def settle(self, p, step):
+        like = self.in2.at[self.number, p]
+        for side in range(2):
+            pltpu.make_async_copy(like, like, self.plane_sem.at[self.number, p, step, side]).wait()
 
     def coordinate(self, p, level):
         return self.at[self.AXES[p][level]]
@@ -156,7 +171,7 @@
                 self.grad[pl.ds(self.mine, 256), cols].astype(F32)
                 + self.half[:, cols].astype(F32)
             ).astype(BF16)
-            for shift in (1, 2, 3):
+            for shift in (1, 3, 2):
                 to = pl.multiple_of(lax.rem(self.coordinate(p, 0) + shift, 4) * 64, 64)
                 src = self.acc0.at[pl.ds(to, 64), cols]
                 self.first.append(self.send(p, 0, shift, src, self.in1.at[shift - 1, :, cols]))
@@ -171,51 +186,33 @@
             for k in range(3):
                 total += self.in1[k, :, cols].astype(F32)
             self.acc1[:, cols] = total.astype(BF16)
-            for shift in (1, 2, 3):
-                to = pl.multiple_of(lax.rem(self.coordinate(p, 1) + shift, 4) * 16, 16)
-                src = self.acc1.at[pl.ds(to, 16), cols]
-                self.second.append(self.send(p, 1, shift, src, self.in2.at[shift - 1, :, cols]))
-
-    def exchange(self):
-        for p, (start, width) in enumerate(self.parts):
-            cols = pl.ds(start, width)
-            for copy in self.second[3 * p : 3 * p + 3]:
-                copy.wait()
-            own = pl.multiple_of(self.coordinate(p, 1) * 16, 16)
-            total = self.acc1[pl.ds(own, 16), cols].astype(F32)
-            for k in range(3):
-                total += self.in2[k, :, cols].astype(F32)
-            self.acc2[:, cols] = total.astype(BF16)
-            at = self.coordinate(p, 2)
-            self.in3[at, :, cols] = self.acc2[:, cols]
-            for shift in (1, 2, 3):
-                self.third.append(
-                    self.send(p, 2, shift, self.acc2.at[:, cols], self.in3.at[at, :, cols])
-                )
+            for n, (j, k) in enumerate(self.PLANE):
+                row = pl.multiple_of(lax.rem(self.coordinate(p, 1) + j, 4) * 16, 16)
+                col = pl.multiple_of(start + lax.rem(self.coordinate(p, 2) + k, 4) * 128, 128)
+                src = self.acc1.at[pl.ds(row, 16), pl.ds(col, 128)]
+                self.spread(p, 0, j, k, src, self.in2.at[self.number, p, n])
 
     def gather4(self):
         for p, (start, width) in enumerate(self.parts):
-            cols = pl.ds(start, width)
-            for copy in self.third[3 * p : 3 * p + 3]:
-                copy.wait()
-            total = self.in3[0, :, cols].astype(F32)
-            for k in range(1, 4):
-                total += self.in3[k, :, cols].astype(F32)
-            wide = pl.multiple_of(self.mine + self.coordinate(p, 0) * 64, 64)
-            narrow = pl.multiple_of(wide + self.coordinate(p, 1) * 16, 16)
+            self.settle(p, 0)
+            row = pl.multiple_of(self.coordinate(p, 1) * 16, 16)
+            cols = pl.ds(pl.multiple_of(start + self.coordinate(p, 2) * 128, 128), 128)
+            total = self.acc1[pl.ds(row, 16), cols].astype(F32)
+            for n in range(15):
+                total += self.in2[self.number, p, n].astype(F32)
+            narrow = pl.multiple_of(self.mine + self.coordinate(p, 0) * 64 + row, 16)
             self.total[pl.ds(narrow, 16), cols] = total.astype(BF16)
             piece = self.total.at[pl.ds(narrow, 16), cols]
-            for shift in (1, 2, 3):
-                self.fourth.append(self.send(p, 3, shift, piece, piece))
+            for j, k in self.PLANE:
+                self.spread(p, 1, j, k, piece, piece)
 
     def gather5(self):
         for p, (start, width) in enumerate(self.parts):
-            for copy in self.fourth[3 * p : 3 * p + 3]:
-                copy.wait()
+            self.settle(p, 1)
             wide = pl.multiple_of(self.mine + self.coordinate(p, 0) * 64, 64)
             piece = self.total.at[pl.ds(wide, 64), pl.ds(start, width)]
-            for shift in (1, 2, 3):
-                self.fifth.append(self.send(p, 4, shift, piece, piece))
+            for shift in (1, 3, 2):
+                self.fifth.append(self.send(p, 1, shift, piece, piece))
 
     def restore(self):
         self.last = []
@@ -243,8 +240,9 @@
     loss_ref,
     arrived_t,
     arrived_n,
+    slots_ref,
+    total_ref,
     ids_ref,
-    total_ref,
     item_owner,
     neg_owner,
     item_slot,
@@ -264,8 +262,13 @@
     x32,
     n32,
     nb,
+    turned,
     scale1,
     negatives,
+    placing,
+    packing,
+    seen0,
+    seen1,
     mixed,
     slope,
     weights,
@@ -278,16 +281,15 @@
     d_score,
     d_pre,
     grads,
+    d_negatives,
     box_t,
     box_n,
     grad,
     half,
     acc0,
     acc1,
-    acc2,
     in1,
     in2,
-    in3,
     load_sem,
     id_sem,
     out_sem_t,
@@ -296,8 +298,10 @@
     back_sem_n,
     core_send,
     core_recv,
-    step_send,
-    step_recv,
+    line_send,
+    line_recv,
+    plane_sem,
+    own_sem,
 ):
     place = Place()
     pairs = (
@@ -329,7 +333,8 @@
     high = (onehot * (slot // 64).astype(F32)).astype(BF16)
     low = (onehot * (slot % 64).astype(F32)).astype(BF16)
     asked[...] = (64.0 * nt(high, ranked) + nt(low, ranked)).astype(jnp.int32)
-    pos = rank * DEV + owner
+    pos_t = (owner * CAP_T + rank)[:, :TOK]
+    pos_n = ((rank - CAP_T) * DEV + owner)[:, TOK:]
     pl.semaphore_wait(barrier, DEV - 1)
 
     def each(c, send):
@@ -368,27 +373,21 @@
         table[c * 128 : (c + 1) * 128, :] = block.astype(BF16)
     drain(asked, id_sem)
 
-    def find(wanted, ranks):
-        count = wanted.shape[0]
-        chosen = [
-            (iota((count, ROWS), 1) == wanted[:, r : r + 1]).astype(F32).astype(BF16)
-            for r in ranks
-        ]
-        return nn(jnp.concatenate(chosen, 0), table[...])
-
     def asked_by(c):
         return [ids_ref[pl.ds(d * 16 + t, 1), :] for d, t in peers(place, c)]
 
     def serve(c, carry):
-        found = find(jnp.concatenate(asked_by(c), 0), range(CAP_T))
-        for r in range(CAP_T):
-            for b in range(4):
-                flat_t[pl.ds(4 * r + b, 32, stride=MSG_T), :] = found[
-                    r * 32 : (r + 1) * 32, b * 128 : (b + 1) * 128
-                ]
+        wanted = asked_by(c) + [jnp.zeros((96, 128), jnp.int32)]
+        wanted = jnp.transpose(jnp.concatenate(wanted, 0))[:CAP_T, :]
+        chosen = [
+            (iota((CAP_T, ROWS), 1) == wanted[:, k : k + 1]).astype(F32) for k in range(32)
+        ]
+        found = nn(jnp.concatenate(chosen, 0).astype(BF16), table[...])
+        found = found.reshape(32, CAP_T, D)
+        for b in range(4):
+            flat_t[pl.ds(0, 32), b * 8 : b * 8 + 8, :] = found[:, :, b * 128 : (b + 1) * 128]
         base = c * 32
-        packed = flat_t[pl.ds(0, 32 * MSG_T), :].astype(BF16)
-        outbox_t[pl.ds(base, 32)] = packed.reshape(32, MSG_T, 128)
+        outbox_t[pl.ds(base, 32)] = flat_t[pl.ds(0, 32)].astype(BF16)
 
         def send(k, d, t):
             pltpu.make_async_remote_copy(
@@ -408,7 +407,8 @@
     wanted = jnp.concatenate([row for c in range(4) for row in asked_by(c)], 0)
     flat_n[...] = jnp.zeros((DEV * MSG_N, 128), F32)
     for r in range(CAP_N):
-        found = find(wanted, (CAP_T + r,))
+        at = wanted[:, CAP_T + r : CAP_T + r + 1]
+        found = nn((iota((DEV, ROWS), 1) == at).astype(F32).astype(BF16), table[...])
         for b in range(4):
             flat_n[pl.ds(4 * r + b, DEV, stride=MSG_N), :] = found[:, b * 128 : (b + 1) * 128]
     outbox_n[...] = flat_n[...].astype(BF16).reshape(DEV, MSG_N, 128)
@@ -432,60 +432,25 @@
     lax.fori_loop(0, 4, serve_n, 0)
     rows_n[place.me] = outbox_n[0]
 
-    where = jnp.transpose(jnp.broadcast_to(pos, (128, ALL)))
-    drain(outbox_t, out_sem_t)
-
-    def unpack(rows, flat, msg):
-        for s in range(8):
-            block = rows[s * 16 : (s + 1) * 16].astype(F32)
-            flat[s * 16 * msg : (s + 1) * 16 * msg, :] = block.reshape(16 * msg, 128)
-
-    def hold(flat, first, count, msg):
-        for c in range(count):
-            for b in range(4):
-                piece = flat[pl.ds(4 * c + b, DEV, stride=msg), :]
-                at = (first + c) * 128
-                held[at : at + 128, b * 128 : (b + 1) * 128] = piece.astype(BF16)
-
-    def take(i, first, count):
-        at = where[i * 128 : (i + 1) * 128, :]
-        chosen = [
-            (iota((128, 128), 1) + c * 128 == at).astype(F32).astype(BF16)
-            for c in range(first, first + count)
-        ]
-        return nn(jnp.concatenate(chosen, 1), held[first * 128 : (first + count) * 128, :])
-
-    unpack(rows_t, flat_t, MSG_T)
-    hold(flat_t, 0, CAP_T, MSG_T)
-    for i in range(4):
-        x = take(i, 0, CAP_T)
-        span = pl.ds(i * 128, 128)
-        x32[span, :] = x
-        center = x - jnp.mean(x, -1, keepdims=True)
-        scale = lax.rsqrt(jnp.mean(center * center, -1, keepdims=True) + EPS)
-        normed = center * scale
-        n32[span, :] = normed
-        nb[span, :] = normed.astype(BF16)
-        scale1[span, :] = scale
-
-    loads[6].wait()
-
-    def project(cb, carry):
-        cols = pl.ds(pl.multiple_of(cb * 256, 256), 256)
-        pre = nn(nb[...], w_in[:, cols])
-        sig = jax.nn.sigmoid(pre)
-        mixed[:, cols] = (pre * sig).astype(BF16)
-        slope[:, cols] = (sig * (1.0 + pre * (1.0 - sig))).astype(BF16)
-        return carry
-
-    lax.fori_loop(0, 8, project, 0)
-
+    high = (ids_ref[...] // 64).astype(F32).astype(BF16)
+    low = (ids_ref[...] % 64).astype(F32).astype(BF16)
+    spread = (iota((DEV, CAP_T * DEV), 1) % CAP_T == iota((DEV, CAP_T * DEV), 0)).astype(F32)
+    spread = spread.astype(BF16)
+    own = iota((DEV, CAP_T * DEV), 1) // CAP_T == iota((DEV, CAP_T * DEV), 0)
+    row = jnp.where(own, 64.0 * nn(high, spread) + nn(low, spread), 0.0)
+    slots_ref[:, : CAP_T * DEV] = jnp.sum(row, 0, keepdims=True).astype(jnp.int32)
+    column = jnp.transpose(ids_ref[...])
+    for r in range(CAP_N):
+        at = (CAP_T + r) * DEV
+        slots_ref[:, at : at + DEV] = column[CAP_T + r : CAP_T + r + 1, :]
+    where = jnp.transpose(jnp.broadcast_to(pos_t, (128, TOK)))
+    for c in range(CAP_T):
+        match = iota((TOK, 128), 1) + c * 128 == where
+        placing[:, c * 128 : (c + 1) * 128] = match.astype(F32).astype(BF16)
+    packing[...] = (iota((CAP_T * DEV, TOK), 0) == pos_t).astype(F32).astype(BF16)
     end1 = lengths[0, 0]
     end2 = end1 + lengths[0, 1]
     end3 = end2 + lengths[0, 2]
-
-    def lanes(part, h):
-        return pl.ds(pl.multiple_of(part * 512 + h * 128, 128), 128)
 
     def visible(i):
         row = iota((256, 256 * (i + 1)), 0) + 256 * i
@@ -495,29 +460,69 @@
         )
         return jnp.where((col <= row) & (col >= start), 1.0 / LMAX, 0.0).astype(F32)
 
+    seen0[...] = visible(0)
+    seen1[...] = visible(1)
+    drain(outbox_t, out_sem_t)
+
+    flat_t[...] = rows_t[...].astype(F32)
+    for b in range(4):
+        piece = flat_t[:, b * 8 : b * 8 + 8, :].reshape(CAP_T * DEV, 128)
+        held[: CAP_T * DEV, b * 128 : (b + 1) * 128] = piece.astype(BF16)
+    x32[pl.ds(0, TOK), :] = nn(placing[...], held[: CAP_T * DEV, :])
+    for i in range(4):
+        span = pl.ds(i * 128, 128)
+        x = x32[span, :]
+        center = x - jnp.mean(x, -1, keepdims=True)
+        scale = lax.rsqrt(jnp.mean(center * center, -1, keepdims=True) + EPS)
+        normed = center * scale
+        n32[span, :] = normed
+        nb[span, :] = normed.astype(BF16)
+        scale1[span, :] = scale
+    turned[...] = jnp.transpose(n32[...]).astype(BF16)
+
+    loads[6].wait()
+
+    def project(cb, carry):
+        cols = pl.ds(pl.multiple_of(cb * 256, 256), 256)
+        pre = nn(nb[...], w_in[:, cols])
+        sig = sigmoid(pre)
+        mixed[:, cols] = (pre * sig).astype(BF16)
+        slope[:, cols] = (sig * (1.0 + pre * (1.0 - sig))).astype(BF16)
+        return carry
+
+    lax.fori_loop(0, 8, project, 0, unroll=4)
+
+    def lanes(part, h):
+        at = part * 512 + h * 128
+        return pl.ds(at if isinstance(at, int) else pl.multiple_of(at, 128), 128)
+
     def attend(h, carry):
         for i in range(2):
             span, past = pl.ds(256 * i, 256), pl.ds(0, 256 * (i + 1))
             score = nt(mixed[span, lanes(2, h)], mixed[past, lanes(3, h)])
-            sig = jax.nn.sigmoid(score)
-            seen = visible(i)
+            sig = sigmoid(score)
+            seen = (seen0, seen1)[i][...]
             weight = (score * sig * seen).astype(BF16)
             weights[h, span, past] = weight
             bend[h, span, past] = (sig * (1.0 + score * (1.0 - sig)) * seen).astype(BF16)
             attended[span, lanes(0, h)] = nn(weight, mixed[past, lanes(1, h)])
         return carry
 
-    lax.fori_loop(0, H, attend, 0)
+    lax.fori_loop(0, H, attend, 0, unroll=True)
 
     loads[7].wait()
     drain(outbox_n, out_sem_n)
-    unpack(rows_n, flat_n, MSG_N)
-    hold(flat_n, CAP_T, CAP_N, MSG_N)
-    x = take(4, CAP_T, CAP_N)
+    flat_n[...] = rows_n[...].astype(F32).reshape(DEV * MSG_N, 128)
+    for c in range(CAP_N):
+        for b in range(4):
+            piece = flat_n[pl.ds(4 * c + b, DEV, stride=MSG_N), :]
+            at = (CAP_T + c) * 128
+            held[at : at + 128, b * 128 : (b + 1) * 128] = piece.astype(BF16)
+    x = tn((iota((CAP_N * DEV, NEG), 0) == pos_n).astype(F32).astype(BF16), held[CAP_T * DEV :, :])
     x32[pl.ds(512, 128), :] = x
     negatives[...] = x.astype(BF16)
     d_next[pl.ds(0, 8), :] = jnp.zeros((8, D), F32)
-    d_negatives = jnp.zeros((NEG, D), F32)
+    d_negs = jnp.zeros((NEG, D), F32)
     for i in range(2):
         span = pl.ds(256 * i, 256)
         values = attended[span, :]
@@ -547,7 +552,7 @@
         d_out_b = (d_pos * following + nn(d_neg, negatives[...])).astype(BF16)
         d_out[span, :] = d_out_b
         d_next[pl.ds(256 * i + 8, 256), :] = d_pos * out
-        d_negatives += tn(d_neg, out_b)
+        d_negs += tn(d_neg, out_b)
         d_gated = nt(d_out_b, w_out[...])
         d_pre[span, 0:512] = (d_gated * normed * slope[span, 0:512].astype(F32)).astype(BF16)
         d_normed = d_gated * gate
@@ -557,15 +562,15 @@
             - normed * jnp.mean(d_normed * normed, -1, keepdims=True)
         )
         d_att[span, :] = d_values.astype(BF16)
-    mine = pos[:, TOK:]
-    d_negatives = d_negatives.astype(BF16)
+    d_negatives[...] = d_negs.astype(BF16)
     for c in range(CAP_N):
-        at = iota((DEV, NEG), 0) + (CAP_T + c) * DEV
-        sent = nn((at == mine).astype(F32).astype(BF16), d_negatives)
+        at = iota((DEV, NEG), 0) + c * DEV
+        sent = nn((at == pos_n).astype(F32).astype(BF16), d_negatives[...])
         for b in range(4):
             flat_n[pl.ds(4 * c + b, DEV, stride=MSG_N), :] = sent[:, b * 128 : (b + 1) * 128]
     box_n[...] = flat_n[...].astype(BF16).reshape(DEV, MSG_N, 128)
-    arrived_n[place.me] = box_n[place.me]
+    own_n = pltpu.make_async_copy(box_n.at[place.me], arrived_n.at[place.me], own_sem.at[0])
+    own_n.start()
 
     def post_n(c, carry):
         def send(k, d, t):
@@ -599,9 +604,9 @@
             d_pre[span, lanes(3, h)] = (d_k * slope[span, lanes(3, h)].astype(F32)).astype(BF16)
         return carry
 
-    refs = (grad, total_ref, half, acc0, acc1, acc2, in1, in2, in3)
-    refs += (core_send, core_recv, step_send, step_recv)
-    wave_a = Wave(place, 0, ((0, 384), (384, 384), (768, 256)), refs)
+    refs = (grad, total_ref, half, acc0, acc1, in1, in2)
+    refs += (core_send, core_recv, line_send, line_recv, plane_sem)
+    wave_a = Wave(place, 0, ((0, 512), (512, 512)), refs)
     wave_b = Wave(place, 1, ((1024, 512), (1536, 512), (2048, 512)), refs)
     groups = [peers(place, c) for c in range(4)]
 
@@ -617,21 +622,17 @@
                 device_id_type=MESH,
             ).start()
 
-    for cb in range(2):
-        cols = pl.ds(cb * 256, 256)
-        grad[:, cols] = tn(gated[...], d_out[:, cols]).astype(BF16)
-    for cb in range(2):
-        grad[:, pl.ds(512 + cb * 256, 256)] = tn(nb[...], d_pre[:, pl.ds(cb * 256, 256)]).astype(
-            BF16
-        )
+    grad[:, pl.ds(0, 512)] = tn(gated[...], d_out[...]).astype(BF16)
+    grad[:, pl.ds(512, 512)] = nn(turned[...], d_pre[:, pl.ds(0, 512)]).astype(BF16)
     wave_a.swap()
-    lax.fori_loop(0, 2, back, 0)
+    back(0, 0)
+    back(1, 0)
     wave_a.scatter1()
-    lax.fori_loop(2, 4, back, 0)
-    for cb in range(2, 8):
-        grad[:, pl.ds(512 + cb * 256, 256)] = tn(nb[...], d_pre[:, pl.ds(cb * 256, 256)]).astype(
-            BF16
-        )
+    back(2, 0)
+    back(3, 0)
+    for cb in range(1, 4):
+        cols = pl.ds(cb * 512, 512)
+        grad[:, pl.ds(512 + cb * 512, 512)] = nn(turned[...], d_pre[:, cols]).astype(BF16)
     wave_b.swap()
     wave_a.scatter2()
 
@@ -647,37 +648,31 @@
         d_x += d_out[span, :].astype(F32) + d_next[pl.ds(256 * i + 7, 256), :]
         grads[span, :] = d_x.astype(BF16)
 
-    wave_a.exchange()
-
-    for j in range(CAP_T // 2):
-        at = iota((256, TOK), 0) + j * 256
-        sent = nn((at == pos[:, :TOK]).astype(F32).astype(BF16), grads[...])
-        for c in range(2):
-            for b in range(4):
-                flat_t[pl.ds(4 * (2 * j + c) + b, DEV, stride=MSG_T), :] = sent[
-                    c * 128 : (c + 1) * 128, b * 128 : (b + 1) * 128
-                ]
-    for s in range(8):
-        block = flat_t[s * 16 * MSG_T : (s + 1) * 16 * MSG_T, :].astype(BF16)
-        box_t[s * 16 : (s + 1) * 16] = block.reshape(16, MSG_T, 128)
-
     wave_b.scatter1()
-    arrived_t[place.me] = box_t[place.me]
-    post(1, 32)
+
+    for j in range(4):
+        half_of = pl.ds(j * 256, 256)
+        sent = nn(packing[half_of, :], grads[...]).reshape(32, CAP_T, D)
+        for b in range(4):
+            flat_t[pl.ds(j * 32, 32), b * 8 : b * 8 + 8, :] = sent[:, :, b * 128 : (b + 1) * 128]
+    box_t[...] = flat_t[...].astype(BF16)
+
+    own_t = pltpu.make_async_copy(box_t.at[place.me], arrived_t.at[place.me], own_sem.at[1])
+    own_t.start()
     wave_a.gather4()
-    post(32, 48)
     wave_b.scatter2()
-    post(48, 64)
+    post(1, 50)
+    wave_b.gather4()
+    post(50, 90)
     wave_a.gather5()
-    post(64, 96)
-    wave_b.exchange()
-    post(96, 128)
-    wave_b.gather4()
+    wave_b.gather5()
+    post(90, 128)
     wave_a.restore()
-    wave_b.gather5()
     wave_b.restore()
     wave_a.finish()
     wave_b.finish()
+    own_n.wait()
+    own_t.wait()
     drain(box_n, back_sem_n)
     drain(box_t, back_sem_t)
 
@@ -689,12 +684,13 @@
             jax.ShapeDtypeStruct((1, TOK), F32),
             jax.ShapeDtypeStruct((DEV, MSG_T, 128), BF16),
             jax.ShapeDtypeStruct((DEV, MSG_N, 128), BF16),
-            jax.ShapeDtypeStruct((DEV, 128), jnp.int32),
+            jax.ShapeDtypeStruct((1, CAP * DEV), jnp.int32),
             jax.ShapeDtypeStruct((D, WIDE), BF16),
         ),
         in_specs=[pl.BlockSpec(memory_space=pltpu.SMEM)] + [HBM] * 8,
-        out_specs=(VMEM,) * 5,
+        out_specs=(VMEM, HBM, HBM, VMEM, VMEM),
         scratch_shapes=[
+            pltpu.VMEM((DEV, 128), jnp.int32),
             pltpu.VMEM((1, TOK), jnp.int32),
             pltpu.VMEM((1, NEG), jnp.int32),
             pltpu.VMEM((1, TOK), jnp.int32),
@@ -708,14 +704,19 @@
             pltpu.VMEM((DEV, MSG_N, 128), BF16),
             pltpu.VMEM((DEV, MSG_T, 128), BF16),
             pltpu.VMEM((DEV, MSG_N, 128), BF16),
-            pltpu.VMEM((DEV * MSG_T, 128), F32),
+            pltpu.VMEM((DEV, MSG_T, 128), F32),
             pltpu.VMEM((DEV * MSG_N, 128), F32),
             pltpu.VMEM((CAP * DEV, D), BF16),
             pltpu.VMEM((ALL, D), F32),
             pltpu.VMEM((TOK, D), F32),
             pltpu.VMEM((TOK, D), BF16),
+            pltpu.VMEM((D, TOK), BF16),
             pltpu.VMEM((TOK, 1), F32),
             pltpu.VMEM((NEG, D), BF16),
+            pltpu.VMEM((TOK, CAP_T * DEV), BF16),
+            pltpu.VMEM((CAP_T * DEV, TOK), BF16),
+            pltpu.VMEM((256, 256), F32),
+            pltpu.VMEM((256, 512), F32),
             pltpu.VMEM((TOK, 4 * D), BF16),
             pltpu.VMEM((TOK, 4 * D), BF16),
             pltpu.VMEM((H, TOK, TOK), BF16),
@@ -728,16 +729,15 @@
             pltpu.VMEM((TOK, TOK), BF16),
             pltpu.VMEM((TOK, 4 * D), BF16),
             pltpu.VMEM((TOK, D), BF16),
+            pltpu.VMEM((NEG, D), BF16),
             pltpu.VMEM((DEV, MSG_T, 128), BF16),
             pltpu.VMEM((DEV, MSG_N, 128), BF16),
             pltpu.VMEM((D, WIDE), BF16),
             pltpu.VMEM((256, WIDE), BF16),
             pltpu.VMEM((256, WIDE), BF16),
             pltpu.VMEM((64, WIDE), BF16),
-            pltpu.VMEM((16, WIDE), BF16),
             pltpu.VMEM((3, 64, WIDE), BF16),
-            pltpu.VMEM((3, 16, WIDE), BF16),
-            pltpu.VMEM((4, 16, WIDE), BF16),
+            pltpu.VMEM((2, 3, 15, 16, 128), BF16),
             pltpu.SemaphoreType.DMA((8,)),
             pltpu.SemaphoreType.DMA((2,)),
             pltpu.SemaphoreType.DMA((2,)),
@@ -746,8 +746,10 @@
             pltpu.SemaphoreType.DMA((2,)),
             pltpu.SemaphoreType.DMA((2, 6)),
             pltpu.SemaphoreType.DMA((2, 6)),
-            pltpu.SemaphoreType.DMA((2, 3, 5, 3)),
-            pltpu.SemaphoreType.DMA((2, 3, 5, 3)),
+            pltpu.SemaphoreType.DMA((2, 3, 2, 3)),
+            pltpu.SemaphoreType.DMA((2, 3, 2, 3)),
+            pltpu.SemaphoreType.DMA((2, 3, 2, 2)),
+            pltpu.SemaphoreType.DMA((2,)),
         ],
         compiler_params=pltpu.CompilerParams(
             collective_id=0, has_side_effects=True, vmem_limit_bytes=60 << 20
@@ -757,52 +759,84 @@
 
 
 def scatter_kernel(
-    arrived_t,
-    arrived_n,
-    ids_ref,
+    arrived_t_ref,
+    arrived_n_ref,
+    slots_ref,
     update_ref,
     total_ref,
     out_ref,
     grad_in_ref,
     grad_out_ref,
+    arrived_t,
+    arrived_n,
+    slots,
+    update,
+    total,
     wide_t,
     wide_n,
     rows,
-    slots,
+    chosen0,
+    chosen1,
+    load_sem,
 ):
     step = pl.program_id(0)
-    grad_out_ref[...] = total_ref[:, :D].astype(F32)
-    grad_in_ref[...] = total_ref[:, D:].astype(F32)
+
+    def choose(block, chosen):
+        for half in range(2):
+            local = slots[...] - (block * 512 + half * 256)
+            local = jnp.where((local >= 0) & (local < 256), local, -1).astype(F32).astype(BF16)
+            row = iota((256, 1), 0).astype(F32).astype(BF16)
+            far = jnp.abs(row - local)
+            chosen[half * 256 : (half + 1) * 256, :] = jnp.maximum(1.0 - far, 0.0).astype(BF16)
+
+    def fold(first, chosen):
+        summed = nn(chosen[...], rows[...])
+        for k in range(4):
+            at = first + k
+            out_ref[at * 128 : (at + 1) * 128, :] = (
+                summed[k * 128 : (k + 1) * 128] * fade[:, at : at + 1]
+            )
+
+    pairs = (
+        (arrived_t_ref, arrived_t),
+        (arrived_n_ref, arrived_n),
+        (slots_ref, slots),
+        (update_ref, update),
+        (total_ref, total),
+    )
+    loads = [pltpu.make_async_copy(src, dst, load_sem.at[n]) for n, (src, dst) in enumerate(pairs)]
 
     @pl.when(step == 0)
     def _():
-        for arrived, wide, first, count, msg in (
-            (arrived_t, wide_t, 0, CAP_T, MSG_T),
-            (arrived_n, wide_n, CAP_T, CAP_N, MSG_N),
-        ):
-            for s in range(8):
-                block = arrived[s * 16 : (s + 1) * 16].astype(F32)
-                wide[s * 16 * msg : (s + 1) * 16 * msg, :] = block.reshape(16 * msg, 128)
-            for c in range(count):
-                for b in range(4):
-                    piece = wide[pl.ds(4 * c + b, DEV, stride=msg), :]
-                    at = (first + c) * 128
-                    rows[at : at + 128, b * 128 : (b + 1) * 128] = piece.astype(BF16)
-        slots[...] = jnp.transpose(ids_ref[...])[:16, :]
-
-    fade = jnp.exp((NOW - update_ref[...]).astype(F32) * LOG_RHO)
+        for copy in loads:
+            copy.start()
+        loads[2].wait()
+        choose(0, chosen0)
+        for copy in loads[:2] + loads[3:]:
+            copy.wait()
+        wide_t[...] = arrived_t[...].astype(F32)
+        for b in range(4):
+            piece = wide_t[:, b * 8 : b * 8 + 8, :].reshape(CAP_T * DEV, 128)
+            rows[: CAP_T * DEV, b * 128 : (b + 1) * 128] = piece.astype(BF16)
+        wide_n[...] = arrived_n[...].astype(F32).reshape(DEV * MSG_N, 128)
+        for c in range(CAP_N):
+            for b in range(4):
+                piece = wide_n[pl.ds(4 * c + b, DEV, stride=MSG_N), :]
+                at = (CAP_T + c) * 128
+                rows[at : at + 128, b * 128 : (b + 1) * 128] = piece.astype(BF16)
+
+    part = total[pl.ds(pl.multiple_of(step * 128, 128), 128), :]
+    grad_out_ref[...] = part[:, :D].astype(F32)
+    grad_in_ref[...] = part[:, D:].astype(F32)
+    fade = jnp.exp((NOW - update[pl.ds(pl.multiple_of(step * 8, 8), 8), :]).astype(F32) * LOG_RHO)
     fade = jnp.transpose(jnp.concatenate([fade, jnp.zeros((120, 128), F32)], 0))
-    for s in range(8):
-        first = step * 1024 + s * 128
-        chosen = [
-            (iota((128, 128), 0) + first == slots[c : c + 1, :]).astype(F32).astype(BF16)
-            for c in range(CAP)
-        ]
-        summed = nn(jnp.concatenate(chosen, 1), rows[...])
-        out_ref[s * 128 : (s + 1) * 128, :] = summed * fade[:, s : s + 1]
-
-
-def scatter(arrived_t, arrived_n, ids, update, total):
+    choose(2 * step + 1, chosen1)
+    fold(0, chosen0)
+    choose(2 * step + 2, chosen0)
+    fold(4, chosen1)
+
+
+def scatter(arrived_t, arrived_n, slots, update, total):
     return pl.pallas_call(
         scatter_kernel,
         grid=(4,),
@@ -811,34 +845,35 @@
             jax.ShapeDtypeStruct((D, 4 * D), F32),
             jax.ShapeDtypeStruct((D, D), F32),
         ),
-        in_specs=[
-            pl.BlockSpec((DEV, MSG_T, 128), lambda i: (0, 0, 0)),
-            pl.BlockSpec((DEV, MSG_N, 128), lambda i: (0, 0, 0)),
-            pl.BlockSpec((DEV, 128), lambda i: (0, 0)),
-            pl.BlockSpec((8, 128), lambda i: (i, 0)),
-            pl.BlockSpec((128, WIDE), lambda i: (i, 0)),
-        ],
+        in_specs=[HBM] * 5,
         out_specs=(
             pl.BlockSpec((1024, D), lambda i: (i, 0)),
             pl.BlockSpec((128, 4 * D), lambda i: (i, 0)),
             pl.BlockSpec((128, D), lambda i: (i, 0)),
         ),
         scratch_shapes=[
-            pltpu.VMEM((DEV * MSG_T, 128), F32),
+            pltpu.VMEM((DEV, MSG_T, 128), BF16),
+            pltpu.VMEM((DEV, MSG_N, 128), BF16),
+            pltpu.VMEM((1, CAP * DEV), jnp.int32),
+            pltpu.VMEM((ROWS // 128, 128), jnp.int32),
+            pltpu.VMEM((D, WIDE), BF16),
+            pltpu.VMEM((DEV, MSG_T, 128), F32),
             pltpu.VMEM((DEV * MSG_N, 128), F32),
-            pltpu.VMEM((CAP * 128, D), BF16),
-            pltpu.VMEM((16, 128), jnp.int32),
+            pltpu.VMEM((CAP * DEV, D), BF16),
+            pltpu.VMEM((512, CAP * DEV), BF16),
+            pltpu.VMEM((512, CAP * DEV), BF16),
+            pltpu.SemaphoreType.DMA((5,)),
         ],
-        compiler_params=pltpu.CompilerParams(vmem_limit_bytes=48 << 20),
+        compiler_params=pltpu.CompilerParams(vmem_limit_bytes=60 << 20),
         name="scatter",
-    )(arrived_t, arrived_n, ids, update, total)
+    )(arrived_t, arrived_n, slots, update, total)
 
 
 def on_device(
     table, last_update, item_owner, item_slot, neg_owner, neg_slot, seq_lengths, w_in, w_out
 ):
     update = last_update.reshape(ROWS // 128, 128)
-    losses, arrived_t, arrived_n, ids, total = step(
+    losses, arrived_t, arrived_n, slots, total = step(
         seq_lengths,
         item_owner.reshape(1, TOK),
         neg_owner.reshape(1, NEG),
@@ -849,7 +884,7 @@
         w_in,
         w_out,
     )
-    table_grad, grad_in, grad_out = scatter(arrived_t, arrived_n, ids, update, total)
+    table_grad, grad_in, grad_out = scatter(arrived_t, arrived_n, slots, update, total)
     return (losses.reshape(TOK), table_grad, grad_in, grad_out)
 
 

time: 117 us -> 106 us (0.906)
  Pallas kernels: 111 us -> 104 us
  local copies, waits for them, and re-layouts: 5.43 us -> 0.58 us
    pallas_call x1, Pallas kernels: 101 us -> 93.6 us  [step(): pl.pallas_call(step_kernel, out_shape=(jax.ShapeDtypeStruct((1, TOK), F32...]
    unnamed x13 -> x3, local copies, waits for them, and re-layouts: 5.43 us -> 0.58 us
where the time goes in v5:
time: 106 us
  Pallas kernels  104 us (98%)
    pallas_call x1, Pallas kernels, step(): pl.pallas_call(step_kernel, out_shape=(jax.ShapeDtypeStruct((1, TOK), F32...  93.6 us
    pallas_call x1, Pallas kernels, scatter(): pl.pallas_call(scatter_kernel, grid=(4,), out_shape=(jax.ShapeDtypeStruct...  10.8 us

profile of v5, /device:TPU:1, one launch (start us, length us, event | category | flops | bytes accessed | tf_op | source)
XLA Modules:
  0.0 105.6 jit_solution(1930438141085256332)
XLA Ops:
  0.6 93.6 %step.1 = (f32[1,512]{1,0:T(1,128)}, bf16[128,32,128]{2,1,0:T(8,128)(2,1)}, bf16[128,16,128]{2,1,0:T(8,128)(2,1)}, s32[1,1280]{1,0:T(1,128)}, bf16[512,2560]{1,0:T(8,128)(2,1)}) custom-call(s32[1,4]{1,0:T(1,128)} %lengths.1, s32[1,512]{1,0:T(1,128)} %bitcast.8, s32[1,128]{1,0:T(1,128)} %bitcast.11, s32[1,512]{1,0:T(1,128)} %bitcast.9, s32[1,128]{1,0:T(1,128)} %bitcast.12, ...), custom_call_target="tpu_custom_call" | custom-call | tf_op jit(solution)/shard_map/step/pallas_call | solution.py:681
  94.2 0.0 copy-start
  94.2 10.8 %scatter.1 = (f32[4096,512]{1,0:T(8,128)}, f32[512,2048]{1,0:T(8,128)}, f32[512,512]{1,0:T(8,128)}) custom-call(bf16[128,32,128]{2,1,0:T(8,128)(2,1)} %get-tuple-element.13.arrived_t_ref, bf16[128,16,128]{2,1,0:T(8,128)(2,1)} %get-tuple-element.14.arrived_n_ref, s32[1,1280]{1,0:T(1,128)} %get-tuple-element.15.slots_ref, s32[32,128]{1,0:T(8,128)} %bitcast.7, ...), custom_call_target="tpu_custom_call" | custom-call | tf_op jit(solution)/shard_map/scatter/pallas_call | solution.py:840
  105.0 0.0 copy-done
  105.1 0.6 copy.14
Async XLA Ops:
  94.2 10.8 %copy-start = (f32[1,512]{1,0:T(1,128)S(1)}, f32[1,512]{1,0:T(1,128)}, u32[]{:S(2)}) copy-start(f32[1,512]{1,0:T(1,128)} %get-tuple-element.12) | copy-start | bytes 6148

commit v6 on v5

--- a/solution.py
+++ b/solution.py
@@ -241,6 +241,7 @@
     arrived_t,
     arrived_n,
     slots_ref,
+    total_out,
     total_ref,
     ids_ref,
     item_owner,
@@ -302,6 +303,7 @@
     line_recv,
     plane_sem,
     own_sem,
+    total_sem,
 ):
     place = Place()
     pairs = (
@@ -572,8 +574,9 @@
     own_n = pltpu.make_async_copy(box_n.at[place.me], arrived_n.at[place.me], own_sem.at[0])
     own_n.start()
 
-    def post_n(c, carry):
-        def send(k, d, t):
+    def post_n(first, last):
+        for n in range(first, last):
+            d, t = groups[n // 32][n % 32]
             pltpu.make_async_remote_copy(
                 src_ref=box_n.at[d * 16 + t],
                 dst_ref=arrived_n.at[place.me],
@@ -582,11 +585,6 @@
                 device_id=(d, t),
                 device_id_type=MESH,
             ).start()
-
-        each(c, send)
-        return carry
-
-    lax.fori_loop(0, 4, post_n, 0)
 
     def back(h, carry):
         for i in range(2):
@@ -625,10 +623,14 @@
     grad[:, pl.ds(0, 512)] = tn(gated[...], d_out[...]).astype(BF16)
     grad[:, pl.ds(512, 512)] = nn(turned[...], d_pre[:, pl.ds(0, 512)]).astype(BF16)
     wave_a.swap()
+    post_n(1, 32)
     back(0, 0)
+    post_n(32, 64)
     back(1, 0)
     wave_a.scatter1()
+    post_n(64, 96)
     back(2, 0)
+    post_n(96, 128)
     back(3, 0)
     for cb in range(1, 4):
         cols = pl.ds(cb * 512, 512)
@@ -669,12 +671,26 @@
     post(90, 128)
     wave_a.restore()
     wave_b.restore()
+    rest = pl.ds(1024, 3 * D)
+
+    def leave(n, rows, cols):
+        copy = pltpu.make_async_copy(
+            total_ref.at[rows, cols], total_out.at[rows, cols], total_sem.at[n]
+        )
+        copy.start()
+        return copy
+
+    leaving = [leave(0, pl.ds(wave_b.mine, 256), rest)]
     wave_a.finish()
+    leaving.append(leave(1, pl.ds(0, D), pl.ds(0, 1024)))
     wave_b.finish()
+    leaving.append(leave(2, pl.ds(wave_b.other, 256), rest))
     own_n.wait()
     own_t.wait()
     drain(box_n, back_sem_n)
     drain(box_t, back_sem_t)
+    for copy in leaving:
+        copy.wait()
 
 
 def step(lengths, item_owner, neg_owner, item_slot, neg_slot, table, update, w_in, w_out):
@@ -688,8 +704,9 @@
             jax.ShapeDtypeStruct((D, WIDE), BF16),
         ),
         in_specs=[pl.BlockSpec(memory_space=pltpu.SMEM)] + [HBM] * 8,
-        out_specs=(VMEM, HBM, HBM, VMEM, VMEM),
+        out_specs=(VMEM, HBM, HBM, VMEM, HBM),
         scratch_shapes=[
+            pltpu.VMEM((D, WIDE), BF16),
             pltpu.VMEM((DEV, 128), jnp.int32),
             pltpu.VMEM((1, TOK), jnp.int32),
             pltpu.VMEM((1, NEG), jnp.int32),
@@ -750,6 +767,7 @@
             pltpu.SemaphoreType.DMA((2, 3, 2, 3)),
             pltpu.SemaphoreType.DMA((2, 3, 2, 2)),
             pltpu.SemaphoreType.DMA((2,)),
+            pltpu.SemaphoreType.DMA((3,)),
         ],
         compiler_params=pltpu.CompilerParams(
             collective_id=0, has_side_effects=True, vmem_limit_bytes=60 << 20
@@ -764,14 +782,17 @@
     slots_ref,
     update_ref,
     total_ref,
+    loss_ref,
     out_ref,
     grad_in_ref,
     grad_out_ref,
+    loss_out_ref,
     arrived_t,
     arrived_n,
     slots,
     update,
     total,
+    loss,
     wide_t,
     wide_n,
     rows,
@@ -803,6 +824,7 @@
         (slots_ref, slots),
         (update_ref, update),
         (total_ref, total),
+        (loss_ref, loss),
     )
     loads = [pltpu.make_async_copy(src, dst, load_sem.at[n]) for n, (src, dst) in enumerate(pairs)]
 
@@ -825,6 +847,7 @@
                 at = (CAP_T + c) * 128
                 rows[at : at + 128, b * 128 : (b + 1) * 128] = piece.astype(BF16)
 
+    loss_out_ref[...] = loss[...]
     part = total[pl.ds(pl.multiple_of(step * 128, 128), 128), :]
     grad_out_ref[...] = part[:, :D].astype(F32)
     grad_in_ref[...] = part[:, D:].astype(F32)
@@ -836,7 +859,7 @@
     fold(4, chosen1)
 
 
-def scatter(arrived_t, arrived_n, slots, update, total):
+def scatter(arrived_t, arrived_n, slots, update, total, losses):
     return pl.pallas_call(
         scatter_kernel,
         grid=(4,),
@@ -844,12 +867,14 @@
             jax.ShapeDtypeStruct((ROWS, D), F32),
             jax.ShapeDtypeStruct((D, 4 * D), F32),
             jax.ShapeDtypeStruct((D, D), F32),
+            jax.ShapeDtypeStruct((1, TOK), F32),
         ),
-        in_specs=[HBM] * 5,
+        in_specs=[HBM] * 6,
         out_specs=(
             pl.BlockSpec((1024, D), lambda i: (i, 0)),
             pl.BlockSpec((128, 4 * D), lambda i: (i, 0)),
             pl.BlockSpec((128, D), lambda i: (i, 0)),
+            pl.BlockSpec((1, TOK), lambda i: (0, 0)),
         ),
         scratch_shapes=[
             pltpu.VMEM((DEV, MSG_T, 128), BF16),
@@ -857,16 +882,17 @@
             pltpu.VMEM((1, CAP * DEV), jnp.int32),
             pltpu.VMEM((ROWS // 128, 128), jnp.int32),
             pltpu.VMEM((D, WIDE), BF16),
+            pltpu.VMEM((1, TOK), F32),
             pltpu.VMEM((DEV, MSG_T, 128), F32),
             pltpu.VMEM((DEV * MSG_N, 128), F32),
             pltpu.VMEM((CAP * DEV, D), BF16),
             pltpu.VMEM((512, CAP * DEV), BF16),
             pltpu.VMEM((512, CAP * DEV), BF16),
-            pltpu.SemaphoreType.DMA((5,)),
+            pltpu.SemaphoreType.DMA((6,)),
         ],
         compiler_params=pltpu.CompilerParams(vmem_limit_bytes=60 << 20),
         name="scatter",
-    )(arrived_t, arrived_n, slots, update, total)
+    )(arrived_t, arrived_n, slots, update, total, losses)
 
 
 def on_device(
@@ -884,7 +910,9 @@
         w_in,
         w_out,
     )
-    table_grad, grad_in, grad_out = scatter(arrived_t, arrived_n, slots, update, total)
+    table_grad, grad_in, grad_out, losses = scatter(
+        arrived_t, arrived_n, slots, update, total, losses
+    )
     return (losses.reshape(TOK), table_grad, grad_in, grad_out)
 
 

time: 106 us -> 104 us (0.981)
  no operation moved by 1% of the time
where the time goes in v6:
time: 104 us
  Pallas kernels  103 us (99%)
    pallas_call x1, Pallas kernels, step(): pl.pallas_call(step_kernel, out_shape=(jax.ShapeDtypeStruct((1, TOK), F32...  92.5 us
    pallas_call x1, Pallas kernels, scatter(): pl.pallas_call(scatter_kernel, grid=(4,), out_shape=(jax.ShapeDtypeStruct...  10.8 us

profile of v6, /device:TPU:1, one launch (start us, length us, event | category | flops | bytes accessed | tf_op | source)
XLA Modules:
  0.0 104.2 jit_solution(11623249524616837171)
XLA Ops:
  0.6 92.5 %step.1 = (f32[1,512]{1,0:T(1,128)}, bf16[128,32,128]{2,1,0:T(8,128)(2,1)}, bf16[128,16,128]{2,1,0:T(8,128)(2,1)}, s32[1,1280]{1,0:T(1,128)}, bf16[512,2560]{1,0:T(8,128)(2,1)}) custom-call(s32[1,4]{1,0:T(1,128)} %lengths.1, s32[1,512]{1,0:T(1,128)} %bitcast.8, s32[1,128]{1,0:T(1,128)} %bitcast.10, s32[1,512]{1,0:T(1,128)} %bitcast.9, s32[1,128]{1,0:T(1,128)} %bitcast.11, ...), custom_call_target="tpu_custom_call" | custom-call | tf_op jit(solution)/shard_map/step/pallas_call | solution.py:697
  93.2 10.8 %scatter.1 = (f32[4096,512]{1,0:T(8,128)}, f32[512,2048]{1,0:T(8,128)}, f32[512,512]{1,0:T(8,128)}, f32[1,512]{1,0:T(1,128)}) custom-call(bf16[128,32,128]{2,1,0:T(8,128)(2,1)} %get-tuple-element.13.arrived_t_ref, bf16[128,16,128]{2,1,0:T(8,128)(2,1)} %get-tuple-element.14.arrived_n_ref, s32[1,1280]{1,0:T(1,128)} %get-tuple-element.15.slots_ref, ...), custom_call_target="tpu_custom_call" | custom-call | tf_op jit(solution)/shard_map/scatter/pallas_call | solution.py:863
